TPU v7x, 128 devices: a whole 4x4x4 slice. The times are simulated.
128 devices in a mesh: lat: 32 (over x, z, core), lon: 4 (over y).
Axes of the slice: x: 4, y: 4, z: 4, core: 2. Of those that a mesh axis runs over, the one named last changes fastest.
Arguments:
- grid_fields: bfloat16 [32, 4, 2048, 227], P('lat', 'lon'), may hold values from -6 to 6
- mesh_static: bfloat16 [32, 4, 512, 512], P('lat', 'lon'), may hold values from -6 to 6
- encode_senders: int32 [32, 4, 3072], P('lat', 'lon'), may hold values from 0 to 16639, as said below
- encode_receivers: int32 [32, 4, 3072], P('lat', 'lon'), may hold values from 0 to 511
- encode_geometry: float32 [32, 4, 4, 3072], P('lat', 'lon'), may hold values from -6 to 6
- encode_valid: int32 [32, 4], P('lat', 'lon'), may hold values from 1536 to 3072, as said below
- mesh_senders: int32 [32, 4, 4096], P('lat', 'lon'), may hold values from 0 to 4607
- mesh_receivers: int32 [32, 4, 4096], P('lat', 'lon'), may hold values from 0 to 511
- mesh_geometry: float32 [32, 4, 4, 4096], P('lat', 'lon'), may hold values from -6 to 6
- mesh_valid: int32 [32, 4], P('lat', 'lon'), may hold values from 2048 to 4096, as said below
- decode_senders: int32 [32, 4, 3, 2048], P('lat', 'lon'), may hold values from 0 to 4607
- embed_weight: bfloat16 [227, 512], replicated, may hold values from -0.375 to 0.375
- encode_source: bfloat16 [512, 512], replicated, may hold values from -0.25 to 0.25
- encode_edge: float32 [4, 512], replicated, may hold values from -3 to 3
- encode_second: bfloat16 [512, 512], replicated, may hold values from -0.25 to 0.25
- node_first: bfloat16 [512, 512], replicated, may hold values from -0.25 to 0.25
- node_second: bfloat16 [512, 512], replicated, may hold values from -0.25 to 0.25
- node_gain: float32 [512], replicated, may hold values from 0.1 to 1.9
- process_source: bfloat16 [512, 512], replicated, may hold values from -0.25 to 0.25
- process_target: bfloat16 [512, 512], replicated, may hold values from -0.25 to 0.25
- process_edge: float32 [4, 512], replicated, may hold values from -3 to 3
- process_second: bfloat16 [512, 512], replicated, may hold values from -0.25 to 0.25
- update_message: bfloat16 [512, 512], replicated, may hold values from -0.25 to 0.25
- update_state: bfloat16 [512, 512], replicated, may hold values from -0.25 to 0.25
- update_out: bfloat16 [512, 512], replicated, may hold values from -0.25 to 0.25
- process_gain: float32 [512], replicated, may hold values from 0.1 to 1.9
- decode_source: bfloat16 [512, 512], replicated, may hold values from -0.25 to 0.25
- decode_target: bfloat16 [512, 512], replicated, may hold values from -0.25 to 0.25
- decode_hidden: bfloat16 [512, 512], replicated, may hold values from -0.25 to 0.25
- output_weight: bfloat16 [512, 227], replicated, may hold values from -0.25 to 0.25
Outputs:
- prediction: float32 [32, 4, 2048, 227], P('lat', 'lon')
Inputs may be any that keep to these rules, and one draw needn't show every extreme that they name: `encode_senders`: a sender outside the own block (rows 8192 to 10239) is one of the first 256 cells of its block; every device has an edge at cell 256 - 1 of each of its eight neighbouring blocks and one at cell 0 of the first neighbouring block. `encode_valid`: valid slots are the first ones of a device; the first device fills all 3072. `mesh_valid`: valid slots are the first ones of a device; the first device fills all 4096.
All inputs are finite; a program needn't handle non-finite values.
Results may differ from a plain program's by a relative error of at most 0.017.
Values may be sent and summed in bfloat16 or wider, within the bound.
No kernel may reach another device: no remote copies, remote signals or barrier semaphores. Data moves between devices by JAX's collectives and lax.ppermute only.
A program may use at most 128 MiB of HBM per device.

v0:
```python
import jax
import jax.numpy as jnp
from jax import lax
from jax.sharding import PartitionSpec as P

EPSILON = 1e-05


def extended(cells, sides, width, closed):
    for axis, dim in sides:
        count = lax.axis_size(axis)
        ends = count if closed else count - 1
        head = lax.slice_in_dim(cells, 0, width, axis=dim)
        tail = lax.slice_in_dim(cells, cells.shape[dim] - width, cells.shape[dim], axis=dim)
        cells = jnp.concatenate(
            [
                lax.ppermute(tail, axis, [(i, (i + 1) % count) for i in range(ends)]),
                cells,
                lax.ppermute(head, axis, [((i + 1) % count, i) for i in range(ends)]),
            ],
            axis=dim,
        )
    return cells


def layer_norm(values, gain):
    centre = values - jnp.mean(values, axis=-1, keepdims=True)
    spread = jnp.mean(centre * centre, axis=-1, keepdims=True)
    return centre * lax.rsqrt(spread + EPSILON) * gain


def geometry_term(geometry, weight):
    return jnp.einsum("fe,fl->el", geometry, weight, precision=lax.Precision.HIGHEST)


def collect(receivers, messages, nodes):
    onehot = (receivers[None, :] == jnp.arange(nodes, dtype=jnp.int32)[:, None]).astype(
        jnp.bfloat16
    )
    return jnp.dot(onehot, messages, preferred_element_type=jnp.float32)


def edge_messages(rows, geometry, edge_weight, second, valid):
    hidden = jax.nn.silu(rows + geometry_term(geometry, edge_weight)).astype(jnp.bfloat16)
    keep = jnp.arange(hidden.shape[0], dtype=jnp.int32) < valid
    product = jnp.dot(hidden, second, preferred_element_type=jnp.float32)
    return jnp.where(keep[:, None], product, jnp.zeros((), jnp.float32)).astype(jnp.bfloat16)


def grid_cycle(block):
    wider = extended(block, (("lon", 1),), 1, True)
    return extended(wider, (("lat", 0),), 1, False)


def mesh_cycle(block):
    wider = extended(block, (("lon", 1),), 1, True)
    return extended(wider, (("lat", 0),), 1, False)


def flatten(cycle):
    return cycle.reshape(9 * cycle.shape[2], cycle.shape[3])


def project(values, weight):
    return jnp.dot(values, weight, preferred_element_type=jnp.float32).astype(jnp.bfloat16)


def embed(values, weight):
    return jax.nn.silu(jnp.dot(values, weight, preferred_element_type=jnp.float32)).astype(
        jnp.bfloat16
    )


def shards(
    grid_fields,
    mesh_static,
    encode_senders,
    encode_receivers,
    encode_geometry,
    encode_valid,
    mesh_senders,
    mesh_receivers,
    mesh_geometry,
    mesh_valid,
    decode_senders,
    embed_weight,
    encode_source,
    encode_edge,
    encode_second,
    node_first,
    node_second,
    node_gain,
    process_source,
    process_target,
    process_edge,
    process_second,
    update_message,
    update_state,
    update_out,
    process_gain,
    decode_source,
    decode_target,
    decode_hidden,
    output_weight,
):
    fields = grid_fields[0, 0]
    mesh_nodes = mesh_static.shape[2]
    senders = encode_senders[0, 0]
    embedded = embed(fields, embed_weight)
    cycle_source = project(flatten(grid_cycle(embedded[None, None])), encode_source)
    rows = jnp.take(cycle_source, senders, axis=0).astype(jnp.float32)
    messages = edge_messages(
        rows, encode_geometry[0, 0], encode_edge, encode_second, encode_valid[0, 0]
    )
    gathered = collect(encode_receivers[0, 0], messages, mesh_nodes)
    node_hidden = embed(gathered.astype(jnp.bfloat16), node_first)
    normed = layer_norm(
        jnp.dot(node_hidden, node_second, preferred_element_type=jnp.float32), node_gain
    )
    mesh_start = (mesh_static[0, 0].astype(jnp.float32) + normed).astype(jnp.bfloat16)
    cycle_mesh = project(flatten(mesh_cycle(mesh_start[None, None])), process_source)
    receivers = mesh_receivers[0, 0]
    target_mesh = jnp.dot(mesh_start, process_target, preferred_element_type=jnp.float32)
    rows = jnp.take(cycle_mesh, mesh_senders[0, 0], axis=0).astype(jnp.float32) + jnp.take(
        target_mesh, receivers, axis=0
    )
    messages = edge_messages(
        rows, mesh_geometry[0, 0], process_edge, process_second, mesh_valid[0, 0]
    )
    total = collect(receivers, messages, mesh_nodes).astype(jnp.bfloat16)
    update = jax.nn.silu(
        jnp.dot(total, update_message, preferred_element_type=jnp.float32)
        + jnp.dot(mesh_start, update_state, preferred_element_type=jnp.float32)
    ).astype(jnp.bfloat16)
    normed = layer_norm(
        jnp.dot(update, update_out, preferred_element_type=jnp.float32), process_gain
    )
    mesh_end = (mesh_start.astype(jnp.float32) + normed).astype(jnp.bfloat16)
    cycle_out = project(flatten(mesh_cycle(mesh_end[None, None])), decode_source)
    target_grid = jnp.dot(embedded, decode_target, preferred_element_type=jnp.float32)
    rows = jnp.take(cycle_out, decode_senders[0, 0], axis=0).astype(jnp.float32) + target_grid[None]
    decode_edge = jax.nn.silu(rows).astype(jnp.bfloat16)
    decode_sum = jnp.sum(decode_edge.astype(jnp.float32), axis=0).astype(jnp.bfloat16)
    decode_final = embed(decode_sum, decode_hidden)
    prediction = fields.astype(jnp.float32) + jnp.dot(
        decode_final, output_weight, preferred_element_type=jnp.float32
    )
    return prediction[None, None]


def solution(mesh):
    in_specs = (
        P("lat", "lon", None, None),
        P("lat", "lon", None, None),
        P("lat", "lon", None),
        P("lat", "lon", None),
        P("lat", "lon", None, None),
        P("lat", "lon"),
        P("lat", "lon", None),
        P("lat", "lon", None),
        P("lat", "lon", None, None),
        P("lat", "lon"),
        P("lat", "lon", None, None),
        P(),
        P(),
        P(),
        P(),
        P(),
        P(),
        P(),
        P(),
        P(),
        P(),
        P(),
        P(),
        P(),
        P(),
        P(),
        P(),
        P(),
        P(),
        P(),
    )
    out_specs = P("lat", "lon", None, None)
    return jax.shard_map(shards, mesh=mesh, in_specs=in_specs, out_specs=out_specs, check_vma=False)
```

profile of v0, /device:TPU:3, one launch (start us, length us, event | category | flops | bytes accessed | tf_op | source)
XLA Modules:
  0.0 372.7 jit_solution(11212608356794456020)
XLA Ops:
  0.0 2.6 multiply_convert_fusion.4
  5.6 45.0 %collective-permute-done = bf16[1,1,2048,512]{3,2,1,0:T(8,128)(2,1)S(1)} collective-permute-done((bf16[1,1,2048,512]{3,2,1,0:T(8,128)(2,1)S(1)}, bf16[1,1,2048,512]{3,2,1,0:T(8,128)(2,1)S(1)}, u32[]{:S(2)}, u32[]{:S(2)}) %collective-permute-start) | collective-permute-done | bytes 2097184 | tf_op jit(solution)/shard_map/ppermute | solution.py:17
  51.4 4.9 %collective-permute-start.2 = (bf16[1,3,2048,512]{3,2,1,0:T(8,128)(2,1)S(1)}, bf16[1,3,2048,512]{3,2,1,0:T(8,128)(2,1)S(1)}, u32[]{:S(2)}, u32[]{:S(2)}) collective-permute-start(bf16[1,3,2048,512]{3,2,1,0:T(8,128)(2,1)S(1)} %pad_maximum_fusion.1), channel_id=1, source_target_pairs={{0,4},{4,8},{8,12},{12,16},{16,20},{20,24},{24,28},{28,32},{32,36}... | collective-permute-start | bytes 18874376 | tf_op jit(solution)/shard_map/ppermute | solution.py:17
  56.3 2.4 collective-permute-start.3
  59.5 7.1 %fusion.17 = f32[3072,512]{1,0:T(8,128)} fusion(f32[4,512]{1,0:T(4,128)S(1)} %copy-done.12, f32[1,1,4,3072]{3,2,1,0:T(4,128)S(1)} %copy-done.10), kind=kOutput, calls=%fused_computation.52 | convolution fusion | flops 75497472 | bytes 6348800 | tf_op jit(solution)/shard_map/fe,fl->el/dot_general | solution.py:33
  66.5 57.7 %collective-permute-done.2 = bf16[1,3,2048,512]{3,2,1,0:T(8,128)(2,1)S(1)} collective-permute-done((bf16[1,3,2048,512]{3,2,1,0:T(8,128)(2,1)S(1)}, bf16[1,3,2048,512]{3,2,1,0:T(8,128)(2,1)S(1)}, u32[]{:S(2)}, u32[]{:S(2)}) %collective-permute-start.2) | collective-permute-done | bytes 6291488 | tf_op jit(solution)/shard_map/ppermute | solution.py:17
  124.2 4.4 %collective-permute-done.3 = bf16[1,3,2048,512]{3,2,1,0:T(8,128)(2,1)S(1)} collective-permute-done((bf16[1,3,2048,512]{3,2,1,0:T(8,128)(2,1)S(1)}, bf16[1,3,2048,512]{3,2,1,0:T(8,128)(2,1)S(1)}, u32[]{:S(2)}, u32[]{:S(2)}) %collective-permute-start.3) | collective-permute-done | bytes 6291488 | tf_op jit(solution)/shard_map/ppermute | solution.py:19
  128.6 8.2 %pad_maximum_fusion = bf16[3,3,2048,512]{3,2,1,0:T(8,128)(2,1)} fusion(bf16[1,3,2048,512]{3,2,1,0:T(8,128)(2,1)S(1)} %collective-permute-done.3, bf16[1,1,2048,512]{3,2,1,0:T(8,128)(2,1)S(1)} %collective-permute-done.1, bf16[1,1,2048,512]{3,2,1,0:T(8,128)(2,1)S(1)} %bitcast.78, bf16[1,1,2048,512]{3,2,1,0:T(8,128)(2,1)S(1)} %collective-permute-done, ...), kind=kLoop, calls=%fused_computation.5 | loop fusion | flops 37748736 | bytes 37748736 | tf_op jit(solution)/shard_map/concatenate | solution.py:15
  136.8 20.2 %convolution_convert_fusion = bf16[18432,512]{1,0:T(8,128)(2,1)} fusion(bf16[18432,512]{1,0:T(8,128)(2,1)} %bitcast.79, bf16[512,512]{1,0:T(8,128)(2,1)S(1)} %copy-done), kind=kOutput, calls=%fused_computation.4 | convolution fusion | flops 9673113600 | bytes 38273024 | tf_op jit(solution)/shard_map/dot_general | solution.py:65
  157.0 22.4 %gather_fusion = bf16[3072,512]{1,0:T(8,128)(2,1)} fusion(bf16[18432,512]{1,0:T(8,128)(2,1)} %convolution_convert_fusion, s32[3072]{0:T(1024)S(1)} %broadcast_clamp_fusion.3), kind=kCustom, calls=%fused_computation | custom fusion | bytes 6303744 | tf_op jit(solution)/shard_map/jit(_take)/gather | solution.py:111
  179.4 8.9 %fusion.8 = bf16[512,512]{1,0:T(8,128)(2,1)} fusion(bf16[512,512]{1,0:T(8,128)(2,1)S(1)} %copy-done.15, pred[3072]{0:T(1024)(128)(4,1)S(1)} %get-tuple-element.9, f32[3072,512]{1,0:T(8,128)} %fusion.17, bf16[3072,512]{1,0:T(8,128)(2,1)} %gather_fusion, pred[3072]{0:T(1024)(128)(4,1)S(1)} %get-tuple-element.10, s32[3072]{0:T(1024)S(1)} %bitcast.94), kind=kOutput, calls=%fused_computation.32 | convolution fusion | flops 3238789120 | bytes 10504192 | tf_op jit(solution)/shard_map/dot_general | solution.py:40
  194.6 10.9 %collective-permute-done.4 = bf16[1,1,512,512]{3,2,1,0:T(8,128)(2,1)S(1)} collective-permute-done((bf16[1,1,512,512]{3,2,1,0:T(8,128)(2,1)S(1)}, bf16[1,1,512,512]{3,2,1,0:T(8,128)(2,1)S(1)}, u32[]{:S(2)}, u32[]{:S(2)}) %collective-permute-start.4) | collective-permute-done | bytes 524320 | tf_op jit(solution)/shard_map/ppermute | solution.py:17
  206.8 2.8 collective-permute-start.6
  209.6 2.3 collective-permute-start.7
  212.4 17.1 %gather_fusion.2 = f32[4096,512]{1,0:T(8,128)} fusion(f32[512,512]{1,0:T(8,128)S(1)} %fusion.33, s32[4096]{0:T(1024)S(1)} %broadcast_clamp_fusion.1), kind=kCustom, calls=%fused_computation.2 | custom fusion | bytes 16793600 | tf_op jit(solution)/shard_map/jit(_take)/gather | solution.py:124
  229.5 2.3 collective-permute-done.7
  233.9 4.3 %convolution_convert_fusion.2 = bf16[4608,512]{1,0:T(8,128)(2,1)} fusion(bf16[4608,512]{1,0:T(8,128)(2,1)S(1)} %bitcast.85, bf16[512,512]{1,0:T(8,128)(2,1)S(1)} %copy-done.18), kind=kOutput, calls=%fused_computation.12 | convolution fusion | flops 2418278400 | bytes 9961472 | tf_op jit(solution)/shard_map/dot_general | solution.py:65
  238.2 20.4 %gather_fusion.1 = bf16[4096,512]{1,0:T(8,128)(2,1)} fusion(bf16[4608,512]{1,0:T(8,128)(2,1)} %convolution_convert_fusion.2, s32[4096]{0:T(1024)S(1)} %broadcast_clamp_fusion.2), kind=kCustom, calls=%fused_computation.1 | custom fusion | bytes 8404992 | tf_op jit(solution)/shard_map/jit(_take)/gather | solution.py:124
  258.7 12.3 %multiply_convert_fusion.1 = bf16[4096,512]{1,0:T(8,128)(2,1)S(1)} fusion(f32[4096,512]{1,0:T(8,128)} %gather_fusion.2, f32[4,512]{1,0:T(4,128)S(1)} %copy-done.28, bf16[4096,512]{1,0:T(8,128)(2,1)} %gather_fusion.1, pred[4096]{0:T(1024)(128)(4,1)S(1)} %get-tuple-element.11, pred[4096]{0:T(1024)(128)(4,1)S(1)} %get-tuple-element.12, ...), kind=kOutput, calls=%fused_computation.8 | convolution fusion | flops 121634816 | bytes 16859136 | tf_op jit(solution)/shard_map/fe,fl->el/dot_general | solution.py:33
  271.0 3.8 %select_convert_fusion = bf16[4096,512]{1,0:T(8,128)(2,1)} fusion(bf16[4096,512]{1,0:T(8,128)(2,1)S(1)} %multiply_convert_fusion.1, bf16[512,512]{1,0:T(8,128)(2,1)S(1)} %copy-done.19, pred[4096]{0:T(1024)(128)(4,1)S(1)} %iota_compare_fusion.10), kind=kOutput, calls=%fused_computation.7 | convolution fusion | flops 2151677952 | bytes 8916992 | tf_op jit(solution)/shard_map/dot_general | solution.py:46
  274.8 5.9 %fusion.9 = f32[512,512]{1,0:T(8,128)} fusion(bf16[512,512]{1,0:T(8,128)(2,1)S(1)} %copy-done.20, bf16[4096,512]{1,0:T(8,128)(2,1)} %select_convert_fusion, s32[4096]{0:T(1024)S(1)} %bitcast.89), kind=kOutput, calls=%fused_computation.33 | convolution fusion | flops 2418278400 | bytes 5783552 | tf_op jit(solution)/shard_map/dot_general | solution.py:132
  286.2 9.8 %collective-permute-done.8 = bf16[1,1,512,512]{3,2,1,0:T(8,128)(2,1)S(1)} collective-permute-done((bf16[1,1,512,512]{3,2,1,0:T(8,128)(2,1)S(1)}, bf16[1,1,512,512]{3,2,1,0:T(8,128)(2,1)S(1)}, u32[]{:S(2)}, u32[]{:S(2)}) %collective-permute-start.8) | collective-permute-done | bytes 524320 | tf_op jit(solution)/shard_map/ppermute | solution.py:17
  296.2 3.9 %collective-permute-start.10 = (bf16[1,3,512,512]{3,2,1,0:T(8,128)(2,1)S(1)}, bf16[1,3,512,512]{3,2,1,0:T(8,128)(2,1)S(1)}, u32[]{:S(2)}, u32[]{:S(2)}) collective-permute-start(bf16[1,3,512,512]{3,2,1,0:T(8,128)(2,1)S(1)} %pad_maximum_fusion.5), channel_id=1, source_target_pairs={{0,4},{4,8},{8,12},{12,16},{16,20},{20,24},{24,28},{28,32},{32,36}... | collective-permute-start | bytes 4718600 | tf_op jit(solution)/shard_map/ppermute | solution.py:17
  300.1 3.3 collective-permute-start.11
  303.4 3.3 fusion.34
  306.8 10.6 %collective-permute-done.10 = bf16[1,3,512,512]{3,2,1,0:T(8,128)(2,1)S(1)} collective-permute-done((bf16[1,3,512,512]{3,2,1,0:T(8,128)(2,1)S(1)}, bf16[1,3,512,512]{3,2,1,0:T(8,128)(2,1)S(1)}, u32[]{:S(2)}, u32[]{:S(2)}) %collective-permute-start.10) | collective-permute-done | bytes 1572896 | tf_op jit(solution)/shard_map/ppermute | solution.py:17
  317.4 4.7 %collective-permute-done.11 = bf16[1,3,512,512]{3,2,1,0:T(8,128)(2,1)S(1)} collective-permute-done((bf16[1,3,512,512]{3,2,1,0:T(8,128)(2,1)S(1)}, bf16[1,3,512,512]{3,2,1,0:T(8,128)(2,1)S(1)}, u32[]{:S(2)}, u32[]{:S(2)}) %collective-permute-start.11) | collective-permute-done | bytes 1572896 | tf_op jit(solution)/shard_map/ppermute | solution.py:19
  322.7 4.2 %convolution_convert_fusion.1 = bf16[4608,512]{1,0:T(8,128)(2,1)} fusion(bf16[4608,512]{1,0:T(8,128)(2,1)S(1)} %bitcast.84, bf16[512,512]{1,0:T(8,128)(2,1)S(1)} %copy-done.23), kind=kOutput, calls=%fused_computation.11 | convolution fusion | flops 2418278400 | bytes 9961472 | tf_op jit(solution)/shard_map/dot_general | solution.py:65
  326.9 28.7 %gather_fusion.3 = bf16[6144,512]{1,0:T(8,128)(2,1)} fusion(bf16[4608,512]{1,0:T(8,128)(2,1)} %convolution_convert_fusion.1, s32[6144]{0:T(1024)S(1)} %broadcast_clamp_fusion), kind=kCustom, calls=%fused_computation.3 | custom fusion | bytes 12607488 | tf_op jit(solution)/shard_map/jit(_take)/gather | solution.py:141
  355.6 7.2 %fusion.1 = bf16[2048,512]{1,0:T(8,128)(2,1)S(1)} fusion(f32[2048,512]{1,0:T(8,128)} %fusion.34, bf16[3,2048,512]{2,1,0:T(8,128)(2,1)} %bitcast.74, pred[3,2048]{1,0:T(4,128)(4,1)S(1)} %compare_and_fusion), kind=kLoop, calls=%fused_computation.17 | loop fusion | flops 27262976 | bytes 12589056 | tf_op jit(solution)/shard_map/reduce_sum | solution.py:143
  362.9 4.9 %fusion.5 = f32[1,1,2048,227]{2,3,1,0:T(8,128)} fusion(bf16[512,227]{0,1:T(8,128)(2,1)S(1)} %copy-done.25, bf16[1,1,2048,227]{2,3,1,0:T(8,128)(2,1)} %param.30, bf16[2048,512]{1,0:T(8,128)(2,1)S(1)} %fusion.1, bf16[512,512]{1,0:T(8,128)(2,1)S(1)} %copy-done.24), kind=kOutput, calls=%fused_computation.26 | convolution fusion | flops 1555968000 | bytes 5643264 | tf_op jit(solution)/shard_map/dot_general | solution.py:145
  367.8 4.7 %copy.32 = f32[1,1,2048,227]{2,1,3,0:T(1,128)} copy(f32[1,1,2048,227]{2,3,1,0:T(8,128)} %fusion.5) | data formatting | bytes 3719168 | tf_op jit(solution)/shard_map/broadcast_in_dim | solution.py:148
  (96 shorter events, 19.5 us)
Async XLA Ops:
  0.0 136.8 %copy-start = (bf16[512,512]{1,0:T(8,128)(2,1)S(1)}, bf16[512,512]{1,0:T(8,128)(2,1)}, u32[]{:S(2)}) copy-start(bf16[512,512]{1,0:T(8,128)(2,1)} %param.42) | copy-start | bytes 1572868
  2.6 125.9 %copy-start.2 = (bf16[2048,512]{1,0:T(8,128)(2,1)}, bf16[2048,512]{1,0:T(8,128)(2,1)S(1)}, u32[]{:S(2)}) copy-start(bf16[2048,512]{1,0:T(8,128)(2,1)S(1)} %multiply_convert_fusion.4) | copy-start | bytes 6291460
  2.6 56.7 %copy-start.11 = (s32[1,1,3072]{2,1,0:T(1,128)S(1)}, s32[1,1,3072]{2,1,0:T(1,128)}, u32[]{:S(2)}) copy-start(s32[1,1,3072]{2,1,0:T(1,128)} %param.32) | copy-start | bytes 36868
  2.7 56.8 %copy-start.10 = (f32[1,1,4,3072]{3,2,1,0:T(4,128)S(1)}, f32[1,1,4,3072]{3,2,1,0:T(4,128)}, u32[]{:S(2)}) copy-start(f32[1,1,4,3072]{3,2,1,0:T(4,128)} %param.34) | copy-start | bytes 147460
  2.7 56.8 %copy-start.12 = (f32[4,512]{1,0:T(4,128)S(1)}, f32[4,512]{1,0:T(4,128)}, u32[]{:S(2)}) copy-start(f32[4,512]{1,0:T(4,128)} %param.43) | copy-start | bytes 24580
  2.7 47.9 %collective-permute-start = (bf16[1,1,2048,512]{3,2,1,0:T(8,128)(2,1)S(1)}, bf16[1,1,2048,512]{3,2,1,0:T(8,128)(2,1)S(1)}, u32[]{:S(2)}, u32[]{:S(2)}) collective-permute-start(bf16[1,1,2048,512]{3,2,1,0:T(8,128)(2,1)S(1)} %bitcast.75), channel_id=1, source_target_pairs={{0,1},{1,2},{2,3},{3,0},{4,5},{5,6},{6,7},{7,4},{8,9},{9,10},{10,1... | collective-permute-start | bytes 6291464 | tf_op jit(solution)/shard_map/ppermute | solution.py:17
  4.0 46.6 %collective-permute-start.1 = (bf16[1,1,2048,512]{3,2,1,0:T(8,128)(2,1)S(1)}, bf16[1,1,2048,512]{3,2,1,0:T(8,128)(2,1)S(1)}, u32[]{:S(2)}, u32[]{:S(2)}) collective-permute-start(bf16[1,1,2048,512]{3,2,1,0:T(8,128)(2,1)S(1)} %bitcast.76), channel_id=1, source_target_pairs={{1,0},{2,1},{3,2},{0,3},{5,4},{6,5},{7,6},{4,7},{9,8},{10,9},{11,1... | collective-permute-start | bytes 6291464 | tf_op jit(solution)/shard_map/ppermute | solution.py:19
  51.4 72.8 %collective-permute-start.2 = (bf16[1,3,2048,512]{3,2,1,0:T(8,128)(2,1)S(1)}, bf16[1,3,2048,512]{3,2,1,0:T(8,128)(2,1)S(1)}, u32[]{:S(2)}, u32[]{:S(2)}) collective-permute-start(bf16[1,3,2048,512]{3,2,1,0:T(8,128)(2,1)S(1)} %pad_maximum_fusion.1), channel_id=1, source_target_pairs={{0,4},{4,8},{8,12},{12,16},{16,20},{20,24},{24,28},{28,32},{32,36}... | collective-permute-start | bytes 18874376 | tf_op jit(solution)/shard_map/ppermute | solution.py:17
  56.3 72.3 %collective-permute-start.3 = (bf16[1,3,2048,512]{3,2,1,0:T(8,128)(2,1)S(1)}, bf16[1,3,2048,512]{3,2,1,0:T(8,128)(2,1)S(1)}, u32[]{:S(2)}, u32[]{:S(2)}) collective-permute-start(bf16[1,3,2048,512]{3,2,1,0:T(8,128)(2,1)S(1)} %pad_maximum_fusion.1), channel_id=1, source_target_pairs={{4,0},{8,4},{12,8},{16,12},{20,16},{24,20},{28,24},{32,28},{36,32}... | collective-permute-start | bytes 18874376 | tf_op jit(solution)/shard_map/ppermute | solution.py:19
  157.0 22.4 %copy-start.15 = (bf16[512,512]{1,0:T(8,128)(2,1)S(1)}, bf16[512,512]{1,0:T(8,128)(2,1)}, u32[]{:S(2)}) copy-start(bf16[512,512]{1,0:T(8,128)(2,1)} %param.44) | copy-start | bytes 1572868
  157.0 22.4 %copy-start.27 = (s32[1,1,3072]{2,1,0:T(1,128)S(1)}, s32[1,1,3072]{2,1,0:T(1,128)}, u32[]{:S(2)}) copy-start(s32[1,1,3072]{2,1,0:T(1,128)} %param.33) | copy-start | bytes 36868
  179.4 8.9 %copy-start.16 = (bf16[512,512]{1,0:T(8,128)(2,1)S(1)}, bf16[512,512]{1,0:T(8,128)(2,1)}, u32[]{:S(2)}) copy-start(bf16[512,512]{1,0:T(8,128)(2,1)} %param.46) | copy-start | bytes 1572868
  179.4 8.9 %copy-start.17 = (bf16[512,512]{1,0:T(8,128)(2,1)S(1)}, bf16[512,512]{1,0:T(8,128)(2,1)}, u32[]{:S(2)}) copy-start(bf16[512,512]{1,0:T(8,128)(2,1)} %param.45) | copy-start | bytes 1572868
  190.4 21.4 %copy-start.9 = (s32[1,1,4096]{2,1,0:T(1,128)S(1)}, s32[1,1,4096]{2,1,0:T(1,128)}, u32[]{:S(2)}) copy-start(s32[1,1,4096]{2,1,0:T(1,128)} %param.37) | copy-start | bytes 49156
  190.4 21.5 %copy-start.6 = (bf16[512,512]{1,0:T(8,128)(2,1)S(1)}, bf16[512,512]{1,0:T(8,128)(2,1)}, u32[]{:S(2)}) copy-start(bf16[512,512]{1,0:T(8,128)(2,1)} %param.49) | copy-start | bytes 1572868
  191.0 14.5 %collective-permute-start.4 = (bf16[1,1,512,512]{3,2,1,0:T(8,128)(2,1)S(1)}, bf16[1,1,512,512]{3,2,1,0:T(8,128)(2,1)S(1)}, u32[]{:S(2)}, u32[]{:S(2)}) collective-permute-start(bf16[1,1,512,512]{3,2,1,0:T(8,128)(2,1)S(1)} %bitcast.80), channel_id=1, source_target_pairs={{0,1},{1,2},{2,3},{3,0},{4,5},{5,6},{6,7},{7,4},{8,9},{9,10},{10,1... | collective-permute-start | bytes 1572872 | tf_op jit(solution)/shard_map/ppermute | solution.py:17
  192.4 13.1 %collective-permute-start.5 = (bf16[1,1,512,512]{3,2,1,0:T(8,128)(2,1)S(1)}, bf16[1,1,512,512]{3,2,1,0:T(8,128)(2,1)S(1)}, u32[]{:S(2)}, u32[]{:S(2)}) collective-permute-start(bf16[1,1,512,512]{3,2,1,0:T(8,128)(2,1)S(1)} %bitcast.81), channel_id=1, source_target_pairs={{1,0},{2,1},{3,2},{0,3},{5,4},{6,5},{7,6},{4,7},{9,8},{10,9},{11,1... | collective-permute-start | bytes 1572872 | tf_op jit(solution)/shard_map/ppermute | solution.py:19
  206.8 22.7 %collective-permute-start.6 = (bf16[1,3,512,512]{3,2,1,0:T(8,128)(2,1)}, bf16[1,3,512,512]{3,2,1,0:T(8,128)(2,1)}, u32[]{:S(2)}, u32[]{:S(2)}) collective-permute-start(bf16[1,3,512,512]{3,2,1,0:T(8,128)(2,1)} %pad_maximum_fusion.4), channel_id=1, source_target_pairs={{0,4},{4,8},{8,12},{12,16},{16,20},{20,24},{24,28},{28,32},{32,36}... | collective-permute-start | bytes 4718600 | tf_op jit(solution)/shard_map/ppermute | solution.py:17
  209.6 22.2 %collective-permute-start.7 = (bf16[1,3,512,512]{3,2,1,0:T(8,128)(2,1)}, bf16[1,3,512,512]{3,2,1,0:T(8,128)(2,1)}, u32[]{:S(2)}, u32[]{:S(2)}) collective-permute-start(bf16[1,3,512,512]{3,2,1,0:T(8,128)(2,1)} %pad_maximum_fusion.4), channel_id=1, source_target_pairs={{4,0},{8,4},{12,8},{16,12},{20,16},{24,20},{28,24},{32,28},{36,32}... | collective-permute-start | bytes 4718600 | tf_op jit(solution)/shard_map/ppermute | solution.py:19
  238.2 20.5 %copy-start.26 = (f32[1,1,4,4096]{3,2,1,0:T(4,128)S(1)}, f32[1,1,4,4096]{3,2,1,0:T(4,128)}, u32[]{:S(2)}) copy-start(f32[1,1,4,4096]{3,2,1,0:T(4,128)} %param.38) | copy-start | bytes 196612
  238.2 20.5 %copy-start.28 = (f32[4,512]{1,0:T(4,128)S(1)}, f32[4,512]{1,0:T(4,128)}, u32[]{:S(2)}) copy-start(f32[4,512]{1,0:T(4,128)} %param.50) | copy-start | bytes 24580
  258.7 12.3 %copy-start.19 = (bf16[512,512]{1,0:T(8,128)(2,1)S(1)}, bf16[512,512]{1,0:T(8,128)(2,1)}, u32[]{:S(2)}) copy-start(bf16[512,512]{1,0:T(8,128)(2,1)} %param.51) | copy-start | bytes 1572868
  282.9 20.5 %copy-start.7 = (s32[1,1,3,2048]{3,1,2,0:T(1,128)S(1)}, s32[1,1,3,2048]{3,1,2,0:T(1,128)}, u32[]{:S(2)}) copy-start(s32[1,1,3,2048]{3,1,2,0:T(1,128)} %param.40) | copy-start | bytes 73732
  282.9 20.5 %copy-start.3 = (bf16[2048,512]{1,0:T(8,128)(2,1)S(1)}, bf16[2048,512]{1,0:T(8,128)(2,1)}, u32[]{:S(2)}) copy-start(bf16[2048,512]{1,0:T(8,128)(2,1)} %copy-done.2) | copy-start | bytes 6291460
  282.9 20.5 %copy-start.5 = (bf16[512,512]{1,0:T(8,128)(2,1)S(1)}, bf16[512,512]{1,0:T(8,128)(2,1)}, u32[]{:S(2)}) copy-start(bf16[512,512]{1,0:T(8,128)(2,1)} %param.57) | copy-start | bytes 1572868
  283.5 12.5 %collective-permute-start.8 = (bf16[1,1,512,512]{3,2,1,0:T(8,128)(2,1)S(1)}, bf16[1,1,512,512]{3,2,1,0:T(8,128)(2,1)S(1)}, u32[]{:S(2)}, u32[]{:S(2)}) collective-permute-start(bf16[1,1,512,512]{3,2,1,0:T(8,128)(2,1)S(1)} %fusion.13), channel_id=1, source_target_pairs={{0,1},{1,2},{2,3},{3,0},{4,5},{5,6},{6,7},{7,4},{8,9},{9,10},{10,1... | collective-permute-start | bytes 1572872 | tf_op jit(solution)/shard_map/ppermute | solution.py:17
  284.5 11.5 %collective-permute-start.9 = (bf16[1,1,512,512]{3,2,1,0:T(8,128)(2,1)S(1)}, bf16[1,1,512,512]{3,2,1,0:T(8,128)(2,1)S(1)}, u32[]{:S(2)}, u32[]{:S(2)}) collective-permute-start(bf16[1,1,512,512]{3,2,1,0:T(8,128)(2,1)S(1)} %fusion.13), channel_id=1, source_target_pairs={{1,0},{2,1},{3,2},{0,3},{5,4},{6,5},{7,6},{4,7},{9,8},{10,9},{11,1... | collective-permute-start | bytes 1572872 | tf_op jit(solution)/shard_map/ppermute | solution.py:19
  296.2 21.2 %collective-permute-start.10 = (bf16[1,3,512,512]{3,2,1,0:T(8,128)(2,1)S(1)}, bf16[1,3,512,512]{3,2,1,0:T(8,128)(2,1)S(1)}, u32[]{:S(2)}, u32[]{:S(2)}) collective-permute-start(bf16[1,3,512,512]{3,2,1,0:T(8,128)(2,1)S(1)} %pad_maximum_fusion.5), channel_id=1, source_target_pairs={{0,4},{4,8},{8,12},{12,16},{16,20},{20,24},{24,28},{28,32},{32,36}... | collective-permute-start | bytes 4718600 | tf_op jit(solution)/shard_map/ppermute | solution.py:17
  300.1 22.0 %collective-permute-start.11 = (bf16[1,3,512,512]{3,2,1,0:T(8,128)(2,1)S(1)}, bf16[1,3,512,512]{3,2,1,0:T(8,128)(2,1)S(1)}, u32[]{:S(2)}, u32[]{:S(2)}) collective-permute-start(bf16[1,3,512,512]{3,2,1,0:T(8,128)(2,1)S(1)} %pad_maximum_fusion.5), channel_id=1, source_target_pairs={{4,0},{8,4},{12,8},{16,12},{20,16},{24,20},{28,24},{32,28},{36,32}... | collective-permute-start | bytes 4718600 | tf_op jit(solution)/shard_map/ppermute | solution.py:19
  306.8 15.9 %copy-start.23 = (bf16[512,512]{1,0:T(8,128)(2,1)S(1)}, bf16[512,512]{1,0:T(8,128)(2,1)}, u32[]{:S(2)}) copy-start(bf16[512,512]{1,0:T(8,128)(2,1)} %param.56) | copy-start | bytes 1572868
  355.6 7.2 %copy-start.25 = (bf16[512,227]{0,1:T(8,128)(2,1)S(1)}, bf16[512,227]{0,1:T(8,128)(2,1)}, u32[]{:S(2)}) copy-start(bf16[512,227]{0,1:T(8,128)(2,1)} %param.59) | copy-start | bytes 697348
  362.8 9.6 %copy-start.1 = (bf16[512,512]{1,0:T(8,128)(2,1)S(1)}, bf16[512,512]{1,0:T(8,128)(2,1)}, u32[]{:S(2)}) copy-start(bf16[512,512]{1,0:T(8,128)(2,1)} %param.42) | copy-start | bytes 1572868
  (9 other events, 40.0 us)
where the time goes:
time: 380 us; the launch traced here: 373 us
  waiting for transfers between devices  145 us (38%)
  local copies, waits for them, and re-layouts  93.4 us (25%)
  matrix products  82.2 us (22%)
  starting transfers between devices  28.1 us (7%)
  other arithmetic  21.6 us (6%)
    ppermute x6, waiting for transfers between devices, extended(): lax.ppermute(tail, axis, [(i, (i + 1) % count) for i in range(ends)])  134 us
    dot_general x3, matrix products, project(): jnp.dot(values, weight, preferred_element_type=jnp.float32)  28.8 us
    gather x1, local copies, waits for them, and re-layouts, shards(): jnp.take(cycle_out, decode_senders[0, 0], axis=0).astype(jnp.float32)  28.7 us
    gather x1, local copies, waits for them, and re-layouts, shards(): rows = jnp.take(cycle_source, senders, axis=0).astype(jnp.float32)  22.4 us
    gather x1, local copies, waits for them, and re-layouts, shards(): jnp.take(cycle_mesh, mesh_senders[0, 0], axis=0).astype(jnp.float32)  20.4 us
    dot_general x2, matrix products, geometry_term(): jnp.einsum('fe,fl->el', geometry, weight, precision=lax.Precision.HIGHEST)  19.3 us
    gather x1, local copies, waits for them, and re-layouts, shards(): jnp.take(target_mesh, receivers, axis=0)  17.1 us
    ppermute x6, starting transfers between devices, extended(): lax.ppermute(tail, axis, [(i, (i + 1) % count) for i in range(ends)])  15.4 us
  transfers between devices with their start and end apart: 12, of which 8 were waited for; matrix products, arithmetic and copies ran while one was open for 8% of the time, Pallas kernels for 0%

commit v1 on v0

v1 whole, which is shorter than its diff:
```python
import functools

import jax
import jax.numpy as jnp
from jax import lax
from jax.experimental import pallas as pl
from jax.experimental.pallas import tpu as pltpu
from jax.sharding import PartitionSpec as P

EPSILON = 1e-05
BF16 = jnp.bfloat16
F32 = jnp.float32
LANES = 128
VMEM_BYTES = 56 * 1024 * 1024

VMEM = pl.BlockSpec(memory_space=pltpu.VMEM)
SMEM = pl.BlockSpec(memory_space=pltpu.SMEM)
ANY = pl.BlockSpec(memory_space=pl.ANY)


def params():
    return pltpu.CompilerParams(vmem_limit_bytes=VMEM_BYTES)


def cost(flops, moved):
    return pl.CostEstimate(flops=flops, bytes_accessed=moved, transcendentals=0)


def silu(values):
    half = 0.5 * values
    return half + half * jnp.tanh(half)


def layer_norm(values, gain):
    centre = values - jnp.mean(values, axis=-1, keepdims=True)
    spread = jnp.mean(centre * centre, axis=-1, keepdims=True)
    return centre * lax.rsqrt(spread + EPSILON) * gain


def dot(a, b):
    return jnp.dot(a, b, preferred_element_type=F32)


def dot_rows(a, b):
    return lax.dot_general(a, b, (((0,), (0,)), ((), ())), preferred_element_type=F32)


def put_table(ref, first, values):
    parts = values.shape[1] // LANES
    for part in range(parts):
        ref[pl.ds(first * parts + part, values.shape[0], stride=parts), :] = values[
            :, part * LANES : (part + 1) * LANES
        ]


def gather(index, first, count, table, rows, parts, unroll=32):
    def body(step, carry):
        for slot in range(unroll):
            edge = step * unroll + slot
            start = pl.multiple_of(index[first + edge], parts)
            rows[pl.ds(pl.multiple_of(edge * parts, parts), parts), :] = table[
                pl.ds(start, parts), :
            ]
        return carry

    lax.fori_loop(0, count // unroll, body, 0)


def onehot(receivers, nodes):
    ids = lax.broadcasted_iota(jnp.int32, (nodes, receivers.shape[1]), 0)
    return jnp.where(ids == receivers, 1.0, 0.0).astype(BF16)


def own_kernel(fields, embed_weight, source_weight, embedded, table):
    values = silu(dot(fields[...], embed_weight[...])).astype(BF16)
    embedded[...] = values
    put_table(table, 0, dot(values, source_weight[...]).astype(BF16).astype(F32))


def embed_own(fields, embed_weight, source_weight):
    cells, channels = fields.shape
    width = embed_weight.shape[1]
    parts = width // LANES
    tile = 512
    return pl.pallas_call(
        own_kernel,
        grid=(cells // tile,),
        in_specs=[
            pl.BlockSpec((tile, channels), lambda i: (i, 0)),
            pl.BlockSpec((channels, width), lambda i: (0, 0)),
            pl.BlockSpec((width, width), lambda i: (0, 0)),
        ],
        out_specs=[
            pl.BlockSpec((tile, width), lambda i: (i, 0)),
            pl.BlockSpec((tile * parts, LANES), lambda i: (i, 0)),
        ],
        out_shape=[
            jax.ShapeDtypeStruct((cells, width), BF16),
            jax.ShapeDtypeStruct((cells * parts, LANES), F32),
        ],
        compiler_params=params(),
        cost_estimate=cost(2 * cells * width * (width + 256), 8 * 2**20),
    )(fields, embed_weight, source_weight)


def encode_kernel(
    index, strip_w, strip_e, strip_o, strip_n, strip_oc, strip_nc, own_table, receivers,
    geometry, edge_weight, embed_weight, source_weight, second, first_weight, node_second,
    gain, static, next_source, mesh_start, next_table,
    table, rows, total, wide, own_sem,
):
    cells = own_table.shape[0]
    parts = second.shape[0] // LANES
    copy = pltpu.make_async_copy(own_table, table.at[pl.ds(0, cells)], own_sem)
    copy.start()
    strips = [strip_w[...], strip_e[...], strip_o[...], strip_n[...]]
    strips += [strip_oc[0], strip_oc[1], strip_nc[0], strip_nc[1]]
    for slot, strip in enumerate(strips):
        values = silu(dot(strip, embed_weight[...])).astype(BF16)
        values = dot(values, source_weight[...]).astype(BF16).astype(F32)
        put_table(table, cells // parts + slot * strip.shape[0], values)
    copy.wait()
    edges = receivers.shape[1]
    gather(index, 0, edges, table, rows, parts)
    total[...] = jnp.zeros_like(total)
    tile = 512

    def step(i, carry):
        begin = pl.multiple_of(i * tile, tile)
        shift = dot_rows(geometry[:, pl.ds(begin, tile)], edge_weight[...])
        hidden = [
            silu(
                rows[pl.ds(begin * parts + part, tile, stride=parts), :]
                + shift[:, part * LANES : (part + 1) * LANES]
            ).astype(BF16)
            for part in range(parts)
        ]
        picks = onehot(receivers[:, pl.ds(begin, tile)], total.shape[0])
        total[...] += dot(picks, jnp.concatenate(hidden, axis=1))
        return carry

    lax.fori_loop(0, edges // tile, step, 0)
    gathered = dot(total[...].astype(BF16), second[...]).astype(BF16)
    node_hidden = silu(dot(gathered, first_weight[...])).astype(BF16)
    normed = layer_norm(dot(node_hidden, node_second[...]), gain[...])
    start = (static[...].astype(F32) + normed).astype(BF16)
    mesh_start[...] = start
    put_table(wide, 0, dot(start, next_source[...]))
    next_table[...] = wide[...].astype(BF16)


def encode(index, strips, own_table, receivers, geometry, edge_weight, weights, static):
    nodes, width = static.shape
    parts = width // LANES
    strip = strips[0].shape[0]
    edges = receivers.shape[1]
    return pl.pallas_call(
        encode_kernel,
        in_specs=[SMEM] + [VMEM] * 6 + [ANY] + [VMEM] * 11,
        out_specs=[VMEM, VMEM],
        out_shape=[
            jax.ShapeDtypeStruct((nodes, width), BF16),
            jax.ShapeDtypeStruct((nodes * parts, LANES), BF16),
        ],
        scratch_shapes=[
            pltpu.VMEM((own_table.shape[0] + 8 * strip * parts, LANES), F32),
            pltpu.VMEM((edges * parts, LANES), F32),
            pltpu.VMEM((nodes, width), F32),
            pltpu.VMEM((nodes * parts, LANES), F32),
            pltpu.SemaphoreType.DMA,
        ],
        compiler_params=params(),
        cost_estimate=cost(2 * edges * width * 2 * width, 10 * 2**20),
    )(
        index, *strips, own_table, receivers, geometry, edge_weight,
        weights[0], weights[1], weights[2], weights[3], weights[4], weights[5], static, weights[6],
    )


def receive_kernel(
    start, target_weight, state_weight, receivers, geometry, edge_weight, shift, state, target
):
    @pl.when(pl.program_id(0) == 0)
    def _():
        target[...] = dot(start[...], target_weight[...]).astype(BF16)
        state[...] = dot(start[...], state_weight[...])

    picks = onehot(receivers[...], start.shape[0])
    shift[...] = (
        dot_rows(picks, target[...]) + dot_rows(geometry[...], edge_weight[...])
    ).astype(BF16)


def receive(start, target_weight, state_weight, receivers, geometry, edge_weight):
    nodes, width = start.shape
    edges = receivers.shape[1]
    tile = 512
    whole = lambda i: (0, 0)
    return pl.pallas_call(
        receive_kernel,
        grid=(edges // tile,),
        in_specs=[
            pl.BlockSpec((nodes, width), whole),
            pl.BlockSpec((width, width), whole),
            pl.BlockSpec((width, width), whole),
            pl.BlockSpec((1, tile), lambda i: (0, i)),
            pl.BlockSpec((geometry.shape[0], tile), lambda i: (0, i)),
            pl.BlockSpec(edge_weight.shape, whole),
        ],
        out_specs=[
            pl.BlockSpec((tile, width), lambda i: (i, 0)),
            pl.BlockSpec((nodes, width), whole),
        ],
        out_shape=[
            jax.ShapeDtypeStruct((edges, width), BF16),
            jax.ShapeDtypeStruct((nodes, width), F32),
        ],
        scratch_shapes=[pltpu.VMEM((nodes, width), BF16)],
        compiler_params=params(),
        cost_estimate=cost(2 * edges * width * 2 * width, 8 * 2**20),
    )(start, target_weight, state_weight, receivers, geometry, edge_weight)


def load_table(blocks, stage, table, sems):
    copies = []
    for slot, (ref, first) in enumerate(blocks):
        count = ref.shape[0]
        copy = pltpu.make_async_copy(ref, stage.at[pl.ds(first, count)], sems.at[slot])
        copy.start()
        copies.append(copy)
    for copy, (ref, first) in zip(copies, blocks):
        copy.wait()
        span = pl.ds(first, ref.shape[0])
        table[span, :] = stage[span, :].astype(F32)


def table_blocks(own, w, e, o, n, oc, ow, oe, nw, ne):
    size = own.shape[0]
    half = size // 2
    blocks = [(ref, slot * size) for slot, ref in enumerate((own, w, e, o, n))]
    blocks += [(oc.at[0], 5 * size), (ow, 5 * size + half)]
    blocks += [(oc.at[1], 6 * size), (oe, 6 * size + half)]
    return blocks + [(nw, 7 * size), (ne, 8 * size)]


def process_kernel(
    index, own, w, e, o, n, oc, ow, oe, nw, ne, receivers, shift, state, start, second,
    message_weight, out_weight, gain, next_source, next_table,
    stage, table, rows, total, wide, sems,
):
    parts = second.shape[0] // LANES
    load_table(table_blocks(own, w, e, o, n, oc, ow, oe, nw, ne), stage, table, sems)
    edges = receivers.shape[1]
    gather(index, 0, edges, table, rows, parts)
    total[...] = jnp.zeros_like(total)
    tile = 512

    def step(i, carry):
        begin = pl.multiple_of(i * tile, tile)
        hidden = [
            silu(
                rows[pl.ds(begin * parts + part, tile, stride=parts), :]
                + shift[pl.ds(begin, tile), part * LANES : (part + 1) * LANES].astype(F32)
            ).astype(BF16)
            for part in range(parts)
        ]
        picks = onehot(receivers[:, pl.ds(begin, tile)], total.shape[0])
        total[...] += dot(picks, jnp.concatenate(hidden, axis=1))
        return carry

    lax.fori_loop(0, edges // tile, step, 0)
    summed = dot(total[...].astype(BF16), second[...]).astype(BF16)
    update = silu(dot(summed, message_weight[...]) + state[...]).astype(BF16)
    normed = layer_norm(dot(update, out_weight[...]), gain[...])
    end = (start[...].astype(F32) + normed).astype(BF16)
    put_table(wide, 0, dot(end, next_source[...]))
    next_table[...] = wide[...].astype(BF16)


def process(index, blocks, receivers, shift, state, start, weights):
    nodes, width = start.shape
    parts = width // LANES
    edges = receivers.shape[1]
    return pl.pallas_call(
        process_kernel,
        in_specs=[SMEM] + [ANY] * 10 + [VMEM] * 9,
        out_specs=VMEM,
        out_shape=jax.ShapeDtypeStruct((nodes * parts, LANES), BF16),
        scratch_shapes=[
            pltpu.VMEM((9 * nodes * parts, LANES), BF16),
            pltpu.VMEM((9 * nodes * parts, LANES), F32),
            pltpu.VMEM((edges * parts, LANES), F32),
            pltpu.VMEM((nodes, width), F32),
            pltpu.VMEM((nodes * parts, LANES), F32),
            pltpu.SemaphoreType.DMA((11,)),
        ],
        compiler_params=params(),
        cost_estimate=cost(2 * edges * width * 2 * width, 12 * 2**20),
    )(index, *blocks, receivers, shift, state, start, *weights)


def decode_kernel(
    index, own, w, e, o, n, oc, ow, oe, nw, ne, embedded, fields, target_weight, hidden_weight,
    output_weight, prediction, stage, table, rows, sems,
):
    tile, width = embedded.shape
    parts = width // LANES
    step = pl.program_id(0)

    @pl.when(step == 0)
    def _():
        load_table(table_blocks(own, w, e, o, n, oc, ow, oe, nw, ne), stage, table, sems)

    senders = 3
    gather(index, step * (senders * tile), senders * tile, table, rows, parts)
    target = dot(embedded[...], target_weight[...])
    summed = []
    for part in range(parts):
        here = target[:, part * LANES : (part + 1) * LANES]
        edge = [
            silu(rows[pl.ds(k * tile * parts + part, tile, stride=parts), :] + here).astype(BF16)
            for k in range(senders)
        ]
        summed.append((edge[0].astype(F32) + edge[1].astype(F32) + edge[2].astype(F32)).astype(BF16))
    final = silu(dot(jnp.concatenate(summed, axis=1), hidden_weight[...])).astype(BF16)
    prediction[...] = fields[...].astype(F32) + dot(final, output_weight[...])


DECODE_TILE = 256


def decode(index, blocks, embedded, fields, target_weight, hidden_weight, output_weight):
    cells, width = embedded.shape
    channels = fields.shape[1]
    parts = width // LANES
    size = blocks[0].shape[0]
    tile = DECODE_TILE
    whole = lambda i: (0, 0)
    return pl.pallas_call(
        decode_kernel,
        grid=(cells // tile,),
        in_specs=[SMEM]
        + [ANY] * 10
        + [
            pl.BlockSpec((tile, width), lambda i: (i, 0)),
            pl.BlockSpec((tile, channels), lambda i: (i, 0)),
            pl.BlockSpec((width, width), whole),
            pl.BlockSpec((width, width), whole),
            pl.BlockSpec((width, channels), whole),
        ],
        out_specs=pl.BlockSpec((tile, channels), lambda i: (i, 0)),
        out_shape=jax.ShapeDtypeStruct((cells, channels), F32),
        scratch_shapes=[
            pltpu.VMEM((9 * size, LANES), BF16),
            pltpu.VMEM((9 * size, LANES), F32),
            pltpu.VMEM((3 * tile * parts, LANES), F32),
            pltpu.SemaphoreType.DMA((11,)),
        ],
        compiler_params=params(),
        cost_estimate=cost(2 * cells * width * 3 * width, 12 * 2**20),
    )(index, *blocks, embedded, fields, target_weight, hidden_weight, output_weight)


def east(values):
    count = lax.axis_size("lon")
    return lax.ppermute(values, "lon", [(i, (i + 1) % count) for i in range(count)])


def west(values):
    count = lax.axis_size("lon")
    return lax.ppermute(values, "lon", [((i + 1) % count, i) for i in range(count)])


def near(values):
    count = lax.axis_size("lat")
    return lax.ppermute(values, "lat", [(i, i ^ 1) for i in range(count)])


def far(values):
    count = lax.axis_size("lat")
    ups = [(i, i + 1) for i in range(1, count - 1, 2)]
    return lax.ppermute(values, "lat", ups + [(b, a) for a, b in ups])


def swap_strips(strip):
    w, e, o, n = east(strip), west(strip), far(strip), near(strip)
    sides = jnp.stack([w, e])
    return w, e, o, n, far(sides), near(sides)


def swap_blocks(block):
    half = block.shape[0] // 2
    w, e, o, n = east(block), west(block), far(block), near(block)
    corners = far(jnp.stack([w[:half], e[:half]]))
    ow, oe = east(o[half:]), west(o[half:])
    return block, w, e, o, n, corners, ow, oe, near(w), near(e)


def slots(block):
    a, b = block // 3, block % 3
    parity = lax.axis_index("lat") % 2
    same = jnp.where(b == 1, 0, jnp.where(b == 0, 1, 2))
    away = jnp.where(b == 1, 3, jnp.where(b == 0, 5, 6))
    close = jnp.where(b == 1, 4, jnp.where(b == 0, 7, 8))
    is_near = (a == 0) == (parity == 1)
    return jnp.where(a == 1, same, jnp.where(is_near, close, away))


def grid_index(senders, cells, strip, parts):
    block, offset = senders // cells, senders % cells
    outside = cells + (slots(block) - 1) * strip + offset % strip
    return jnp.where(block == 4, offset, outside) * parts


def mesh_index(senders, nodes, parts):
    return (slots(senders // nodes) * nodes + senders % nodes) * parts


def split_geometry(geometry, weight):
    def pieces(values):
        high = values.astype(BF16)
        return high, (values - high.astype(F32)).astype(BF16)

    high, low = pieces(geometry)
    weight_high, weight_low = pieces(weight)
    return (
        jnp.concatenate([high, low, high, jnp.zeros_like(high)], axis=0),
        jnp.concatenate(
            [weight_high, weight_high, weight_low, jnp.zeros_like(weight_high)], axis=0
        ),
    )


def valid_receivers(receivers, valid):
    keep = jnp.arange(receivers.shape[0], dtype=jnp.int32) < valid
    return jnp.where(keep, receivers, -1)[None]


def shards(
    grid_fields,
    mesh_static,
    encode_senders,
    encode_receivers,
    encode_geometry,
    encode_valid,
    mesh_senders,
    mesh_receivers,
    mesh_geometry,
    mesh_valid,
    decode_senders,
    embed_weight,
    encode_source,
    encode_edge,
    encode_second,
    node_first,
    node_second,
    node_gain,
    process_source,
    process_target,
    process_edge,
    process_second,
    update_message,
    update_state,
    update_out,
    process_gain,
    decode_source,
    decode_target,
    decode_hidden,
    output_weight,
):
    fields = grid_fields[0, 0]
    static = mesh_static[0, 0]
    cells, nodes, width = fields.shape[0], static.shape[0], static.shape[1]
    parts = width // LANES
    strip = cells // 8
    strips = swap_strips(fields[:strip])
    encode_index = grid_index(encode_senders[0, 0], cells, strip, parts)
    process_index = mesh_index(mesh_senders[0, 0], nodes, parts)
    decode_index = mesh_index(decode_senders[0, 0], nodes, parts)
    decode_index = decode_index.reshape(3, cells // DECODE_TILE, DECODE_TILE)
    decode_index = decode_index.transpose(1, 0, 2).reshape(-1)
    encode_to = valid_receivers(encode_receivers[0, 0], encode_valid[0, 0])
    process_to = valid_receivers(mesh_receivers[0, 0], mesh_valid[0, 0])
    encode_geo, encode_geo_weight = split_geometry(encode_geometry[0, 0], encode_edge)
    process_geo, process_geo_weight = split_geometry(mesh_geometry[0, 0], process_edge)

    embedded, own_table = embed_own(fields, embed_weight, encode_source)
    start, table = encode(
        encode_index,
        strips,
        own_table,
        encode_to,
        encode_geo,
        encode_geo_weight,
        (
            embed_weight,
            encode_source,
            encode_second,
            node_first,
            node_second,
            node_gain[None],
            process_source,
        ),
        static,
    )
    blocks = swap_blocks(table)
    shift, state = receive(
        start, process_target, update_state, process_to, process_geo, process_geo_weight
    )
    table = process(
        process_index,
        blocks,
        process_to,
        shift,
        state,
        start,
        (process_second, update_message, update_out, process_gain[None], decode_source),
    )
    blocks = swap_blocks(table)
    prediction = decode(
        decode_index, blocks, embedded, fields, decode_target, decode_hidden, output_weight
    )
    return prediction[None, None]


def solution(mesh):
    devices = P("lat", "lon")
    in_specs = (devices,) * 11 + (P(),) * 19
    return jax.shard_map(
        shards, mesh=mesh, in_specs=in_specs, out_specs=devices, check_vma=False
    )
```

time: 380 us -> 147 us (0.39); the launches traced: 373 us -> 145 us
  waiting for transfers between devices: 145 us -> 20.7 us
  matrix products: 82.2 us -> 0 us
  local copies, waits for them, and re-layouts: 93.4 us -> 12.1 us
  Pallas kernels: 0 us -> 65.4 us
  other arithmetic: 21.6 us -> 5.06 us
  starting transfers between devices: 28.1 us -> 40.2 us
    ppermute x12 -> x24, waiting for transfers between devices: 145 us -> 20.7 us  [the longest x5 12.9 us: west(): lax.ppermute(values, 'lon', [((i + 1) % count, i) for i in range(count)])]
    gather x4 -> x0, local copies, waits for them, and re-layouts: 88.6 us -> none  [the longest x1 28.7 us: shards(): jnp.take(cycle_out, decode_senders[0, 0], axis=0).astype(jnp.float32)]
    dot_general x14 -> x0, matrix products: 82.2 us -> none  [the longest x3 28.8 us: project(): jnp.dot(values, weight, preferred_element_type=jnp.float32)]
    pallas_call x0 -> x5, Pallas kernels: none -> 65.4 us  [the longest x1 19.9 us: decode(): pl.pallas_call(decode_kernel, grid=(cells // tile,), in_specs=[SMEM] + [A...]
    ppermute x12 -> x24, starting transfers between devices: 28.1 us -> 40.2 us  [the longest x6 21.5 us: far(): return lax.ppermute(values, 'lat', ups + [(b, a) for a, b in ups])]
    concatenate x6 -> x3, other arithmetic: 13.2 us -> 2.12 us  [the longest x2 1.44 us: split_geometry(): jnp.concatenate([high, low, high, jnp.zeros_like(high)], axis=0)]
    reduce_sum x3 -> x0, other arithmetic: 7.73 us -> none  [the longest x1 7.22 us: shards(): jnp.sum(decode_edge.astype(jnp.float32), axis=0).astype(jnp.bfloat16)]
    unnamed x58 -> x64, local copies, waits for them, and re-layouts: 0.14 us -> 5.27 us
  transfers between devices with their start and end apart: 12 -> 24, of which waited for: 8 -> 5; matrix products, arithmetic and copies ran while one was open for 8% -> 5% of each run, Pallas kernels for 0% -> 10%
where the time goes in v1:
time: 147 us; the launch traced here: 145 us
  Pallas kernels  65.4 us (44%)
  starting transfers between devices  40.2 us (27%)
  waiting for transfers between devices  20.7 us (14%)
  local copies, waits for them, and re-layouts  12.1 us (8%)
  other arithmetic  5.06 us (3%)
  between operations  1.85 us (1%)
    ppermute x6, starting transfers between devices, far(): return lax.ppermute(values, 'lat', ups + [(b, a) for a, b in ups])  21.5 us
    pallas_call x1, Pallas kernels, decode(): pl.pallas_call(decode_kernel, grid=(cells // tile,), in_specs=[SMEM] + [A...  19.9 us
    pallas_call x1, Pallas kernels, process(): pl.pallas_call(process_kernel, in_specs=[SMEM] + [ANY] * 10 + [VMEM] * 9,...  16.4 us
    pallas_call x1, Pallas kernels, encode(): pl.pallas_call(encode_kernel, in_specs=[SMEM] + [VMEM] * 6 + [ANY] + [VME...  15 us
    ppermute x5, waiting for transfers between devices, west(): lax.ppermute(values, 'lon', [((i + 1) % count, i) for i in range(count)])  12.9 us
    pallas_call x1, Pallas kernels, receive(): pl.pallas_call(receive_kernel, grid=(edges // tile,), in_specs=[pl.BlockS...  8.53 us
    ppermute x5, starting transfers between devices, west(): lax.ppermute(values, 'lon', [((i + 1) % count, i) for i in range(count)])  8.22 us
    ppermute x5, waiting for transfers between devices, east(): lax.ppermute(values, 'lon', [(i, (i + 1) % count) for i in range(count)])  7.77 us
  transfers between devices with their start and end apart: 24, of which 5 were waited for; matrix products, arithmetic and copies ran while one was open for 5% of the time, Pallas kernels for 10%

profile of v1, /device:TPU:3, one launch (start us, length us, event | category | flops | bytes accessed | tf_op | source)
XLA Modules:
  0.0 145.3 jit_solution(10812956923607271417)
XLA Ops:
  0.0 1.5 %copy.39 = bf16[1,1,2048,227]{3,2,1,0:T(8,128)(2,1)S(1)} copy(bf16[1,1,2048,227]{2,3,1,0:T(8,128)(2,1)} %param.30) | data formatting | bytes 1859584 | tf_op args[0]
  1.6 1.4 collective-permute-start
  3.0 1.5 %collective-permute-start.1 = (bf16[256,227]{1,0:T(8,128)(2,1)S(1)}, bf16[256,227]{1,0:T(8,128)(2,1)S(1)}, u32[]{:S(2)}, u32[]{:S(2)}) collective-permute-start(bf16[256,227]{1,0:T(8,128)(2,1)S(1)} %slice_bitcast_fusion.4), channel_id=1, source_target_pairs={{1,0},{2,1},{3,2},{0,3},{5,4},{6,5},{7,6},{4,7},{9,8},{10,9},{11,1... | collective-permute-start | bytes 348680 | tf_op jit(solution)/shard_map/ppermute | solution.py:371
  4.5 4.5 %collective-permute-start.2 = (bf16[256,227]{1,0:T(8,128)(2,1)S(1)}, bf16[256,227]{1,0:T(8,128)(2,1)S(1)}, u32[]{:S(2)}, u32[]{:S(2)}) collective-permute-start(bf16[256,227]{1,0:T(8,128)(2,1)S(1)} %slice_bitcast_fusion.4), channel_id=1, source_target_pairs={{4,8},{12,16},{20,24},{28,32},{36,40},{44,48},{52,56},{60,64},{68,... | collective-permute-start | bytes 348680 | tf_op jit(solution)/shard_map/ppermute | solution.py:382
  9.0 1.6 %collective-permute-start.3 = (bf16[256,227]{1,0:T(8,128)(2,1)S(1)}, bf16[256,227]{1,0:T(8,128)(2,1)S(1)}, u32[]{:S(2)}, u32[]{:S(2)}) collective-permute-start(bf16[256,227]{1,0:T(8,128)(2,1)S(1)} %slice_bitcast_fusion.4), channel_id=1, source_target_pairs={{0,4},{4,0},{8,12},{12,8},{16,20},{20,16},{24,28},{28,24},{32,36},... | collective-permute-start | bytes 348680 | tf_op jit(solution)/shard_map/ppermute | solution.py:376
  12.1 0.7 maximum_maximum_fusion.1.geometry
  12.8 0.7 maximum_maximum_fusion.geometry
  13.5 0.7 maximum_maximum_fusion.3
  14.3 2.4 %collective-permute-start.4 = (bf16[2,256,227]{2,1,0:T(8,128)(2,1)S(1)}, bf16[2,256,227]{2,1,0:T(8,128)(2,1)S(1)}, u32[]{:S(2)}, u32[]{:S(2)}) collective-permute-start(bf16[2,256,227]{2,1,0:T(8,128)(2,1)S(1)} %pad_maximum_fusion.2), channel_id=1, source_target_pairs={{4,8},{12,16},{20,24},{28,32},{36,40},{44,48},{52,56},{60,64},{68,... | collective-permute-start | bytes 697352 | tf_op jit(solution)/shard_map/ppermute | solution.py:382
  18.7 5.6 %shard_map.280 = (bf16[2048,512]{1,0:T(8,128)(2,1)}, f32[8192,128]{1,0:T(8,128)}) custom-call(bf16[2048,227]{1,0:T(8,128)(2,1)} %bitcast.43, bf16[227,512]{1,0:T(8,128)(2,1)} %embed_weight.3, bf16[512,512]{1,0:T(8,128)(2,1)} %source_weight.3), custom_call_target="tpu_custom_call" | custom-call | flops 1610612736 | bytes 8388608 | tf_op jit(solution)/shard_map/pallas_call | solution.py:85
  25.2 15.0 %shard_map.281 = (bf16[512,512]{1,0:T(8,128)(2,1)}, bf16[2048,128]{1,0:T(8,128)(2,1)}) custom-call(s32[3072]{0:T(1024)} %fusion.14.index, bf16[256,227]{1,0:T(8,128)(2,1)} %copy-done.8, bf16[256,227]{1,0:T(8,128)(2,1)} %copy-done.9, bf16[256,227]{1,0:T(8,128)(2,1)} %copy-done.29, bf16[256,227]{1,0:T(8,128)(2,1)} %copy-done.30, ...), custom_call_target="tpu_custom_call" | custom-call | flops 3221225472 | bytes 10485760 | tf_op jit(solution)/shard_map/pallas_call | solution.py:157
  40.2 1.6 %collective-permute-start.7 = (bf16[2048,128]{1,0:T(8,128)(2,1)}, bf16[2048,128]{1,0:T(8,128)(2,1)S(1)}, u32[]{:S(2)}, u32[]{:S(2)}) collective-permute-start(bf16[2048,128]{1,0:T(8,128)(2,1)} %get-tuple-element.12.own), channel_id=1, source_target_pairs={{1,0},{2,1},{3,2},{0,3},{5,4},{6,5},{7,6},{4,7},{9,8},{10,9},{11,1... | collective-permute-start | bytes 1572872 | tf_op jit(solution)/shard_map/ppermute | solution.py:371
  42.4 3.5 %collective-permute-start.8 = (bf16[2048,128]{1,0:T(8,128)(2,1)}, bf16[2048,128]{1,0:T(8,128)(2,1)S(1)}, u32[]{:S(2)}, u32[]{:S(2)}) collective-permute-start(bf16[2048,128]{1,0:T(8,128)(2,1)} %get-tuple-element.12.own), channel_id=1, source_target_pairs={{4,8},{12,16},{20,24},{28,32},{36,40},{44,48},{52,56},{60,64},{68,... | collective-permute-start | bytes 1572872 | tf_op jit(solution)/shard_map/ppermute | solution.py:382
  45.9 1.2 collective-permute-start.9
  47.1 6.8 %collective-permute-done.7.e = bf16[2048,128]{1,0:T(8,128)(2,1)S(1)} collective-permute-done((bf16[2048,128]{1,0:T(8,128)(2,1)}, bf16[2048,128]{1,0:T(8,128)(2,1)S(1)}, u32[]{:S(2)}, u32[]{:S(2)}) %collective-permute-start.7) | collective-permute-done | bytes 524320 | tf_op jit(solution)/shard_map/ppermute | solution.py:371
  54.0 2.4 %collective-permute-done.6.w = bf16[2048,128]{1,0:T(8,128)(2,1)S(1)} collective-permute-done((bf16[2048,128]{1,0:T(8,128)(2,1)}, bf16[2048,128]{1,0:T(8,128)(2,1)S(1)}, u32[]{:S(2)}, u32[]{:S(2)}) %collective-permute-start.6) | collective-permute-done | bytes 524320 | tf_op jit(solution)/shard_map/ppermute | solution.py:366
  56.5 3.7 %collective-permute-start.10 = (bf16[2,1024,128]{2,1,0:T(8,128)(2,1)S(1)}, bf16[2,1024,128]{2,1,0:T(8,128)(2,1)S(1)}, u32[]{:S(2)}, u32[]{:S(2)}) collective-permute-start(bf16[2,1024,128]{2,1,0:T(8,128)(2,1)S(1)} %pad_maximum_fusion), channel_id=1, source_target_pairs={{4,8},{12,16},{20,24},{28,32},{36,40},{44,48},{52,56},{60,64},{68,... | collective-permute-start | bytes 1572872 | tf_op jit(solution)/shard_map/ppermute | solution.py:382
  61.6 2.6 %collective-permute-start.12 = (bf16[1024,128]{1,0:T(8,128)(2,1)S(1)}, bf16[1024,128]{1,0:T(8,128)(2,1)S(1)}, u32[]{:S(2)}, u32[]{:S(2)}) collective-permute-start(bf16[1024,128]{1,0:T(8,128)(2,1)S(1)} %slice.37), channel_id=1, source_target_pairs={{1,0},{2,1},{3,2},{0,3},{5,4},{6,5},{7,6},{4,7},{9,8},{10,9},{11,1... | collective-permute-start | bytes 786440 | tf_op jit(solution)/shard_map/ppermute | solution.py:371
  64.2 8.5 %shard_map.282 = (bf16[4096,512]{1,0:T(8,128)(2,1)}, f32[512,512]{1,0:T(8,128)}) custom-call(bf16[512,512]{1,0:T(8,128)(2,1)} %get-tuple-element.13.start, bf16[512,512]{1,0:T(8,128)(2,1)} %target_weight.2, bf16[512,512]{1,0:T(8,128)(2,1)} %state_weight.1, s32[1,4096]{1,0:T(1,128)} %compare_select_fusion.receivers, ...), custom_call_target="tpu_custom_call" | custom-call | flops 4294967296 | bytes 8388608 | tf_op jit(solution)/shard_map/pallas_call | solution.py:199
  74.2 16.4 %shard_map.283.own = bf16[2048,128]{1,0:T(8,128)(2,1)} custom-call(s32[4096]{0:T(1024)} %fusion.8.index, bf16[2048,128]{1,0:T(8,128)(2,1)} %get-tuple-element.12.own, bf16[2048,128]{1,0:T(8,128)(2,1)} %copy-done.4, bf16[2048,128]{1,0:T(8,128)(2,1)} %copy-done.2, bf16[2048,128]{1,0:T(8,128)(2,1)} %copy-done.6, bf16[2048,128]{1,0:T(8,128)(2,1)} %copy-done.19, ...), custom_call_target="tpu_custom_call" | custom-call | flops 4294967296 | bytes 12582912 | tf_op jit(solution)/shard_map/pallas_call | solution.py:284
  90.9 1.3 collective-permute-start.15
  92.2 3.1 %collective-permute-start.17 = (bf16[2048,128]{1,0:T(8,128)(2,1)}, bf16[2048,128]{1,0:T(8,128)(2,1)S(1)}, u32[]{:S(2)}, u32[]{:S(2)}) collective-permute-start(bf16[2048,128]{1,0:T(8,128)(2,1)} %shard_map.283.own), channel_id=1, source_target_pairs={{4,8},{12,16},{20,24},{28,32},{36,40},{44,48},{52,56},{60,64},{68,... | collective-permute-start | bytes 1572872 | tf_op jit(solution)/shard_map/ppermute | solution.py:382
  95.3 2.1 %collective-permute-start.18 = (bf16[2048,128]{1,0:T(8,128)(2,1)}, bf16[2048,128]{1,0:T(8,128)(2,1)S(1)}, u32[]{:S(2)}, u32[]{:S(2)}) collective-permute-start(bf16[2048,128]{1,0:T(8,128)(2,1)} %shard_map.283.own), channel_id=1, source_target_pairs={{0,4},{4,0},{8,12},{12,8},{16,20},{20,16},{24,28},{28,24},{32,36},... | collective-permute-start | bytes 1572872 | tf_op jit(solution)/shard_map/ppermute | solution.py:376
  97.3 6.1 %collective-permute-done.16.e = bf16[2048,128]{1,0:T(8,128)(2,1)S(1)} collective-permute-done((bf16[2048,128]{1,0:T(8,128)(2,1)}, bf16[2048,128]{1,0:T(8,128)(2,1)S(1)}, u32[]{:S(2)}, u32[]{:S(2)}) %collective-permute-start.16) | collective-permute-done | bytes 524320 | tf_op jit(solution)/shard_map/ppermute | solution.py:371
  103.4 0.9 collective-permute-done.15.w
  104.5 4.2 %collective-permute-start.19 = (bf16[2,1024,128]{2,1,0:T(8,128)(2,1)S(1)}, bf16[2,1024,128]{2,1,0:T(8,128)(2,1)}, u32[]{:S(2)}, u32[]{:S(2)}) collective-permute-start(bf16[2,1024,128]{2,1,0:T(8,128)(2,1)S(1)} %pad_maximum_fusion.1), channel_id=1, source_target_pairs={{4,8},{12,16},{20,24},{28,32},{36,40},{44,48},{52,56},{60,64},{68,... | collective-permute-start | bytes 1572872 | tf_op jit(solution)/shard_map/ppermute | solution.py:382
  108.7 1.0 collective-permute-start.22
  110.4 2.2 %collective-permute-start.21 = (bf16[1024,128]{1,0:T(8,128)(2,1)S(1)}, bf16[1024,128]{1,0:T(8,128)(2,1)}, u32[]{:S(2)}, u32[]{:S(2)}) collective-permute-start(bf16[1024,128]{1,0:T(8,128)(2,1)S(1)} %slice.40), channel_id=1, source_target_pairs={{1,0},{2,1},{3,2},{0,3},{5,4},{6,5},{7,6},{4,7},{9,8},{10,9},{11,1... | collective-permute-start | bytes 786440 | tf_op jit(solution)/shard_map/ppermute | solution.py:371
  113.4 0.8 copy.41.output_weight
  114.2 4.4 %collective-permute-done.20.ow = bf16[1024,128]{1,0:T(8,128)(2,1)S(1)} collective-permute-done((bf16[1024,128]{1,0:T(8,128)(2,1)S(1)}, bf16[1024,128]{1,0:T(8,128)(2,1)S(1)}, u32[]{:S(2)}, u32[]{:S(2)}) %collective-permute-start.20) | collective-permute-done | bytes 262176 | tf_op jit(solution)/shard_map/ppermute | solution.py:366
  119.4 19.9 %shard_map.284 = f32[2048,227]{1,0:T(8,128)} custom-call(s32[6144]{0:T(1024)} %reshape.40.index, bf16[2048,128]{1,0:T(8,128)(2,1)} %shard_map.283.own, bf16[2048,128]{1,0:T(8,128)(2,1)} %copy-done.5, bf16[2048,128]{1,0:T(8,128)(2,1)} %copy-done.3, bf16[2048,128]{1,0:T(8,128)(2,1)} %copy-done.7, bf16[2048,128]{1,0:T(8,128)(2,1)} %copy-done.20, ...), custom_call_target="tpu_custom_call" | custom-call | flops 3221225472 | bytes 12582912 | tf_op jit(solution)/shard_map/pallas_call | solution.py:339
  139.3 6.0 %copy.42 = f32[1,1,2048,227]{2,1,3,0:T(1,128)} copy(f32[1,1,2048,227]{3,2,1,0:T(8,128)} %bitcast.42) | data formatting | bytes 3719168 | tf_op jit(solution)/shard_map/broadcast_in_dim | solution.py:523
  (111 shorter events, 9.0 us)
Async XLA Ops:
  0.0 17.3 %copy-start.16 = (s32[1,1,3072]{2,1,0:T(1,128)S(1)}, s32[1,1,3072]{2,1,0:T(1,128)}, u32[]{:S(2)}) copy-start(s32[1,1,3072]{2,1,0:T(1,128)} %param.32) | copy-start | bytes 36868
  1.6 17.1 %copy-start = (bf16[1,1,2048,227]{3,2,1,0:T(8,128)(2,1)}, bf16[1,1,2048,227]{3,2,1,0:T(8,128)(2,1)S(1)}, u32[]{:S(2)}) copy-start(bf16[1,1,2048,227]{3,2,1,0:T(8,128)(2,1)S(1)} %copy.39) | copy-start | bytes 2789380
  1.6 12.6 %collective-permute-start = (bf16[256,227]{1,0:T(8,128)(2,1)S(1)}, bf16[256,227]{1,0:T(8,128)(2,1)S(1)}, u32[]{:S(2)}, u32[]{:S(2)}) collective-permute-start(bf16[256,227]{1,0:T(8,128)(2,1)S(1)} %slice_bitcast_fusion.4), channel_id=1, source_target_pairs={{0,1},{1,2},{2,3},{3,0},{4,5},{5,6},{6,7},{7,4},{8,9},{9,10},{10,1... | collective-permute-start | bytes 348680 | tf_op jit(solution)/shard_map/ppermute | solution.py:366
  3.0 11.2 %collective-permute-start.1 = (bf16[256,227]{1,0:T(8,128)(2,1)S(1)}, bf16[256,227]{1,0:T(8,128)(2,1)S(1)}, u32[]{:S(2)}, u32[]{:S(2)}) collective-permute-start(bf16[256,227]{1,0:T(8,128)(2,1)S(1)} %slice_bitcast_fusion.4), channel_id=1, source_target_pairs={{1,0},{2,1},{3,2},{0,3},{5,4},{6,5},{7,6},{4,7},{9,8},{10,9},{11,1... | collective-permute-start | bytes 348680 | tf_op jit(solution)/shard_map/ppermute | solution.py:371
  4.5 19.8 %collective-permute-start.2 = (bf16[256,227]{1,0:T(8,128)(2,1)S(1)}, bf16[256,227]{1,0:T(8,128)(2,1)S(1)}, u32[]{:S(2)}, u32[]{:S(2)}) collective-permute-start(bf16[256,227]{1,0:T(8,128)(2,1)S(1)} %slice_bitcast_fusion.4), channel_id=1, source_target_pairs={{4,8},{12,16},{20,24},{28,32},{36,40},{44,48},{52,56},{60,64},{68,... | collective-permute-start | bytes 348680 | tf_op jit(solution)/shard_map/ppermute | solution.py:382
  9.0 15.3 %collective-permute-start.3 = (bf16[256,227]{1,0:T(8,128)(2,1)S(1)}, bf16[256,227]{1,0:T(8,128)(2,1)S(1)}, u32[]{:S(2)}, u32[]{:S(2)}) collective-permute-start(bf16[256,227]{1,0:T(8,128)(2,1)S(1)} %slice_bitcast_fusion.4), channel_id=1, source_target_pairs={{0,4},{4,0},{8,12},{12,8},{16,20},{20,16},{24,28},{28,24},{32,36},... | collective-permute-start | bytes 348680 | tf_op jit(solution)/shard_map/ppermute | solution.py:376
  14.3 10.1 %collective-permute-start.4 = (bf16[2,256,227]{2,1,0:T(8,128)(2,1)S(1)}, bf16[2,256,227]{2,1,0:T(8,128)(2,1)S(1)}, u32[]{:S(2)}, u32[]{:S(2)}) collective-permute-start(bf16[2,256,227]{2,1,0:T(8,128)(2,1)S(1)} %pad_maximum_fusion.2), channel_id=1, source_target_pairs={{4,8},{12,16},{20,24},{28,32},{36,40},{44,48},{52,56},{60,64},{68,... | collective-permute-start | bytes 697352 | tf_op jit(solution)/shard_map/ppermute | solution.py:382
  16.7 7.6 %collective-permute-start.5 = (bf16[2,256,227]{2,1,0:T(8,128)(2,1)S(1)}, bf16[2,256,227]{2,1,0:T(8,128)(2,1)S(1)}, u32[]{:S(2)}, u32[]{:S(2)}) collective-permute-start(bf16[2,256,227]{2,1,0:T(8,128)(2,1)S(1)} %pad_maximum_fusion.2), channel_id=1, source_target_pairs={{0,4},{4,0},{8,12},{12,8},{16,20},{20,16},{24,28},{28,24},{32,36},... | collective-permute-start | bytes 697352 | tf_op jit(solution)/shard_map/ppermute | solution.py:376
  25.2 16.6 %copy-start.13 = (s32[1,1,4096]{2,1,0:T(1,128)S(1)}, s32[1,1,4096]{2,1,0:T(1,128)}, u32[]{:S(2)}) copy-start(s32[1,1,4096]{2,1,0:T(1,128)} %param.37) | copy-start | bytes 49156
  40.1 20.6 %copy-start.14 = (s32[1,1,4096]{2,1,0:T(1,128)S(1)}, s32[1,1,4096]{2,1,0:T(1,128)}, u32[]{:S(2)}) copy-start(s32[1,1,4096]{2,1,0:T(1,128)} %param.36) | copy-start | bytes 49156
  40.2 13.8 %collective-permute-start.7 = (bf16[2048,128]{1,0:T(8,128)(2,1)}, bf16[2048,128]{1,0:T(8,128)(2,1)S(1)}, u32[]{:S(2)}, u32[]{:S(2)}) collective-permute-start(bf16[2048,128]{1,0:T(8,128)(2,1)} %get-tuple-element.12.own), channel_id=1, source_target_pairs={{1,0},{2,1},{3,2},{0,3},{5,4},{6,5},{7,6},{4,7},{9,8},{10,9},{11,1... | collective-permute-start | bytes 1572872 | tf_op jit(solution)/shard_map/ppermute | solution.py:371
  41.8 14.6 %collective-permute-start.6 = (bf16[2048,128]{1,0:T(8,128)(2,1)}, bf16[2048,128]{1,0:T(8,128)(2,1)S(1)}, u32[]{:S(2)}, u32[]{:S(2)}) collective-permute-start(bf16[2048,128]{1,0:T(8,128)(2,1)} %get-tuple-element.12.own), channel_id=1, source_target_pairs={{0,1},{1,2},{2,3},{3,0},{4,5},{5,6},{6,7},{7,4},{8,9},{9,10},{10,1... | collective-permute-start | bytes 1572872 | tf_op jit(solution)/shard_map/ppermute | solution.py:366
  42.4 19.0 %collective-permute-start.8 = (bf16[2048,128]{1,0:T(8,128)(2,1)}, bf16[2048,128]{1,0:T(8,128)(2,1)S(1)}, u32[]{:S(2)}, u32[]{:S(2)}) collective-permute-start(bf16[2048,128]{1,0:T(8,128)(2,1)} %get-tuple-element.12.own), channel_id=1, source_target_pairs={{4,8},{12,16},{20,24},{28,32},{36,40},{44,48},{52,56},{60,64},{68,... | collective-permute-start | bytes 1572872 | tf_op jit(solution)/shard_map/ppermute | solution.py:382
  45.9 15.6 %collective-permute-start.9 = (bf16[2048,128]{1,0:T(8,128)(2,1)}, bf16[2048,128]{1,0:T(8,128)(2,1)S(1)}, u32[]{:S(2)}, u32[]{:S(2)}) collective-permute-start(bf16[2048,128]{1,0:T(8,128)(2,1)} %get-tuple-element.12.own), channel_id=1, source_target_pairs={{0,4},{4,0},{8,12},{12,8},{16,20},{20,16},{24,28},{28,24},{32,36},... | collective-permute-start | bytes 1572872 | tf_op jit(solution)/shard_map/ppermute | solution.py:376
  53.9 18.8 %copy-start.2 = (bf16[2048,128]{1,0:T(8,128)(2,1)}, bf16[2048,128]{1,0:T(8,128)(2,1)S(1)}, u32[]{:S(2)}) copy-start(bf16[2048,128]{1,0:T(8,128)(2,1)S(1)} %collective-permute-done.7.e) | copy-start | bytes 1572868
  56.4 16.3 %copy-start.4 = (bf16[2048,128]{1,0:T(8,128)(2,1)}, bf16[2048,128]{1,0:T(8,128)(2,1)S(1)}, u32[]{:S(2)}) copy-start(bf16[2048,128]{1,0:T(8,128)(2,1)S(1)} %collective-permute-done.6.w) | copy-start | bytes 1572868
  56.5 16.3 %collective-permute-start.10 = (bf16[2,1024,128]{2,1,0:T(8,128)(2,1)S(1)}, bf16[2,1024,128]{2,1,0:T(8,128)(2,1)S(1)}, u32[]{:S(2)}, u32[]{:S(2)}) collective-permute-start(bf16[2,1024,128]{2,1,0:T(8,128)(2,1)S(1)} %pad_maximum_fusion), channel_id=1, source_target_pairs={{4,8},{12,16},{20,24},{28,32},{36,40},{44,48},{52,56},{60,64},{68,... | collective-permute-start | bytes 1572872 | tf_op jit(solution)/shard_map/ppermute | solution.py:382
  60.2 12.6 %collective-permute-start.13 = (bf16[2048,128]{1,0:T(8,128)(2,1)S(1)}, bf16[2048,128]{1,0:T(8,128)(2,1)S(1)}, u32[]{:S(2)}, u32[]{:S(2)}) collective-permute-start(bf16[2048,128]{1,0:T(8,128)(2,1)S(1)} %collective-permute-done.6.w), channel_id=1, source_target_pairs={{0,4},{4,0},{8,12},{12,8},{16,20},{20,16},{24,28},{28,24},{32,36},... | collective-permute-start | bytes 1572872 | tf_op jit(solution)/shard_map/ppermute | solution.py:376
  60.6 12.2 %collective-permute-start.14 = (bf16[2048,128]{1,0:T(8,128)(2,1)S(1)}, bf16[2048,128]{1,0:T(8,128)(2,1)S(1)}, u32[]{:S(2)}, u32[]{:S(2)}) collective-permute-start(bf16[2048,128]{1,0:T(8,128)(2,1)S(1)} %collective-permute-done.7.e), channel_id=1, source_target_pairs={{0,4},{4,0},{8,12},{12,8},{16,20},{20,16},{24,28},{28,24},{32,36},... | collective-permute-start | bytes 1572872 | tf_op jit(solution)/shard_map/ppermute | solution.py:376
  61.5 11.3 %collective-permute-start.11 = (bf16[1024,128]{1,0:T(8,128)(2,1)S(1)}, bf16[1024,128]{1,0:T(8,128)(2,1)S(1)}, u32[]{:S(2)}, u32[]{:S(2)}) collective-permute-start(bf16[1024,128]{1,0:T(8,128)(2,1)S(1)} %slice.37), channel_id=1, source_target_pairs={{0,1},{1,2},{2,3},{3,0},{4,5},{5,6},{6,7},{7,4},{8,9},{9,10},{10,1... | collective-permute-start | bytes 786440 | tf_op jit(solution)/shard_map/ppermute | solution.py:366
  61.6 11.2 %collective-permute-start.12 = (bf16[1024,128]{1,0:T(8,128)(2,1)S(1)}, bf16[1024,128]{1,0:T(8,128)(2,1)S(1)}, u32[]{:S(2)}, u32[]{:S(2)}) collective-permute-start(bf16[1024,128]{1,0:T(8,128)(2,1)S(1)} %slice.37), channel_id=1, source_target_pairs={{1,0},{2,1},{3,2},{0,3},{5,4},{6,5},{7,6},{4,7},{9,8},{10,9},{11,1... | collective-permute-start | bytes 786440 | tf_op jit(solution)/shard_map/ppermute | solution.py:371
  90.6 22.0 %copy-start.12 = (s32[1,1,3,2048]{3,1,2,0:T(1,128)S(1)}, s32[1,1,3,2048]{3,1,2,0:T(1,128)}, u32[]{:S(2)}) copy-start(s32[1,1,3,2048]{3,1,2,0:T(1,128)} %param.40) | copy-start | bytes 73732
  90.6 22.8 %copy-start.1 = (bf16[512,227]{0,1:T(8,128)(2,1)S(1)}, bf16[512,227]{0,1:T(8,128)(2,1)}, u32[]{:S(2)}) copy-start(bf16[512,227]{0,1:T(8,128)(2,1)} %param.59) | copy-start | bytes 697348
  90.6 12.8 %collective-permute-start.16 = (bf16[2048,128]{1,0:T(8,128)(2,1)}, bf16[2048,128]{1,0:T(8,128)(2,1)S(1)}, u32[]{:S(2)}, u32[]{:S(2)}) collective-permute-start(bf16[2048,128]{1,0:T(8,128)(2,1)} %shard_map.283.own), channel_id=1, source_target_pairs={{1,0},{2,1},{3,2},{0,3},{5,4},{6,5},{7,6},{4,7},{9,8},{10,9},{11,1... | collective-permute-start | bytes 1572872 | tf_op jit(solution)/shard_map/ppermute | solution.py:371
  90.9 13.5 %collective-permute-start.15 = (bf16[2048,128]{1,0:T(8,128)(2,1)}, bf16[2048,128]{1,0:T(8,128)(2,1)S(1)}, u32[]{:S(2)}, u32[]{:S(2)}) collective-permute-start(bf16[2048,128]{1,0:T(8,128)(2,1)} %shard_map.283.own), channel_id=1, source_target_pairs={{0,1},{1,2},{2,3},{3,0},{4,5},{5,6},{6,7},{7,4},{8,9},{9,10},{10,1... | collective-permute-start | bytes 1572872 | tf_op jit(solution)/shard_map/ppermute | solution.py:366
  92.2 17.6 %collective-permute-start.17 = (bf16[2048,128]{1,0:T(8,128)(2,1)}, bf16[2048,128]{1,0:T(8,128)(2,1)S(1)}, u32[]{:S(2)}, u32[]{:S(2)}) collective-permute-start(bf16[2048,128]{1,0:T(8,128)(2,1)} %shard_map.283.own), channel_id=1, source_target_pairs={{4,8},{12,16},{20,24},{28,32},{36,40},{44,48},{52,56},{60,64},{68,... | collective-permute-start | bytes 1572872 | tf_op jit(solution)/shard_map/ppermute | solution.py:382
  95.3 15.1 %collective-permute-start.18 = (bf16[2048,128]{1,0:T(8,128)(2,1)}, bf16[2048,128]{1,0:T(8,128)(2,1)S(1)}, u32[]{:S(2)}, u32[]{:S(2)}) collective-permute-start(bf16[2048,128]{1,0:T(8,128)(2,1)} %shard_map.283.own), channel_id=1, source_target_pairs={{0,4},{4,0},{8,12},{12,8},{16,20},{20,16},{24,28},{28,24},{32,36},... | collective-permute-start | bytes 1572872 | tf_op jit(solution)/shard_map/ppermute | solution.py:376
  104.5 14.2 %collective-permute-start.19 = (bf16[2,1024,128]{2,1,0:T(8,128)(2,1)S(1)}, bf16[2,1024,128]{2,1,0:T(8,128)(2,1)}, u32[]{:S(2)}, u32[]{:S(2)}) collective-permute-start(bf16[2,1024,128]{2,1,0:T(8,128)(2,1)S(1)} %pad_maximum_fusion.1), channel_id=1, source_target_pairs={{4,8},{12,16},{20,24},{28,32},{36,40},{44,48},{52,56},{60,64},{68,... | collective-permute-start | bytes 1572872 | tf_op jit(solution)/shard_map/ppermute | solution.py:382
  108.7 10.0 %collective-permute-start.22 = (bf16[2048,128]{1,0:T(8,128)(2,1)S(1)}, bf16[2048,128]{1,0:T(8,128)(2,1)}, u32[]{:S(2)}, u32[]{:S(2)}) collective-permute-start(bf16[2048,128]{1,0:T(8,128)(2,1)S(1)} %collective-permute-done.15.w), channel_id=1, source_target_pairs={{0,4},{4,0},{8,12},{12,8},{16,20},{20,16},{24,28},{28,24},{32,36},... | collective-permute-start | bytes 1572872 | tf_op jit(solution)/shard_map/ppermute | solution.py:376
  109.7 9.0 %collective-permute-start.23 = (bf16[2048,128]{1,0:T(8,128)(2,1)S(1)}, bf16[2048,128]{1,0:T(8,128)(2,1)}, u32[]{:S(2)}, u32[]{:S(2)}) collective-permute-start(bf16[2048,128]{1,0:T(8,128)(2,1)S(1)} %collective-permute-done.16.e), channel_id=1, source_target_pairs={{0,4},{4,0},{8,12},{12,8},{16,20},{20,16},{24,28},{28,24},{32,36},... | collective-permute-start | bytes 1572872 | tf_op jit(solution)/shard_map/ppermute | solution.py:376
  109.8 8.9 %collective-permute-start.20 = (bf16[1024,128]{1,0:T(8,128)(2,1)S(1)}, bf16[1024,128]{1,0:T(8,128)(2,1)S(1)}, u32[]{:S(2)}, u32[]{:S(2)}) collective-permute-start(bf16[1024,128]{1,0:T(8,128)(2,1)S(1)} %slice.40), channel_id=1, source_target_pairs={{0,1},{1,2},{2,3},{3,0},{4,5},{5,6},{6,7},{7,4},{8,9},{9,10},{10,1... | collective-permute-start | bytes 786440 | tf_op jit(solution)/shard_map/ppermute | solution.py:366
  110.4 8.3 %collective-permute-start.21 = (bf16[1024,128]{1,0:T(8,128)(2,1)S(1)}, bf16[1024,128]{1,0:T(8,128)(2,1)}, u32[]{:S(2)}, u32[]{:S(2)}) collective-permute-start(bf16[1024,128]{1,0:T(8,128)(2,1)S(1)} %slice.40), channel_id=1, source_target_pairs={{1,0},{2,1},{3,2},{0,3},{5,4},{6,5},{7,6},{4,7},{9,8},{10,9},{11,1... | collective-permute-start | bytes 786440 | tf_op jit(solution)/shard_map/ppermute | solution.py:371
  (23 other events, 154.0 us)

commit v2 on v1

v2 whole, which is shorter than its diff:
```python
import functools

import jax
import jax.numpy as jnp
from jax import lax
from jax.experimental import pallas as pl
from jax.experimental.pallas import tpu as pltpu
from jax.sharding import PartitionSpec as P

EPSILON = 1e-05
BF16 = jnp.bfloat16
F32 = jnp.float32
LANES = 128
MIB = 1024 * 1024

VMEM = pl.BlockSpec(memory_space=pltpu.VMEM)
SMEM = pl.BlockSpec(memory_space=pltpu.SMEM)
ANY = pl.BlockSpec(memory_space=pl.ANY)


def params(mib):
    return pltpu.CompilerParams(vmem_limit_bytes=mib * MIB)


def cost(flops, moved):
    return pl.CostEstimate(flops=flops, bytes_accessed=moved, transcendentals=0)


def silu(values):
    half = 0.5 * values
    return half + half * jnp.tanh(half)


def layer_norm(values, gain):
    centre = values - jnp.mean(values, axis=-1, keepdims=True)
    spread = jnp.mean(centre * centre, axis=-1, keepdims=True)
    return centre * lax.rsqrt(spread + EPSILON) * gain


def dot(a, b):
    return jnp.dot(a, b, preferred_element_type=F32)


def dot_rows(a, b):
    return lax.dot_general(a, b, (((0,), (0,)), ((), ())), preferred_element_type=F32)


def put_table(ref, first, values):
    parts = values.shape[1] // LANES
    for part in range(parts):
        ref[pl.ds(first * parts + part, values.shape[0], stride=parts), :] = values[
            :, part * LANES : (part + 1) * LANES
        ]


def gather(index, first, count, table, rows, base, parts):
    for edge in range(count):
        start = pl.multiple_of(index[first + edge], parts)
        rows[pl.ds((base + edge) * parts, parts), :] = table[pl.ds(start, parts), :]


def pipeline(tiles, fetch, work, one, two):
    fetch(0, one, 0, 1)

    def body(pair, carry):
        tile = 2 * pair
        work(tile, one, functools.partial(fetch, tile + 1, two))
        work(tile + 1, two, functools.partial(fetch, jnp.minimum(tile + 2, tiles - 1), one))
        return carry

    lax.fori_loop(0, tiles // 2, body, 0)


def onehot(receivers, begin, valid, nodes):
    shape = receivers.shape
    slot = begin + lax.broadcasted_iota(jnp.int32, shape, 1)
    target = jnp.where(slot < valid, receivers, -1)
    ids = lax.broadcasted_iota(jnp.int32, (nodes, shape[1]), 0)
    return jnp.where(ids == target, 1.0, 0.0).astype(BF16)


def pieces(geometry, order):
    high = geometry.astype(BF16).astype(F32)
    low = geometry - high
    parts = [(high, low)[i] for i in order] + [jnp.zeros_like(high)]
    return jnp.concatenate(parts, axis=0).astype(BF16)


def geometry_term(geometry, edge_weight):
    return dot_rows(pieces(geometry, (0, 1, 0)), pieces(edge_weight, (0, 0, 1)))


def copy_kernel(source, target):
    target[...] = source[...]


def take_strip(fields, strip):
    channels = fields.shape[0]
    block = pl.BlockSpec((channels, strip), lambda i: (0, 0))
    return pl.pallas_call(
        copy_kernel,
        grid=(1,),
        in_specs=[block],
        out_specs=block,
        out_shape=jax.ShapeDtypeStruct((channels, strip), fields.dtype),
        compiler_params=params(60),
        cost_estimate=cost(0, MIB),
    )(fields)


def band_kernel(left, middle, right, band):
    band[...] = jnp.concatenate([left[...], middle[...], right[...]], axis=1)


def make_band(left, middle, right):
    channels, strip = middle.shape
    return pl.pallas_call(
        band_kernel,
        in_specs=[VMEM] * 3,
        out_specs=VMEM,
        out_shape=jax.ShapeDtypeStruct((channels, 3 * strip), middle.dtype),
        compiler_params=params(16),
        cost_estimate=cost(0, MIB),
    )(left, middle, right)


def own_kernel(fields, embed_weight, source_weight, embedded, table):
    values = silu(dot_rows(fields[...], embed_weight[...])).astype(BF16)
    embedded[...] = values
    put_table(table, 0, dot(values, source_weight[...]).astype(BF16).astype(F32))


def embed_own(fields, embed_weight, source_weight):
    channels, cells = fields.shape
    width = embed_weight.shape[1]
    parts = width // LANES
    tile = 512
    return pl.pallas_call(
        own_kernel,
        grid=(cells // tile,),
        in_specs=[
            pl.BlockSpec((channels, tile), lambda i: (0, i)),
            pl.BlockSpec((channels, width), lambda i: (0, 0)),
            pl.BlockSpec((width, width), lambda i: (0, 0)),
        ],
        out_specs=[
            pl.BlockSpec((tile, width), lambda i: (i, 0)),
            pl.BlockSpec((tile * parts, LANES), lambda i: (i, 0)),
        ],
        out_shape=[
            jax.ShapeDtypeStruct((cells, width), BF16),
            jax.ShapeDtypeStruct((cells * parts, LANES), F32),
        ],
        compiler_params=params(20),
        cost_estimate=cost(2 * cells * width * (width + 256), 8 * MIB),
    )(fields, embed_weight, source_weight)


ENCODE_TILE = 512


def encode_kernel(
    index, valid, strip_w, strip_e, strip_far, strip_near, own_table, receivers, geometry,
    edge_weight, embed_weight, source_weight, second, first_weight, node_second, gain, static,
    next_source, mesh_start, next_table, table, one, two, total, wide, sem,
):
    cells = own_table.shape[0]
    parts = second.shape[0] // LANES
    copy = pltpu.make_async_copy(own_table, table.at[pl.ds(0, cells)], sem)
    copy.start()
    done = cells // parts
    sides = jnp.concatenate([strip_w[...], strip_e[...]], axis=1)
    for strip in (sides, strip_far[...], strip_near[...]):
        values = silu(dot_rows(strip, embed_weight[...])).astype(BF16)
        values = dot(values, source_weight[...]).astype(BF16).astype(F32)
        put_table(table, done, values)
        done += strip.shape[1]
    total[...] = jnp.zeros_like(total)
    copy.wait()
    tile = ENCODE_TILE

    def fetch(i, rows, piece, pieces_):
        count = tile // pieces_
        gather(index, i * tile + piece * count, count, table, rows, piece * count, parts)

    def work(i, rows, more):
        begin = pl.multiple_of(i * tile, tile)
        span = pl.ds(begin, tile)
        shift = geometry_term(geometry[:, span], edge_weight[...])
        picks = onehot(receivers[:, span], begin, valid[0, 0], total.shape[0])
        more(0, 8)
        hidden = []
        for part in range(parts):
            here = shift[:, part * LANES : (part + 1) * LANES]
            hidden.append(silu(rows[pl.ds(part, tile, stride=parts), :] + here).astype(BF16))
            more(1 + part, 8)
        more(5, 8)
        total[...] += dot(picks, jnp.concatenate(hidden, axis=1))
        more(6, 8)
        more(7, 8)

    pipeline(receivers.shape[1] // tile, fetch, work, one, two)
    gathered = dot(total[...].astype(BF16), second[...]).astype(BF16)
    node_hidden = silu(dot(gathered, first_weight[...])).astype(BF16)
    normed = layer_norm(dot(node_hidden, node_second[...]), gain[...])
    start = (static[...].astype(F32) + normed).astype(BF16)
    mesh_start[...] = start
    put_table(wide, 0, dot(start, next_source[...]))
    next_table[...] = wide[...].astype(BF16)


def encode(index, valid, strips, own_table, receivers, geometry, edge_weight, weights, static):
    nodes, width = static.shape
    parts = width // LANES
    strip = strips[0].shape[1]
    tile = pltpu.VMEM((ENCODE_TILE * parts, LANES), F32)
    return pl.pallas_call(
        encode_kernel,
        in_specs=[SMEM] * 2 + [VMEM] * 4 + [ANY] + [VMEM] * 11,
        out_specs=[VMEM, VMEM],
        out_shape=[
            jax.ShapeDtypeStruct((nodes, width), BF16),
            jax.ShapeDtypeStruct((nodes * parts, LANES), BF16),
        ],
        scratch_shapes=[
            pltpu.VMEM((own_table.shape[0] + 8 * strip * parts, LANES), F32),
            tile,
            tile,
            pltpu.VMEM((nodes, width), F32),
            pltpu.VMEM((nodes * parts, LANES), F32),
            pltpu.SemaphoreType.DMA,
        ],
        compiler_params=params(36),
        cost_estimate=cost(2 * receivers.shape[1] * width * 2 * width, 10 * MIB),
    )(
        index, valid, *strips, own_table, receivers, geometry, edge_weight,
        weights[0], weights[1], weights[2], weights[3], weights[4], weights[5], static, weights[6],
    )


def receive_kernel(
    valid, start, target_weight, state_weight, receivers, geometry, edge_weight, shift, state, target
):
    @pl.when(pl.program_id(0) == 0)
    def _():
        target[...] = dot(start[...], target_weight[...]).astype(BF16)
        state[...] = dot(start[...], state_weight[...])

    begin = pl.program_id(0) * receivers.shape[1]
    picks = onehot(receivers[...], begin, valid[0, 0], start.shape[0])
    shift[...] = (
        dot_rows(picks, target[...]) + geometry_term(geometry[...], edge_weight[...])
    ).astype(BF16)


def receive(valid, start, target_weight, state_weight, receivers, geometry, edge_weight):
    nodes, width = start.shape
    edges = receivers.shape[1]
    tile = 512
    whole = lambda i: (0, 0)
    return pl.pallas_call(
        receive_kernel,
        grid=(edges // tile,),
        in_specs=[
            SMEM,
            pl.BlockSpec((nodes, width), whole),
            pl.BlockSpec((width, width), whole),
            pl.BlockSpec((width, width), whole),
            pl.BlockSpec((1, tile), lambda i: (0, i)),
            pl.BlockSpec((geometry.shape[0], tile), lambda i: (0, i)),
            pl.BlockSpec(edge_weight.shape, whole),
        ],
        out_specs=[
            pl.BlockSpec((tile, width), lambda i: (i, 0)),
            pl.BlockSpec((nodes, width), whole),
        ],
        out_shape=[
            jax.ShapeDtypeStruct((edges, width), BF16),
            jax.ShapeDtypeStruct((nodes, width), F32),
        ],
        scratch_shapes=[pltpu.VMEM((nodes, width), BF16)],
        compiler_params=params(20),
        cost_estimate=cost(2 * edges * width * 2 * width, 8 * MIB),
    )(valid, start, target_weight, state_weight, receivers, geometry, edge_weight)


def fill_table(blocks, table):
    size = blocks[0].shape[0]
    for slot, block in enumerate(blocks):
        table[pl.ds(slot * size, size), :] = block[...].astype(F32)


PROCESS_TILE = 512


def process_kernel(
    index, valid, b0, b1, b2, b3, b4, b5, b6, b7, b8, receivers, shift, state, start, second,
    message_weight, out_weight, gain, next_source, next_table, table, one, two, total, wide,
):
    parts = second.shape[0] // LANES
    total[...] = jnp.zeros_like(total)
    fill_table((b0, b1, b2, b3, b4, b5, b6, b7, b8), table)
    tile = PROCESS_TILE

    def fetch(i, rows, piece, pieces_):
        count = tile // pieces_
        gather(index, i * tile + piece * count, count, table, rows, piece * count, parts)

    def work(i, rows, more):
        begin = pl.multiple_of(i * tile, tile)
        span = pl.ds(begin, tile)
        picks = onehot(receivers[:, span], begin, valid[0, 0], total.shape[0])
        more(0, 8)
        hidden = []
        for part in range(parts):
            here = shift[span, part * LANES : (part + 1) * LANES].astype(F32)
            hidden.append(silu(rows[pl.ds(part, tile, stride=parts), :] + here).astype(BF16))
            more(1 + part, 8)
        more(5, 8)
        total[...] += dot(picks, jnp.concatenate(hidden, axis=1))
        more(6, 8)
        more(7, 8)

    pipeline(receivers.shape[1] // tile, fetch, work, one, two)
    summed = dot(total[...].astype(BF16), second[...]).astype(BF16)
    update = silu(dot(summed, message_weight[...]) + state[...]).astype(BF16)
    normed = layer_norm(dot(update, out_weight[...]), gain[...])
    end = (start[...].astype(F32) + normed).astype(BF16)
    put_table(wide, 0, dot(end, next_source[...]))
    next_table[...] = wide[...].astype(BF16)


def process(index, valid, blocks, receivers, shift, state, start, weights):
    nodes, width = start.shape
    parts = width // LANES
    edges = receivers.shape[1]
    tile = pltpu.VMEM((PROCESS_TILE * parts, LANES), F32)
    return pl.pallas_call(
        process_kernel,
        in_specs=[SMEM] * 2 + [VMEM] * 18,
        out_specs=VMEM,
        out_shape=jax.ShapeDtypeStruct((nodes * parts, LANES), BF16),
        scratch_shapes=[
            pltpu.VMEM((9 * nodes * parts, LANES), F32),
            tile,
            tile,
            pltpu.VMEM((nodes, width), F32),
            pltpu.VMEM((nodes * parts, LANES), F32),
        ],
        compiler_params=params(36),
        cost_estimate=cost(2 * edges * width * 2 * width, 12 * MIB),
    )(index, valid, *blocks, receivers, shift, state, start, *weights)


DECODE_TILE = 256


def decode_kernel(
    index, b0, b1, b2, b3, b4, b5, b6, b7, b8, embedded, fields, target_weight, hidden_weight,
    output_weight, prediction, table, one, two,
):
    cells, width = embedded.shape
    parts = width // LANES
    fill_table((b0, b1, b2, b3, b4, b5, b6, b7, b8), table)
    tile = DECODE_TILE

    def fetch(i, rows, piece, pieces_):
        count = tile // pieces_
        for k in range(3):
            first = k * cells + i * tile + piece * count
            gather(index, first, count, table, rows, k * tile + piece * count, parts)

    def work(i, rows, more):
        begin = pl.multiple_of(i * tile, tile)
        target = dot(embedded[pl.ds(begin, tile), :], target_weight[...])
        summed = []
        for part in range(parts):
            here = target[:, part * LANES : (part + 1) * LANES]
            edge = [
                silu(rows[pl.ds(k * tile * parts + part, tile, stride=parts), :] + here)
                .astype(BF16)
                .astype(F32)
                for k in range(3)
            ]
            summed.append((edge[0] + edge[1] + edge[2]).astype(BF16))
            more(part, 8)
        more(4, 8)
        more(5, 8)
        final = silu(dot(jnp.concatenate(summed, axis=1), hidden_weight[...])).astype(BF16)
        more(6, 8)
        more(7, 8)
        change = lax.dot_general(
            output_weight[...], final, (((1,), (1,)), ((), ())), preferred_element_type=F32
        )
        result = fields[:, pl.ds(begin, tile)].astype(F32) + change
        prediction[:, 0, pl.ds(begin, tile)] = result

    pipeline(cells // tile, fetch, work, one, two)


def decode(index, blocks, embedded, fields, target_weight, hidden_weight, output_weight):
    cells, width = embedded.shape
    channels = fields.shape[0]
    parts = width // LANES
    size = blocks[0].shape[0]
    tile = pltpu.VMEM((3 * DECODE_TILE * parts, LANES), F32)
    return pl.pallas_call(
        decode_kernel,
        in_specs=[SMEM] + [VMEM] * 14,
        out_specs=VMEM,
        out_shape=jax.ShapeDtypeStruct((channels, 1, cells), F32),
        scratch_shapes=[pltpu.VMEM((9 * size, LANES), F32), tile, tile],
        compiler_params=params(36),
        cost_estimate=cost(2 * cells * width * 3 * width, 12 * MIB),
    )(index, *blocks, embedded, fields, target_weight, hidden_weight, output_weight)


def east(values):
    count = lax.axis_size("lon")
    return lax.ppermute(values, "lon", [(i, (i + 1) % count) for i in range(count)])


def west(values):
    count = lax.axis_size("lon")
    return lax.ppermute(values, "lon", [((i + 1) % count, i) for i in range(count)])


def near(values):
    count = lax.axis_size("lat")
    return lax.ppermute(values, "lat", [(i, i ^ 1) for i in range(count)])


def far(values):
    count = lax.axis_size("lat")
    ups = [(i, i + 1) for i in range(1, count - 1, 2)]
    return lax.ppermute(values, "lat", ups + [(b, a) for a, b in ups])


def swap_strips(strip):
    w, e = east(strip), west(strip)
    band = make_band(w, strip, e)
    return w, e, far(band), near(band)


def lon_shift(values, turn):
    bands, sectors = lax.axis_size("lat"), lax.axis_size("lon")
    pairs = []
    for i in range(bands):
        step = turn if i % 2 == 0 else -turn
        pairs += [(i * sectors + j, i * sectors + (j + step) % sectors) for j in range(sectors)]
    return lax.ppermute(values, ("lat", "lon"), pairs)


def swap_blocks(block):
    fore = lon_shift(block, -1)
    away = far(block)
    close = near(block)
    again, fore = lax.optimization_barrier((block, fore))
    aft = lon_shift(again, 1)
    corner_fore = lon_shift(away, -1)
    corner_aft = far(fore)
    return block, fore, aft, away, close, corner_fore, corner_aft, near(fore), near(aft)


def slots(block, same, away, close):
    a, b = block // 3, block % 3
    is_near = (a == 0) == (lax.axis_index("lat") % 2 == 1)

    def choose(three):
        return jnp.where(b == 0, three[0], jnp.where(b == 1, three[1], three[2]))

    return jnp.where(a == 1, choose(same), jnp.where(is_near, choose(close), choose(away)))


def grid_index(senders, cells, strip, parts):
    block, offset = senders // cells, senders % cells
    slot = slots(block, (0, 0, 1), (2, 3, 4), (5, 6, 7))
    outside = cells + slot * strip + offset % strip
    return jnp.where(block == 4, offset, outside) * parts


def mesh_index(senders, nodes, parts):
    block = senders // nodes
    odd = lax.axis_index("lat") % 2 == 1
    block = jnp.where(odd, block // 3 * 3 + 2 - block % 3, block)
    slot = slots(block, (2, 0, 1), (6, 3, 5), (7, 4, 8))
    return (slot * nodes + senders % nodes) * parts


def shards(
    grid_fields,
    mesh_static,
    encode_senders,
    encode_receivers,
    encode_geometry,
    encode_valid,
    mesh_senders,
    mesh_receivers,
    mesh_geometry,
    mesh_valid,
    decode_senders,
    embed_weight,
    encode_source,
    encode_edge,
    encode_second,
    node_first,
    node_second,
    node_gain,
    process_source,
    process_target,
    process_edge,
    process_second,
    update_message,
    update_state,
    update_out,
    process_gain,
    decode_source,
    decode_target,
    decode_hidden,
    output_weight,
):
    fields = grid_fields[0, 0].T
    static = mesh_static[0, 0]
    cells, nodes, width = fields.shape[1], static.shape[0], static.shape[1]
    parts = width // LANES
    strip = cells // 8
    strips = swap_strips(take_strip(fields, strip))
    encode_index = grid_index(encode_senders[0, 0], cells, strip, parts)
    process_index = mesh_index(mesh_senders[0, 0], nodes, parts)
    decode_index = mesh_index(decode_senders[0, 0].reshape(-1), nodes, parts)
    embedded, own_table = embed_own(fields, embed_weight, encode_source)
    start, table = encode(
        encode_index,
        encode_valid,
        strips,
        own_table,
        encode_receivers[0],
        encode_geometry[0, 0],
        encode_edge,
        (
            embed_weight,
            encode_source,
            encode_second,
            node_first,
            node_second,
            node_gain[None],
            process_source,
        ),
        static,
    )
    blocks = swap_blocks(table)
    shift, state = receive(
        mesh_valid,
        start,
        process_target,
        update_state,
        mesh_receivers[0],
        mesh_geometry[0, 0],
        process_edge,
    )
    table = process(
        process_index,
        mesh_valid,
        blocks,
        mesh_receivers[0],
        shift,
        state,
        start,
        (process_second, update_message, update_out, process_gain[None], decode_source),
    )
    blocks = swap_blocks(table)
    prediction = decode(
        decode_index, blocks, embedded, fields, decode_target, decode_hidden, output_weight.T
    )
    return prediction.transpose(1, 2, 0)[None]


def solution(mesh):
    devices = P("lat", "lon")
    in_specs = (devices,) * 11 + (P(),) * 19
    return jax.shard_map(
        shards, mesh=mesh, in_specs=in_specs, out_specs=devices, check_vma=False
    )
```

time: 147 us -> 107 us (0.73)
  Pallas kernels: 65.4 us -> 42.9 us
  local copies, waits for them, and re-layouts: 12.1 us -> 4.22 us
  other arithmetic: 5.06 us -> 0.22 us
  starting transfers between devices: 40.2 us -> 38 us
  waiting for transfers between devices: 20.7 us -> 18.9 us
    pallas_call x4 -> x6, Pallas kernels: 59.8 us -> 39.9 us  [the longest x1 13.4 us: decode(): pl.pallas_call(decode_kernel, in_specs=[SMEM] + [VMEM] * 14, out_specs=VM...]
    ppermute x0 -> x6, waiting for transfers between devices: none -> 16.6 us  [lon_shift(): return lax.ppermute(values, ('lat', 'lon'), pairs)]
    ppermute x5 -> x1, waiting for transfers between devices: 12.9 us -> 0.01 us  [west(): lax.ppermute(values, 'lon', [((i + 1) % count, i) for i in range(count)])]
    ppermute x5 -> x1, starting transfers between devices: 8.22 us -> 1.44 us  [west(): lax.ppermute(values, 'lon', [((i + 1) % count, i) for i in range(count)])]
    broadcast_in_dim x2 -> x0, local copies, waits for them, and re-layouts: 6 us -> none  [the longest x1 5.99 us: shards(): return prediction[None, None]]
    ppermute x5 -> x1, waiting for transfers between devices: 7.77 us -> 2.27 us  [east(): lax.ppermute(values, 'lon', [(i, (i + 1) % count) for i in range(count)])]
    ppermute x0 -> x6, starting transfers between devices: none -> 4.47 us  [lon_shift(): return lax.ppermute(values, ('lat', 'lon'), pairs)]
    pallas_call x1, Pallas kernels: 5.6 us -> 2.99 us  [embed_own(): pl.pallas_call(own_kernel, grid=(cells // tile,), in_specs=[pl.BlockSpec(...]
  transfers between devices with their start and end apart: 24 -> 20, of which waited for: 5 -> 6; matrix products, arithmetic and copies ran while one was open for 5% -> 0% of each run, Pallas kernels for 10% -> 8%
where the time goes in v2:
time: 107 us; the launch traced here: 106 us
  Pallas kernels  42.9 us (40%)
  starting transfers between devices  38 us (36%)
  waiting for transfers between devices  18.9 us (18%)
  local copies, waits for them, and re-layouts  4.22 us (4%)
  between operations  1.85 us (2%)
    ppermute x5, starting transfers between devices, far(): return lax.ppermute(values, 'lat', ups + [(b, a) for a, b in ups])  21.7 us
    ppermute x6, waiting for transfers between devices, lon_shift(): return lax.ppermute(values, ('lat', 'lon'), pairs)  16.6 us
    pallas_call x1, Pallas kernels, decode(): pl.pallas_call(decode_kernel, in_specs=[SMEM] + [VMEM] * 14, out_specs=VM...  13.4 us
    pallas_call x1, Pallas kernels, encode(): pl.pallas_call(encode_kernel, in_specs=[SMEM] * 2 + [VMEM] * 4 + [ANY] +...  10.2 us
    ppermute x7, starting transfers between devices, near(): return lax.ppermute(values, 'lat', [(i, i ^ 1) for i in range(count)])  9.13 us
    pallas_call x1, Pallas kernels, process(): pl.pallas_call(process_kernel, in_specs=[SMEM] * 2 + [VMEM] * 18, out_spe...  9.01 us
    pallas_call x1, Pallas kernels, receive(): pl.pallas_call(receive_kernel, grid=(edges // tile,), in_specs=[SMEM, pl....  5.73 us
    ppermute x6, starting transfers between devices, lon_shift(): return lax.ppermute(values, ('lat', 'lon'), pairs)  4.47 us
  transfers between devices with their start and end apart: 20, of which 6 were waited for; matrix products, arithmetic and copies ran while one was open for 0% of the time, Pallas kernels for 8%

profile of v2, /device:TPU:3, one launch (start us, length us, event | category | flops | bytes accessed | tf_op | source)
XLA Modules:
  0.0 106.2 jit_solution(5756644927252913066)
XLA Ops:
  0.0 1.6 %shard_map.280.middle = bf16[227,256]{1,0:T(8,128)(2,1)} custom-call(bf16[227,2048]{1,0:T(8,128)(2,1)} %bitcast.19), custom_call_target="tpu_custom_call" | custom-call | bytes 1048576 | tf_op jit(solution)/shard_map/pallas_call | solution.py:100
  1.7 1.3 %collective-permute-start = (bf16[227,256]{1,0:T(8,128)(2,1)}, bf16[227,256]{1,0:T(8,128)(2,1)S(1)}, u32[]{:S(2)}, u32[]{:S(2)}) collective-permute-start(bf16[227,256]{1,0:T(8,128)(2,1)} %shard_map.280.middle), channel_id=1, source_target_pairs={{0,1},{1,2},{2,3},{3,0},{4,5},{5,6},{6,7},{7,4},{8,9},{9,10},{10,1... | collective-permute-start | bytes 348680 | tf_op jit(solution)/shard_map/ppermute | solution.py:420
  3.0 1.4 %collective-permute-start.1 = (bf16[227,256]{1,0:T(8,128)(2,1)}, bf16[227,256]{1,0:T(8,128)(2,1)S(1)}, u32[]{:S(2)}, u32[]{:S(2)}) collective-permute-start(bf16[227,256]{1,0:T(8,128)(2,1)} %shard_map.280.middle), channel_id=1, source_target_pairs={{1,0},{2,1},{3,2},{0,3},{5,4},{6,5},{7,6},{4,7},{9,8},{10,9},{11,1... | collective-permute-start | bytes 348680 | tf_op jit(solution)/shard_map/ppermute | solution.py:425
  5.1 2.3 %collective-permute-done.left.strip_w = bf16[227,256]{1,0:T(8,128)(2,1)S(1)} collective-permute-done((bf16[227,256]{1,0:T(8,128)(2,1)}, bf16[227,256]{1,0:T(8,128)(2,1)S(1)}, u32[]{:S(2)}, u32[]{:S(2)}) %collective-permute-start) | collective-permute-done | bytes 116256 | tf_op jit(solution)/shard_map/ppermute | solution.py:420
  7.3 0.9 copy-done.2
  8.3 5.2 %collective-permute-start.2 = (bf16[227,768]{1,0:T(8,128)(2,1)S(1)}, bf16[227,768]{1,0:T(8,128)(2,1)S(1)}, u32[]{:S(2)}, u32[]{:S(2)}) collective-permute-start(bf16[227,768]{1,0:T(8,128)(2,1)S(1)} %shard_map.281), channel_id=1, source_target_pairs={{4,8},{12,16},{20,24},{28,32},{36,40},{44,48},{52,56},{60,64},{68,... | collective-permute-start | bytes 1046024 | tf_op jit(solution)/shard_map/ppermute | solution.py:436
  13.5 1.0 collective-permute-start.3
  14.5 1.2 %copy-done = bf16[1,1,2048,227]{2,3,1,0:T(8,128)(2,1)S(1)} copy-done((bf16[1,1,2048,227]{2,3,1,0:T(8,128)(2,1)S(1)}, bf16[1,1,2048,227]{2,3,1,0:T(8,128)(2,1)}, u32[]{:S(2)}) %copy-start) | copy-done | bytes 929816
  15.7 1.0 copy-done.3
  16.8 0.9 copy-done.18
  17.7 3.0 %shard_map.282 = (bf16[2048,512]{1,0:T(8,128)(2,1)S(1)}, f32[8192,128]{1,0:T(8,128)S(1)}) custom-call(bf16[227,2048]{1,0:T(8,128)(2,1)S(1)} %bitcast.20, bf16[227,512]{1,0:T(8,128)(2,1)S(1)} %copy-done.18, bf16[512,512]{1,0:T(8,128)(2,1)S(1)} %copy-done.3), custom_call_target="tpu_custom_call" | custom-call | flops 1610612736 | bytes 8388608 | tf_op jit(solution)/shard_map/pallas_call | solution.py:138
  21.0 10.2 %shard_map.283 = (bf16[512,512]{1,0:T(8,128)(2,1)S(1)}, bf16[2048,128]{1,0:T(8,128)(2,1)S(1)}) custom-call(s32[3072]{0:T(1024)S(1)} %fusion.21.index, s32[1,1]{1,0:T(1,128)S(6)} %copy.32.valid, bf16[227,256]{1,0:T(8,128)(2,1)S(1)} %collective-permute-done.left.strip_w, bf16[227,256]{1,0:T(8,128)(2,1)S(1)} %collective-permute-done.1.right.strip_e, ...), custom_call_target="tpu_custom_call" | custom-call | flops 3221225472 | bytes 10485760 | tf_op jit(solution)/shard_map/pallas_call | solution.py:217
  31.1 1.1 %collective-permute-start.4 = (bf16[2048,128]{1,0:T(8,128)(2,1)S(1)}, bf16[2048,128]{1,0:T(8,128)(2,1)S(1)}, u32[]{:S(2)}, u32[]{:S(2)}) collective-permute-start(bf16[2048,128]{1,0:T(8,128)(2,1)S(1)} %get-tuple-element.18.b0), channel_id=1, source_target_pairs={{0,3},{1,0},{2,1},{3,2},{4,5},{5,6},{6,7},{7,4},{8,11},{9,8},{10,9... | collective-permute-start | bytes 1572872 | tf_op jit(solution)/shard_map/ppermute | solution.py:451
  32.3 4.8 %collective-permute-start.6 = (bf16[2048,128]{1,0:T(8,128)(2,1)S(1)}, bf16[2048,128]{1,0:T(8,128)(2,1)S(1)}, u32[]{:S(2)}, u32[]{:S(2)}) collective-permute-start(bf16[2048,128]{1,0:T(8,128)(2,1)S(1)} %get-tuple-element.18.b0), channel_id=1, source_target_pairs={{4,8},{12,16},{20,24},{28,32},{36,40},{44,48},{52,56},{60,64},{68,... | collective-permute-start | bytes 1572872 | tf_op jit(solution)/shard_map/ppermute | solution.py:436
  37.1 3.7 %collective-permute-done.4.b1 = bf16[2048,128]{1,0:T(8,128)(2,1)S(1)} collective-permute-done((bf16[2048,128]{1,0:T(8,128)(2,1)S(1)}, bf16[2048,128]{1,0:T(8,128)(2,1)S(1)}, u32[]{:S(2)}, u32[]{:S(2)}) %collective-permute-start.4) | collective-permute-done | bytes 524320 | tf_op jit(solution)/shard_map/ppermute | solution.py:451
  40.7 1.0 collective-permute-start.5
  42.4 0.4 collective-permute-start.7
  43.0 3.2 %collective-permute-start.9 = (bf16[2048,128]{1,0:T(8,128)(2,1)S(1)}, bf16[2048,128]{1,0:T(8,128)(2,1)S(1)}, u32[]{:S(2)}, u32[]{:S(2)}) collective-permute-start(bf16[2048,128]{1,0:T(8,128)(2,1)S(1)} %collective-permute-done.4.b1), channel_id=1, source_target_pairs={{4,8},{12,16},{20,24},{28,32},{36,40},{44,48},{52,56},{60,64},{68,... | collective-permute-start | bytes 1572872 | tf_op jit(solution)/shard_map/ppermute | solution.py:436
  46.2 1.1 collective-permute-start.8
  47.2 1.8 %collective-permute-done.5.b2 = bf16[2048,128]{1,0:T(8,128)(2,1)S(1)} collective-permute-done((bf16[2048,128]{1,0:T(8,128)(2,1)S(1)}, bf16[2048,128]{1,0:T(8,128)(2,1)S(1)}, u32[]{:S(2)}, u32[]{:S(2)}) %collective-permute-start.5) | collective-permute-done | bytes 524320 | tf_op jit(solution)/shard_map/ppermute | solution.py:451
  49.1 3.7 %collective-permute-start.11 = (bf16[2048,128]{1,0:T(8,128)(2,1)S(1)}, bf16[2048,128]{1,0:T(8,128)(2,1)S(1)}, u32[]{:S(2)}, u32[]{:S(2)}) collective-permute-start(bf16[2048,128]{1,0:T(8,128)(2,1)S(1)} %collective-permute-done.5.b2), channel_id=1, source_target_pairs={{0,4},{4,0},{8,12},{12,8},{16,20},{20,16},{24,28},{28,24},{32,36},... | collective-permute-start | bytes 1572872 | tf_op jit(solution)/shard_map/ppermute | solution.py:430
  52.9 5.7 %shard_map.284 = (bf16[4096,512]{1,0:T(8,128)(2,1)S(1)}, f32[512,512]{1,0:T(8,128)S(1)}) custom-call(s32[1,1]{1,0:T(1,128)S(6)} %copy.33.valid, bf16[512,512]{1,0:T(8,128)(2,1)S(1)} %get-tuple-element.19.start, bf16[512,512]{1,0:T(8,128)(2,1)S(1)} %copy-done.10, bf16[512,512]{1,0:T(8,128)(2,1)S(1)} %copy-done.11, s32[1,4096]{1,0:T(1,128)S(1)} %bitcast.26, ...), custom_call_target="tpu_custom_call" | custom-call | flops 4294967296 | bytes 8388608 | tf_op jit(solution)/shard_map/pallas_call | solution.py:261
  58.8 9.0 %shard_map.285.b0 = bf16[2048,128]{1,0:T(8,128)(2,1)S(1)} custom-call(s32[4096]{0:T(1024)S(1)} %fusion.14.index, s32[1,1]{1,0:T(1,128)S(6)} %copy.33.valid, bf16[2048,128]{1,0:T(8,128)(2,1)S(1)} %get-tuple-element.18.b0, bf16[2048,128]{1,0:T(8,128)(2,1)S(1)} %collective-permute-done.4.b1, bf16[2048,128]{1,0:T(8,128)(2,1)S(1)} %collective-permute-done.5.b2, ...), custom_call_target="tpu_custom_call" | custom-call | flops 4294967296 | bytes 12582912 | tf_op jit(solution)/shard_map/pallas_call | solution.py:338
  67.9 5.2 %collective-permute-start.14 = (bf16[2048,128]{1,0:T(8,128)(2,1)S(1)}, bf16[2048,128]{1,0:T(8,128)(2,1)S(1)}, u32[]{:S(2)}, u32[]{:S(2)}) collective-permute-start(bf16[2048,128]{1,0:T(8,128)(2,1)S(1)} %shard_map.285.b0), channel_id=1, source_target_pairs={{4,8},{12,16},{20,24},{28,32},{36,40},{44,48},{52,56},{60,64},{68,... | collective-permute-start | bytes 1572872 | tf_op jit(solution)/shard_map/ppermute | solution.py:436
  73.1 4.3 %collective-permute-done.12.b1 = bf16[2048,128]{1,0:T(8,128)(2,1)S(1)} collective-permute-done((bf16[2048,128]{1,0:T(8,128)(2,1)S(1)}, bf16[2048,128]{1,0:T(8,128)(2,1)S(1)}, u32[]{:S(2)}, u32[]{:S(2)}) %collective-permute-start.12) | collective-permute-done | bytes 524320 | tf_op jit(solution)/shard_map/ppermute | solution.py:451
  77.4 0.9 collective-permute-start.13
  78.4 3.3 %collective-permute-start.17 = (bf16[2048,128]{1,0:T(8,128)(2,1)S(1)}, bf16[2048,128]{1,0:T(8,128)(2,1)S(1)}, u32[]{:S(2)}, u32[]{:S(2)}) collective-permute-start(bf16[2048,128]{1,0:T(8,128)(2,1)S(1)} %collective-permute-done.12.b1), channel_id=1, source_target_pairs={{4,8},{12,16},{20,24},{28,32},{36,40},{44,48},{52,56},{60,64},{68,... | collective-permute-start | bytes 1572872 | tf_op jit(solution)/shard_map/ppermute | solution.py:436
  81.8 0.3 collective-permute-start.16
  82.1 3.7 %collective-permute-done.13.b2 = bf16[2048,128]{1,0:T(8,128)(2,1)S(1)} collective-permute-done((bf16[2048,128]{1,0:T(8,128)(2,1)S(1)}, bf16[2048,128]{1,0:T(8,128)(2,1)S(1)}, u32[]{:S(2)}, u32[]{:S(2)}) %collective-permute-start.13) | collective-permute-done | bytes 524320 | tf_op jit(solution)/shard_map/ppermute | solution.py:451
  85.8 3.8 %collective-permute-start.19 = (bf16[2048,128]{1,0:T(8,128)(2,1)S(1)}, bf16[2048,128]{1,0:T(8,128)(2,1)S(1)}, u32[]{:S(2)}, u32[]{:S(2)}) collective-permute-start(bf16[2048,128]{1,0:T(8,128)(2,1)S(1)} %collective-permute-done.13.b2), channel_id=1, source_target_pairs={{0,4},{4,0},{8,12},{12,8},{16,20},{20,16},{24,28},{28,24},{32,36},... | collective-permute-start | bytes 1572872 | tf_op jit(solution)/shard_map/ppermute | solution.py:430
  89.7 3.1 %collective-permute-done.16.b5 = bf16[2048,128]{1,0:T(8,128)(2,1)S(1)} collective-permute-done((bf16[2048,128]{1,0:T(8,128)(2,1)S(1)}, bf16[2048,128]{1,0:T(8,128)(2,1)S(1)}, u32[]{:S(2)}, u32[]{:S(2)}) %collective-permute-start.16) | collective-permute-done | bytes 524320 | tf_op jit(solution)/shard_map/ppermute | solution.py:451
  92.8 13.4 %shard_map.286 = f32[227,1,2048]{2,1,0:T(1,128)} custom-call(s32[6144]{0:T(1024)S(1)} %fusion.5.index, bf16[2048,128]{1,0:T(8,128)(2,1)S(1)} %shard_map.285.b0, bf16[2048,128]{1,0:T(8,128)(2,1)S(1)} %collective-permute-done.12.b1, bf16[2048,128]{1,0:T(8,128)(2,1)S(1)} %collective-permute-done.13.b2, bf16[2048,128]{1,0:T(8,128)(2,1)S(1)} %collective-permute-done.14.b3, ...), custom_call_target="tpu_custom_call" | custom-call | flops 3221225472 | bytes 12582912 | tf_op jit(solution)/shard_map/pallas_call | solution.py:407
  (82 shorter events, 0.8 us)
Async XLA Ops:
  0.0 20.8 %copy-start.5 = (bf16[512,512]{1,0:T(8,128)(2,1)S(1)}, bf16[512,512]{1,0:T(8,128)(2,1)}, u32[]{:S(2)}) copy-start(bf16[512,512]{1,0:T(8,128)(2,1)} %second.2) | copy-start | bytes 1572868
  1.7 5.7 %collective-permute-start = (bf16[227,256]{1,0:T(8,128)(2,1)}, bf16[227,256]{1,0:T(8,128)(2,1)S(1)}, u32[]{:S(2)}, u32[]{:S(2)}) collective-permute-start(bf16[227,256]{1,0:T(8,128)(2,1)} %shard_map.280.middle), channel_id=1, source_target_pairs={{0,1},{1,2},{2,3},{3,0},{4,5},{5,6},{6,7},{7,4},{8,9},{9,10},{10,1... | collective-permute-start | bytes 348680 | tf_op jit(solution)/shard_map/ppermute | solution.py:420
  3.0 4.4 %collective-permute-start.1 = (bf16[227,256]{1,0:T(8,128)(2,1)}, bf16[227,256]{1,0:T(8,128)(2,1)S(1)}, u32[]{:S(2)}, u32[]{:S(2)}) collective-permute-start(bf16[227,256]{1,0:T(8,128)(2,1)} %shard_map.280.middle), channel_id=1, source_target_pairs={{1,0},{2,1},{3,2},{0,3},{5,4},{6,5},{7,6},{4,7},{9,8},{10,9},{11,1... | collective-permute-start | bytes 348680 | tf_op jit(solution)/shard_map/ppermute | solution.py:425
  8.3 12.5 %collective-permute-start.2 = (bf16[227,768]{1,0:T(8,128)(2,1)S(1)}, bf16[227,768]{1,0:T(8,128)(2,1)S(1)}, u32[]{:S(2)}, u32[]{:S(2)}) collective-permute-start(bf16[227,768]{1,0:T(8,128)(2,1)S(1)} %shard_map.281), channel_id=1, source_target_pairs={{4,8},{12,16},{20,24},{28,32},{36,40},{44,48},{52,56},{60,64},{68,... | collective-permute-start | bytes 1046024 | tf_op jit(solution)/shard_map/ppermute | solution.py:436
  13.5 7.3 %collective-permute-start.3 = (bf16[227,768]{1,0:T(8,128)(2,1)S(1)}, bf16[227,768]{1,0:T(8,128)(2,1)S(1)}, u32[]{:S(2)}, u32[]{:S(2)}) collective-permute-start(bf16[227,768]{1,0:T(8,128)(2,1)S(1)} %shard_map.281), channel_id=1, source_target_pairs={{0,4},{4,0},{8,12},{12,8},{16,20},{20,16},{24,28},{28,24},{32,36},... | collective-permute-start | bytes 1046024 | tf_op jit(solution)/shard_map/ppermute | solution.py:430
  20.9 31.8 %copy-start.30 = (s32[1,1,4096]{2,1,0:T(1,128)S(1)}, s32[1,1,4096]{2,1,0:T(1,128)}, u32[]{:S(2)}) copy-start(s32[1,1,4096]{2,1,0:T(1,128)} %param.36) | copy-start | bytes 49156
  20.9 31.9 %copy-start.10 = (bf16[512,512]{1,0:T(8,128)(2,1)S(1)}, bf16[512,512]{1,0:T(8,128)(2,1)}, u32[]{:S(2)}) copy-start(bf16[512,512]{1,0:T(8,128)(2,1)} %target_weight.2) | copy-start | bytes 1572868
  20.9 31.9 %copy-start.11 = (bf16[512,512]{1,0:T(8,128)(2,1)S(1)}, bf16[512,512]{1,0:T(8,128)(2,1)}, u32[]{:S(2)}) copy-start(bf16[512,512]{1,0:T(8,128)(2,1)} %state_weight.1) | copy-start | bytes 1572868
  20.9 31.9 %copy-start.21 = (f32[1,1,4,4096]{3,2,1,0:T(4,128)S(1)}, f32[1,1,4,4096]{3,2,1,0:T(4,128)}, u32[]{:S(2)}) copy-start(f32[1,1,4,4096]{3,2,1,0:T(4,128)} %param.38) | copy-start | bytes 196612
  21.0 31.9 %copy-start.23 = (s32[1,1,4096]{2,1,0:T(1,128)S(1)}, s32[1,1,4096]{2,1,0:T(1,128)}, u32[]{:S(2)}) copy-start(s32[1,1,4096]{2,1,0:T(1,128)} %param.37) | copy-start | bytes 49156
  21.0 31.9 %copy-start.26 = (f32[4,512]{1,0:T(4,128)S(1)}, f32[4,512]{1,0:T(4,128)}, u32[]{:S(2)}) copy-start(f32[4,512]{1,0:T(4,128)} %edge_weight.3) | copy-start | bytes 24580
  31.1 9.6 %collective-permute-start.4 = (bf16[2048,128]{1,0:T(8,128)(2,1)S(1)}, bf16[2048,128]{1,0:T(8,128)(2,1)S(1)}, u32[]{:S(2)}, u32[]{:S(2)}) collective-permute-start(bf16[2048,128]{1,0:T(8,128)(2,1)S(1)} %get-tuple-element.18.b0), channel_id=1, source_target_pairs={{0,3},{1,0},{2,1},{3,2},{4,5},{5,6},{6,7},{7,4},{8,11},{9,8},{10,9... | collective-permute-start | bytes 1572872 | tf_op jit(solution)/shard_map/ppermute | solution.py:451
  32.3 13.9 %collective-permute-start.6 = (bf16[2048,128]{1,0:T(8,128)(2,1)S(1)}, bf16[2048,128]{1,0:T(8,128)(2,1)S(1)}, u32[]{:S(2)}, u32[]{:S(2)}) collective-permute-start(bf16[2048,128]{1,0:T(8,128)(2,1)S(1)} %get-tuple-element.18.b0), channel_id=1, source_target_pairs={{4,8},{12,16},{20,24},{28,32},{36,40},{44,48},{52,56},{60,64},{68,... | collective-permute-start | bytes 1572872 | tf_op jit(solution)/shard_map/ppermute | solution.py:436
  40.7 8.3 %collective-permute-start.5 = (bf16[2048,128]{1,0:T(8,128)(2,1)S(1)}, bf16[2048,128]{1,0:T(8,128)(2,1)S(1)}, u32[]{:S(2)}, u32[]{:S(2)}) collective-permute-start(bf16[2048,128]{1,0:T(8,128)(2,1)S(1)} %get-tuple-element.18.b0), channel_id=1, source_target_pairs={{0,1},{1,2},{2,3},{3,0},{4,7},{5,4},{6,5},{7,6},{8,9},{9,10},{10,1... | collective-permute-start | bytes 1572872 | tf_op jit(solution)/shard_map/ppermute | solution.py:451
  42.4 16.3 %collective-permute-start.7 = (bf16[2048,128]{1,0:T(8,128)(2,1)S(1)}, bf16[2048,128]{1,0:T(8,128)(2,1)S(1)}, u32[]{:S(2)}, u32[]{:S(2)}) collective-permute-start(bf16[2048,128]{1,0:T(8,128)(2,1)S(1)} %get-tuple-element.18.b0), channel_id=1, source_target_pairs={{0,4},{4,0},{8,12},{12,8},{16,20},{20,16},{24,28},{28,24},{32,36},... | collective-permute-start | bytes 1572872 | tf_op jit(solution)/shard_map/ppermute | solution.py:430
  42.7 15.9 %collective-permute-start.10 = (bf16[2048,128]{1,0:T(8,128)(2,1)S(1)}, bf16[2048,128]{1,0:T(8,128)(2,1)S(1)}, u32[]{:S(2)}, u32[]{:S(2)}) collective-permute-start(bf16[2048,128]{1,0:T(8,128)(2,1)S(1)} %collective-permute-done.4.b1), channel_id=1, source_target_pairs={{0,4},{4,0},{8,12},{12,8},{16,20},{20,16},{24,28},{28,24},{32,36},... | collective-permute-start | bytes 1572872 | tf_op jit(solution)/shard_map/ppermute | solution.py:430
  43.0 15.7 %collective-permute-start.9 = (bf16[2048,128]{1,0:T(8,128)(2,1)S(1)}, bf16[2048,128]{1,0:T(8,128)(2,1)S(1)}, u32[]{:S(2)}, u32[]{:S(2)}) collective-permute-start(bf16[2048,128]{1,0:T(8,128)(2,1)S(1)} %collective-permute-done.4.b1), channel_id=1, source_target_pairs={{4,8},{12,16},{20,24},{28,32},{36,40},{44,48},{52,56},{60,64},{68,... | collective-permute-start | bytes 1572872 | tf_op jit(solution)/shard_map/ppermute | solution.py:436
  46.2 12.5 %collective-permute-start.8 = (bf16[2048,128]{1,0:T(8,128)(2,1)S(1)}, bf16[2048,128]{1,0:T(8,128)(2,1)S(1)}, u32[]{:S(2)}, u32[]{:S(2)}) collective-permute-start(bf16[2048,128]{1,0:T(8,128)(2,1)S(1)} %collective-permute-done.6.b3), channel_id=1, source_target_pairs={{0,3},{1,0},{2,1},{3,2},{4,5},{5,6},{6,7},{7,4},{8,11},{9,8},{10,9... | collective-permute-start | bytes 1572872 | tf_op jit(solution)/shard_map/ppermute | solution.py:451
  49.1 9.6 %collective-permute-start.11 = (bf16[2048,128]{1,0:T(8,128)(2,1)S(1)}, bf16[2048,128]{1,0:T(8,128)(2,1)S(1)}, u32[]{:S(2)}, u32[]{:S(2)}) collective-permute-start(bf16[2048,128]{1,0:T(8,128)(2,1)S(1)} %collective-permute-done.5.b2), channel_id=1, source_target_pairs={{0,4},{4,0},{8,12},{12,8},{16,20},{20,16},{24,28},{28,24},{32,36},... | collective-permute-start | bytes 1572872 | tf_op jit(solution)/shard_map/ppermute | solution.py:430
  58.8 30.8 %copy-start.29 = (s32[1,1,3,2048]{3,1,2,0:T(1,128)S(1)}, s32[1,1,3,2048]{3,1,2,0:T(1,128)}, u32[]{:S(2)}) copy-start(s32[1,1,3,2048]{3,1,2,0:T(1,128)} %param.40) | copy-start | bytes 73732
  58.8 34.0 %copy-start.1 = (bf16[1,1,2048,227]{2,3,1,0:T(8,128)(2,1)S(1)}, bf16[1,1,2048,227]{2,3,1,0:T(8,128)(2,1)}, u32[]{:S(2)}) copy-start(bf16[1,1,2048,227]{2,3,1,0:T(8,128)(2,1)} %param.30) | copy-start | bytes 2789380
  58.8 34.0 %copy-start.16 = (bf16[512,512]{1,0:T(8,128)(2,1)S(1)}, bf16[512,512]{1,0:T(8,128)(2,1)}, u32[]{:S(2)}) copy-start(bf16[512,512]{1,0:T(8,128)(2,1)} %target_weight.3) | copy-start | bytes 1572868
  58.8 34.0 %copy-start.17 = (bf16[512,512]{1,0:T(8,128)(2,1)S(1)}, bf16[512,512]{1,0:T(8,128)(2,1)}, u32[]{:S(2)}) copy-start(bf16[512,512]{1,0:T(8,128)(2,1)} %hidden_weight.1) | copy-start | bytes 1572868
  58.8 34.0 %copy-start.20 = (bf16[512,227]{0,1:T(8,128)(2,1)S(1)}, bf16[512,227]{0,1:T(8,128)(2,1)}, u32[]{:S(2)}) copy-start(bf16[512,227]{0,1:T(8,128)(2,1)} %param.59) | copy-start | bytes 697348
  67.8 9.6 %collective-permute-start.12 = (bf16[2048,128]{1,0:T(8,128)(2,1)S(1)}, bf16[2048,128]{1,0:T(8,128)(2,1)S(1)}, u32[]{:S(2)}, u32[]{:S(2)}) collective-permute-start(bf16[2048,128]{1,0:T(8,128)(2,1)S(1)} %shard_map.285.b0), channel_id=1, source_target_pairs={{0,3},{1,0},{2,1},{3,2},{4,5},{5,6},{6,7},{7,4},{8,11},{9,8},{10,9... | collective-permute-start | bytes 1572872 | tf_op jit(solution)/shard_map/ppermute | solution.py:451
  67.9 13.8 %collective-permute-start.14 = (bf16[2048,128]{1,0:T(8,128)(2,1)S(1)}, bf16[2048,128]{1,0:T(8,128)(2,1)S(1)}, u32[]{:S(2)}, u32[]{:S(2)}) collective-permute-start(bf16[2048,128]{1,0:T(8,128)(2,1)S(1)} %shard_map.285.b0), channel_id=1, source_target_pairs={{4,8},{12,16},{20,24},{28,32},{36,40},{44,48},{52,56},{60,64},{68,... | collective-permute-start | bytes 1572872 | tf_op jit(solution)/shard_map/ppermute | solution.py:436
  77.4 8.3 %collective-permute-start.13 = (bf16[2048,128]{1,0:T(8,128)(2,1)S(1)}, bf16[2048,128]{1,0:T(8,128)(2,1)S(1)}, u32[]{:S(2)}, u32[]{:S(2)}) collective-permute-start(bf16[2048,128]{1,0:T(8,128)(2,1)S(1)} %shard_map.285.b0), channel_id=1, source_target_pairs={{0,1},{1,2},{2,3},{3,0},{4,7},{5,4},{6,5},{7,6},{8,9},{9,10},{10,1... | collective-permute-start | bytes 1572872 | tf_op jit(solution)/shard_map/ppermute | solution.py:451
  78.4 11.3 %collective-permute-start.15 = (bf16[2048,128]{1,0:T(8,128)(2,1)S(1)}, bf16[2048,128]{1,0:T(8,128)(2,1)S(1)}, u32[]{:S(2)}, u32[]{:S(2)}) collective-permute-start(bf16[2048,128]{1,0:T(8,128)(2,1)S(1)} %shard_map.285.b0), channel_id=1, source_target_pairs={{0,4},{4,0},{8,12},{12,8},{16,20},{20,16},{24,28},{28,24},{32,36},... | collective-permute-start | bytes 1572872 | tf_op jit(solution)/shard_map/ppermute | solution.py:430
  78.4 11.3 %collective-permute-start.17 = (bf16[2048,128]{1,0:T(8,128)(2,1)S(1)}, bf16[2048,128]{1,0:T(8,128)(2,1)S(1)}, u32[]{:S(2)}, u32[]{:S(2)}) collective-permute-start(bf16[2048,128]{1,0:T(8,128)(2,1)S(1)} %collective-permute-done.12.b1), channel_id=1, source_target_pairs={{4,8},{12,16},{20,24},{28,32},{36,40},{44,48},{52,56},{60,64},{68,... | collective-permute-start | bytes 1572872 | tf_op jit(solution)/shard_map/ppermute | solution.py:436
  81.7 8.0 %collective-permute-start.18 = (bf16[2048,128]{1,0:T(8,128)(2,1)S(1)}, bf16[2048,128]{1,0:T(8,128)(2,1)S(1)}, u32[]{:S(2)}, u32[]{:S(2)}) collective-permute-start(bf16[2048,128]{1,0:T(8,128)(2,1)S(1)} %collective-permute-done.12.b1), channel_id=1, source_target_pairs={{0,4},{4,0},{8,12},{12,8},{16,20},{20,16},{24,28},{28,24},{32,36},... | collective-permute-start | bytes 1572872 | tf_op jit(solution)/shard_map/ppermute | solution.py:430
  81.8 11.0 %collective-permute-start.16 = (bf16[2048,128]{1,0:T(8,128)(2,1)S(1)}, bf16[2048,128]{1,0:T(8,128)(2,1)S(1)}, u32[]{:S(2)}, u32[]{:S(2)}) collective-permute-start(bf16[2048,128]{1,0:T(8,128)(2,1)S(1)} %collective-permute-done.14.b3), channel_id=1, source_target_pairs={{0,3},{1,0},{2,1},{3,2},{4,5},{5,6},{6,7},{7,4},{8,11},{9,8},{10,9... | collective-permute-start | bytes 1572872 | tf_op jit(solution)/shard_map/ppermute | solution.py:451
  85.8 7.0 %collective-permute-start.19 = (bf16[2048,128]{1,0:T(8,128)(2,1)S(1)}, bf16[2048,128]{1,0:T(8,128)(2,1)S(1)}, u32[]{:S(2)}, u32[]{:S(2)}) collective-permute-start(bf16[2048,128]{1,0:T(8,128)(2,1)S(1)} %collective-permute-done.13.b2), channel_id=1, source_target_pairs={{0,4},{4,0},{8,12},{12,8},{16,20},{20,16},{24,28},{28,24},{32,36},... | collective-permute-start | bytes 1572872 | tf_op jit(solution)/shard_map/ppermute | solution.py:430
  (20 other events, 158.8 us)

commit v3 on v2

--- a/solution.py
+++ b/solution.py
@@ -16,6 +16,7 @@
 VMEM = pl.BlockSpec(memory_space=pltpu.VMEM)
 SMEM = pl.BlockSpec(memory_space=pltpu.SMEM)
 ANY = pl.BlockSpec(memory_space=pl.ANY)
+HBM = pl.BlockSpec(memory_space=pltpu.HBM)
 
 
 def params(mib):
@@ -28,6 +29,11 @@
 
 def silu(values):
     half = 0.5 * values
+    return half + half * jnp.tanh(half)
+
+
+def silu_half(values):
+    half = (0.5 * values).astype(BF16)
     return half + half * jnp.tanh(half)
 
 
@@ -59,10 +65,11 @@
         rows[pl.ds((base + edge) * parts, parts), :] = table[pl.ds(start, parts), :]
 
 
-def pipeline(tiles, fetch, work, one, two):
+def pipeline(tiles, fetch, work, one, two, at_pair=lambda pair: None):
     fetch(0, one, 0, 1)
 
     def body(pair, carry):
+        at_pair(pair)
         tile = 2 * pair
         work(tile, one, functools.partial(fetch, tile + 1, two))
         work(tile + 1, two, functools.partial(fetch, jnp.minimum(tile + 2, tiles - 1), one))
@@ -90,20 +97,25 @@
     return dot_rows(pieces(geometry, (0, 1, 0)), pieces(edge_weight, (0, 0, 1)))
 
 
-def copy_kernel(source, target):
-    target[...] = source[...]
+def strip_kernel(fields, kept, strip, sem):
+    copy = pltpu.make_async_copy(fields.at[:, pl.ds(0, strip.shape[1])], strip, sem)
+    copy.start()
+    copy.wait()
 
 
 def take_strip(fields, strip):
     channels = fields.shape[0]
-    block = pl.BlockSpec((channels, strip), lambda i: (0, 0))
-    return pl.pallas_call(
-        copy_kernel,
-        grid=(1,),
-        in_specs=[block],
-        out_specs=block,
-        out_shape=jax.ShapeDtypeStruct((channels, strip), fields.dtype),
-        compiler_params=params(60),
+    return pl.pallas_call(
+        strip_kernel,
+        in_specs=[ANY],
+        out_specs=[ANY, VMEM],
+        out_shape=[
+            jax.ShapeDtypeStruct(fields.shape, fields.dtype),
+            jax.ShapeDtypeStruct((channels, strip), fields.dtype),
+        ],
+        scratch_shapes=[pltpu.SemaphoreType.DMA],
+        input_output_aliases={0: 0},
+        compiler_params=params(16),
         cost_estimate=cost(0, MIB),
     )(fields)
 
@@ -120,36 +132,57 @@
         out_specs=VMEM,
         out_shape=jax.ShapeDtypeStruct((channels, 3 * strip), middle.dtype),
         compiler_params=params(16),
-        cost_estimate=cost(0, MIB),
+        cost_estimate=cost(4 * 10**9, MIB),
     )(left, middle, right)
 
 
-def own_kernel(fields, embed_weight, source_weight, embedded, table):
-    values = silu(dot_rows(fields[...], embed_weight[...])).astype(BF16)
-    embedded[...] = values
-    put_table(table, 0, dot(values, source_weight[...]).astype(BF16).astype(F32))
+OWN_TILE = 512
+
+
+def own_kernel(
+    fields_hbm, embed_hbm, source_hbm, embedded, table, fields, embed_weight, source_weight, sems
+):
+    cells, width = embedded.shape
+    tile = OWN_TILE
+    weights = [
+        pltpu.make_async_copy(embed_hbm, embed_weight, sems.at[0]),
+        pltpu.make_async_copy(source_hbm, source_weight, sems.at[1]),
+    ]
+    weights[0].start()
+    loads = []
+    for i in range(cells // tile):
+        span = pl.ds(i * tile, tile)
+        loads.append(pltpu.make_async_copy(fields_hbm.at[:, span], fields.at[:, span], sems.at[2 + i]))
+        loads[-1].start()
+    weights[1].start()
+    weights[0].wait()
+    for i in range(cells // tile):
+        span = pl.ds(i * tile, tile)
+        loads[i].wait()
+        values = silu(dot_rows(fields[:, span], embed_weight[...])).astype(BF16)
+        embedded[span, :] = values
+        if i == 0:
+            weights[1].wait()
+        put_table(table, i * tile, dot(values, source_weight[...]))
 
 
 def embed_own(fields, embed_weight, source_weight):
     channels, cells = fields.shape
     width = embed_weight.shape[1]
     parts = width // LANES
-    tile = 512
     return pl.pallas_call(
         own_kernel,
-        grid=(cells // tile,),
-        in_specs=[
-            pl.BlockSpec((channels, tile), lambda i: (0, i)),
-            pl.BlockSpec((channels, width), lambda i: (0, 0)),
-            pl.BlockSpec((width, width), lambda i: (0, 0)),
-        ],
-        out_specs=[
-            pl.BlockSpec((tile, width), lambda i: (i, 0)),
-            pl.BlockSpec((tile * parts, LANES), lambda i: (i, 0)),
-        ],
+        in_specs=[ANY] * 3,
+        out_specs=[VMEM, VMEM],
         out_shape=[
             jax.ShapeDtypeStruct((cells, width), BF16),
             jax.ShapeDtypeStruct((cells * parts, LANES), F32),
+        ],
+        scratch_shapes=[
+            pltpu.VMEM(fields.shape, BF16),
+            pltpu.VMEM(embed_weight.shape, BF16),
+            pltpu.VMEM(source_weight.shape, BF16),
+            pltpu.SemaphoreType.DMA((2 + cells // OWN_TILE,)),
         ],
         compiler_params=params(20),
         cost_estimate=cost(2 * cells * width * (width + 256), 8 * MIB),
@@ -171,9 +204,8 @@
     done = cells // parts
     sides = jnp.concatenate([strip_w[...], strip_e[...]], axis=1)
     for strip in (sides, strip_far[...], strip_near[...]):
-        values = silu(dot_rows(strip, embed_weight[...])).astype(BF16)
-        values = dot(values, source_weight[...]).astype(BF16).astype(F32)
-        put_table(table, done, values)
+        values = silu_half(dot_rows(strip, embed_weight[...]))
+        put_table(table, done, dot(values, source_weight[...]))
         done += strip.shape[1]
     total[...] = jnp.zeros_like(total)
     copy.wait()
@@ -192,7 +224,7 @@
         hidden = []
         for part in range(parts):
             here = shift[:, part * LANES : (part + 1) * LANES]
-            hidden.append(silu(rows[pl.ds(part, tile, stride=parts), :] + here).astype(BF16))
+            hidden.append(silu_half(rows[pl.ds(part, tile, stride=parts), :] + here))
             more(1 + part, 8)
         more(5, 8)
         total[...] += dot(picks, jnp.concatenate(hidden, axis=1))
@@ -238,34 +270,46 @@
     )
 
 
+def edge_shift(receivers, geometry, edge_weight, target):
+    ids = lax.broadcasted_iota(jnp.int32, (target.shape[0], receivers.shape[1]), 0)
+    picks = jnp.where(ids == receivers, 1.0, 0.0).astype(BF16)
+    return (dot_rows(picks, target) + geometry_term(geometry, edge_weight)).astype(BF16)
+
+
 def receive_kernel(
-    valid, start, target_weight, state_weight, receivers, geometry, edge_weight, shift, state, target
+    start, target_weight, state_weight, receivers, geometry, edge_weight, shift, state, target
 ):
     @pl.when(pl.program_id(0) == 0)
     def _():
         target[...] = dot(start[...], target_weight[...]).astype(BF16)
         state[...] = dot(start[...], state_weight[...])
 
-    begin = pl.program_id(0) * receivers.shape[1]
-    picks = onehot(receivers[...], begin, valid[0, 0], start.shape[0])
-    shift[...] = (
-        dot_rows(picks, target[...]) + geometry_term(geometry[...], edge_weight[...])
-    ).astype(BF16)
-
-
-def receive(valid, start, target_weight, state_weight, receivers, geometry, edge_weight):
+    shift[...] = edge_shift(receivers[...], geometry[...], edge_weight[...], target[...])
+
+
+def receive_rest_kernel(target, receivers, geometry, edge_weight, shift_before, shift):
+    shift[...] = edge_shift(receivers[...], geometry[...], edge_weight[...], target[...])
+
+
+RECEIVE_TILE = 512
+
+
+def whole(i):
+    return 0, 0
+
+
+def receive(start, target_weight, state_weight, receivers, geometry, edge_weight, tiles):
     nodes, width = start.shape
     edges = receivers.shape[1]
-    tile = 512
-    whole = lambda i: (0, 0)
+    tile = RECEIVE_TILE
+    square = pl.BlockSpec((width, width), whole)
     return pl.pallas_call(
         receive_kernel,
-        grid=(edges // tile,),
+        grid=(tiles,),
         in_specs=[
-            SMEM,
             pl.BlockSpec((nodes, width), whole),
-            pl.BlockSpec((width, width), whole),
-            pl.BlockSpec((width, width), whole),
+            square,
+            square,
             pl.BlockSpec((1, tile), lambda i: (0, i)),
             pl.BlockSpec((geometry.shape[0], tile), lambda i: (0, i)),
             pl.BlockSpec(edge_weight.shape, whole),
@@ -273,15 +317,38 @@
         out_specs=[
             pl.BlockSpec((tile, width), lambda i: (i, 0)),
             pl.BlockSpec((nodes, width), whole),
+            pl.BlockSpec((nodes, width), whole),
         ],
         out_shape=[
             jax.ShapeDtypeStruct((edges, width), BF16),
             jax.ShapeDtypeStruct((nodes, width), F32),
-        ],
-        scratch_shapes=[pltpu.VMEM((nodes, width), BF16)],
+            jax.ShapeDtypeStruct((nodes, width), BF16),
+        ],
         compiler_params=params(20),
-        cost_estimate=cost(2 * edges * width * 2 * width, 8 * MIB),
-    )(valid, start, target_weight, state_weight, receivers, geometry, edge_weight)
+        cost_estimate=cost(2 * tiles * tile * width * 2 * width, 8 * MIB),
+    )(start, target_weight, state_weight, receivers, geometry, edge_weight)
+
+
+def receive_rest(target, receivers, geometry, edge_weight, shift, tiles):
+    nodes, width = target.shape
+    tile = RECEIVE_TILE
+    rest = receivers.shape[1] // tile - tiles
+    return pl.pallas_call(
+        receive_rest_kernel,
+        grid=(rest,),
+        in_specs=[
+            pl.BlockSpec((nodes, width), whole),
+            pl.BlockSpec((1, tile), lambda i: (0, i + tiles)),
+            pl.BlockSpec((geometry.shape[0], tile), lambda i: (0, i + tiles)),
+            pl.BlockSpec(edge_weight.shape, whole),
+            ANY,
+        ],
+        out_specs=pl.BlockSpec((tile, width), lambda i: (i + tiles, 0)),
+        out_shape=jax.ShapeDtypeStruct(shift.shape, BF16),
+        input_output_aliases={4: 0},
+        compiler_params=params(20),
+        cost_estimate=cost(2 * rest * tile * width * 2 * width, 8 * MIB),
+    )(target, receivers, geometry, edge_weight, shift)
 
 
 def fill_table(blocks, table):
@@ -314,7 +381,7 @@
         hidden = []
         for part in range(parts):
             here = shift[span, part * LANES : (part + 1) * LANES].astype(F32)
-            hidden.append(silu(rows[pl.ds(part, tile, stride=parts), :] + here).astype(BF16))
+            hidden.append(silu_half(rows[pl.ds(part, tile, stride=parts), :] + here))
             more(1 + part, 8)
         more(5, 8)
         total[...] += dot(picks, jnp.concatenate(hidden, axis=1))
@@ -352,17 +419,43 @@
     )(index, valid, *blocks, receivers, shift, state, start, *weights)
 
 
-DECODE_TILE = 256
+def target_kernel(embedded, weight, target):
+    target[...] = dot(embedded[...], weight[...]).astype(BF16)
+
+
+def grid_target(embedded, weight):
+    cells, width = embedded.shape
+    tile = 512
+    return pl.pallas_call(
+        target_kernel,
+        grid=(cells // tile,),
+        in_specs=[
+            pl.BlockSpec((tile, width), lambda i: (i, 0)),
+            pl.BlockSpec((width, width), lambda i: (0, 0)),
+        ],
+        out_specs=pl.BlockSpec((tile, width), lambda i: (i, 0)),
+        out_shape=jax.ShapeDtypeStruct((cells, width), BF16),
+        compiler_params=params(16),
+        cost_estimate=cost(2 * cells * width * width, 4 * MIB),
+    )(embedded, weight)
+
+
+DECODE_TILE = 512
 
 
 def decode_kernel(
-    index, b0, b1, b2, b3, b4, b5, b6, b7, b8, embedded, fields, target_weight, hidden_weight,
-    output_weight, prediction, table, one, two,
+    index, b0, b1, b2, b3, b4, b5, b6, b7, b8, target, fields, hidden_weight, output_weight,
+    prediction, table, one, two, result, sems,
 ):
-    cells, width = embedded.shape
+    cells, width = target.shape
     parts = width // LANES
     fill_table((b0, b1, b2, b3, b4, b5, b6, b7, b8), table)
     tile = DECODE_TILE
+    tiles = cells // tile
+    halves = [
+        pltpu.make_async_copy(result.at[:, :, span], prediction.at[:, :, span], sems.at[i])
+        for i, span in enumerate((pl.ds(0, cells // 2), pl.ds(cells // 2, cells // 2)))
+    ]
 
     def fetch(i, rows, piece, pieces_):
         count = tile // pieces_
@@ -372,47 +465,59 @@
 
     def work(i, rows, more):
         begin = pl.multiple_of(i * tile, tile)
-        target = dot(embedded[pl.ds(begin, tile), :], target_weight[...])
+        span = pl.ds(begin, tile)
         summed = []
         for part in range(parts):
-            here = target[:, part * LANES : (part + 1) * LANES]
+            here = target[span, part * LANES : (part + 1) * LANES].astype(F32)
             edge = [
-                silu(rows[pl.ds(k * tile * parts + part, tile, stride=parts), :] + here)
-                .astype(BF16)
-                .astype(F32)
+                silu_half(rows[pl.ds(k * tile * parts + part, tile, stride=parts), :] + here)
                 for k in range(3)
             ]
-            summed.append((edge[0] + edge[1] + edge[2]).astype(BF16))
+            total = edge[0].astype(F32) + edge[1].astype(F32) + edge[2].astype(F32)
+            summed.append(total.astype(BF16))
             more(part, 8)
         more(4, 8)
         more(5, 8)
-        final = silu(dot(jnp.concatenate(summed, axis=1), hidden_weight[...])).astype(BF16)
+        final = silu_half(dot(jnp.concatenate(summed, axis=1), hidden_weight[...]))
         more(6, 8)
         more(7, 8)
         change = lax.dot_general(
             output_weight[...], final, (((1,), (1,)), ((), ())), preferred_element_type=F32
         )
-        result = fields[:, pl.ds(begin, tile)].astype(F32) + change
-        prediction[:, 0, pl.ds(begin, tile)] = result
-
-    pipeline(cells // tile, fetch, work, one, two)
-
-
-def decode(index, blocks, embedded, fields, target_weight, hidden_weight, output_weight):
-    cells, width = embedded.shape
+        result[:, 0, span] = fields[:, span].astype(F32) + change
+
+    def at_pair(pair):
+        @pl.when(pair == tiles // 4)
+        def _():
+            halves[0].start()
+
+    pipeline(tiles, fetch, work, one, two, at_pair)
+    halves[1].start()
+    halves[0].wait()
+    halves[1].wait()
+
+
+def decode(index, blocks, target, fields, hidden_weight, output_weight):
+    cells, width = target.shape
     channels = fields.shape[0]
     parts = width // LANES
     size = blocks[0].shape[0]
     tile = pltpu.VMEM((3 * DECODE_TILE * parts, LANES), F32)
     return pl.pallas_call(
         decode_kernel,
-        in_specs=[SMEM] + [VMEM] * 14,
-        out_specs=VMEM,
+        in_specs=[SMEM] + [VMEM] * 13,
+        out_specs=HBM,
         out_shape=jax.ShapeDtypeStruct((channels, 1, cells), F32),
-        scratch_shapes=[pltpu.VMEM((9 * size, LANES), F32), tile, tile],
+        scratch_shapes=[
+            pltpu.VMEM((9 * size, LANES), F32),
+            tile,
+            tile,
+            pltpu.VMEM((channels, 1, cells), F32),
+            pltpu.SemaphoreType.DMA((2,)),
+        ],
         compiler_params=params(36),
         cost_estimate=cost(2 * cells * width * 3 * width, 12 * MIB),
-    )(index, *blocks, embedded, fields, target_weight, hidden_weight, output_weight)
+    )(index, *blocks, target, fields, hidden_weight, output_weight)
 
 
 def east(values):
@@ -451,15 +556,16 @@
     return lax.ppermute(values, ("lat", "lon"), pairs)
 
 
-def swap_blocks(block):
+def swap_blocks(block, beside=tuple):
     fore = lon_shift(block, -1)
     away = far(block)
     close = near(block)
-    again, fore = lax.optimization_barrier((block, fore))
+    again, fore, work = lax.optimization_barrier((block, fore, beside()))
     aft = lon_shift(again, 1)
     corner_fore = lon_shift(away, -1)
     corner_aft = far(fore)
-    return block, fore, aft, away, close, corner_fore, corner_aft, near(fore), near(aft)
+    blocks = block, fore, aft, away, close, corner_fore, corner_aft, near(fore), near(aft)
+    return blocks, work
 
 
 def slots(block, same, away, close):
@@ -524,7 +630,8 @@
     cells, nodes, width = fields.shape[1], static.shape[0], static.shape[1]
     parts = width // LANES
     strip = cells // 8
-    strips = swap_strips(take_strip(fields, strip))
+    fields, own_strip = take_strip(fields, strip)
+    strips = swap_strips(own_strip)
     encode_index = grid_index(encode_senders[0, 0], cells, strip, parts)
     process_index = mesh_index(mesh_senders[0, 0], nodes, parts)
     decode_index = mesh_index(decode_senders[0, 0].reshape(-1), nodes, parts)
@@ -548,30 +655,28 @@
         ),
         static,
     )
-    blocks = swap_blocks(table)
-    shift, state = receive(
-        mesh_valid,
-        start,
-        process_target,
-        update_state,
-        mesh_receivers[0],
-        mesh_geometry[0, 0],
-        process_edge,
+    receivers, geometry = mesh_receivers[0], mesh_geometry[0, 0]
+    tiles = receivers.shape[1] // RECEIVE_TILE * 5 // 8
+    blocks, (shift, state, target) = swap_blocks(
+        table,
+        lambda: receive(
+            start, process_target, update_state, receivers, geometry, process_edge, tiles
+        ),
     )
+    shift = receive_rest(target, receivers, geometry, process_edge, shift, tiles)
     table = process(
         process_index,
         mesh_valid,
         blocks,
-        mesh_receivers[0],
+        receivers,
         shift,
         state,
         start,
         (process_second, update_message, update_out, process_gain[None], decode_source),
     )
-    blocks = swap_blocks(table)
-    prediction = decode(
-        decode_index, blocks, embedded, fields, decode_target, decode_hidden, output_weight.T
-    )
+    blocks, _ = swap_blocks(table)
+    target = grid_target(embedded, decode_target)
+    prediction = decode(decode_index, blocks, target, fields, decode_hidden, output_weight.T)
     return prediction.transpose(1, 2, 0)[None]
 
 

time: 107 us -> 101 us (0.944)
  local copies, waits for them, and re-layouts: 4.22 us -> 1.36 us
  Pallas kernels: 42.9 us -> 40.6 us
  waiting for transfers between devices: 18.9 us -> 16.6 us
  starting transfers between devices: 38 us -> 40.1 us
    ppermute x7, starting transfers between devices: 9.13 us -> 15.6 us  [near(): return lax.ppermute(values, 'lat', [(i, i ^ 1) for i in range(count)])]
    ppermute x5, starting transfers between devices: 21.7 us -> 16.8 us  [far(): return lax.ppermute(values, 'lat', ups + [(b, a) for a, b in ups])]
    unnamed x64 -> x55, local copies, waits for them, and re-layouts: 4.22 us -> 1.36 us
    ppermute x6, waiting for transfers between devices: 16.6 us -> 14 us  [lon_shift(): return lax.ppermute(values, ('lat', 'lon'), pairs)]
    pallas_call x4 -> x6, Pallas kernels: 23.7 us -> 22 us  [the longest x1 10.9 us: decode(): pl.pallas_call(decode_kernel, in_specs=[SMEM] + [VMEM] * 13, out_specs=HB...]
  transfers between devices with their start and end apart: 20 -> 20, of which waited for: 6 -> 6; matrix products, arithmetic and copies ran while one was open for 0% -> 0% of each run, Pallas kernels for 8% -> 11%
where the time goes in v3:
time: 101 us
  Pallas kernels  40.6 us (40%)
  starting transfers between devices  40.1 us (40%)
  waiting for transfers between devices  16.6 us (16%)
  between operations  2.07 us (2%)
  local copies, waits for them, and re-layouts  1.36 us (1%)
    ppermute x5, starting transfers between devices, far(): return lax.ppermute(values, 'lat', ups + [(b, a) for a, b in ups])  16.8 us
    ppermute x7, starting transfers between devices, near(): return lax.ppermute(values, 'lat', [(i, i ^ 1) for i in range(count)])  15.6 us
    ppermute x6, waiting for transfers between devices, lon_shift(): return lax.ppermute(values, ('lat', 'lon'), pairs)  14 us
    pallas_call x1, Pallas kernels, decode(): pl.pallas_call(decode_kernel, in_specs=[SMEM] + [VMEM] * 13, out_specs=HB...  10.9 us
    pallas_call x1, Pallas kernels, encode(): pl.pallas_call(encode_kernel, in_specs=[SMEM] * 2 + [VMEM] * 4 + [ANY] +...  9.61 us
    pallas_call x1, Pallas kernels, process(): pl.pallas_call(process_kernel, in_specs=[SMEM] * 2 + [VMEM] * 18, out_spe...  8.92 us
    ppermute x6, starting transfers between devices, lon_shift(): return lax.ppermute(values, ('lat', 'lon'), pairs)  4.87 us
    pallas_call x1, Pallas kernels, receive(): pl.pallas_call(receive_kernel, grid=(tiles,), in_specs=[pl.BlockSpec((nod...  3.85 us
  transfers between devices with their start and end apart: 20, of which 6 were waited for; matrix products, arithmetic and copies ran while one was open for 0% of the time, Pallas kernels for 11%

profile of v3, /device:TPU:3, one launch (start us, length us, event | category | flops | bytes accessed | tf_op | source)
XLA Modules:
  0.0 100.9 jit_solution(4360833849210313430)
XLA Ops:
  0.0 1.2 %copy.39 = bf16[1,1,2048,227]{2,3,1,0:T(8,128)(2,1)S(1)} copy(bf16[1,1,2048,227]{2,3,1,0:T(8,128)(2,1)} %param.30) | data formatting | bytes 1859584
  1.2 1.4 %collective-permute-start = (bf16[227,256]{1,0:T(8,128)(2,1)S(1)}, bf16[227,256]{1,0:T(8,128)(2,1)S(1)}, u32[]{:S(2)}, u32[]{:S(2)}) collective-permute-start(bf16[227,256]{1,0:T(8,128)(2,1)S(1)} %get-tuple-element.21.middle), channel_id=1, source_target_pairs={{0,1},{1,2},{2,3},{3,0},{4,5},{5,6},{6,7},{7,4},{8,9},{9,10},{10,1... | collective-permute-start | bytes 348680 | tf_op jit(solution)/shard_map/ppermute | solution.py:525
  2.6 1.5 %collective-permute-start.1 = (bf16[227,256]{1,0:T(8,128)(2,1)S(1)}, bf16[227,256]{1,0:T(8,128)(2,1)S(1)}, u32[]{:S(2)}, u32[]{:S(2)}) collective-permute-start(bf16[227,256]{1,0:T(8,128)(2,1)S(1)} %get-tuple-element.21.middle), channel_id=1, source_target_pairs={{1,0},{2,1},{3,2},{0,3},{5,4},{6,5},{7,6},{4,7},{9,8},{10,9},{11,1... | collective-permute-start | bytes 348680 | tf_op jit(solution)/shard_map/ppermute | solution.py:530
  4.8 2.0 %collective-permute-done.left.strip_w = bf16[227,256]{1,0:T(8,128)(2,1)S(1)} collective-permute-done((bf16[227,256]{1,0:T(8,128)(2,1)S(1)}, bf16[227,256]{1,0:T(8,128)(2,1)S(1)}, u32[]{:S(2)}, u32[]{:S(2)}) %collective-permute-start) | collective-permute-done | bytes 116256 | tf_op jit(solution)/shard_map/ppermute | solution.py:525
  6.9 5.2 %collective-permute-start.2 = (bf16[227,768]{1,0:T(8,128)(2,1)S(1)}, bf16[227,768]{1,0:T(8,128)(2,1)S(1)}, u32[]{:S(2)}, u32[]{:S(2)}) collective-permute-start(bf16[227,768]{1,0:T(8,128)(2,1)S(1)} %shard_map.281), channel_id=1, source_target_pairs={{4,8},{12,16},{20,24},{28,32},{36,40},{44,48},{52,56},{60,64},{68,... | collective-permute-start | bytes 1046024 | tf_op jit(solution)/shard_map/ppermute | solution.py:541
  12.1 1.0 %collective-permute-start.3 = (bf16[227,768]{1,0:T(8,128)(2,1)S(1)}, bf16[227,768]{1,0:T(8,128)(2,1)S(1)}, u32[]{:S(2)}, u32[]{:S(2)}) collective-permute-start(bf16[227,768]{1,0:T(8,128)(2,1)S(1)} %shard_map.281), channel_id=1, source_target_pairs={{0,4},{4,0},{8,12},{12,8},{16,20},{20,16},{24,28},{28,24},{32,36},... | collective-permute-start | bytes 1046024 | tf_op jit(solution)/shard_map/ppermute | solution.py:535
  13.2 3.5 %shard_map.282 = (bf16[2048,512]{1,0:T(8,128)(2,1)S(1)}, f32[8192,128]{1,0:T(8,128)S(1)}) custom-call(bf16[227,2048]{1,0:T(8,128)(2,1)S(1)} %get-tuple-element.22.fields_hbm.fields, bf16[227,512]{1,0:T(8,128)(2,1)S(1)} %copy-done.17, bf16[512,512]{1,0:T(8,128)(2,1)S(1)} %copy-done.4), custom_call_target="tpu_custom_call" | custom-call | flops 1610612736 | bytes 8388608 | tf_op jit(solution)/shard_map/pallas_call | solution.py:173
  16.8 0.7 collective-permute-done.2.strip_far
  17.6 9.6 %shard_map.283 = (bf16[512,512]{1,0:T(8,128)(2,1)S(1)}, bf16[2048,128]{1,0:T(8,128)(2,1)S(1)}) custom-call(s32[3072]{0:T(1024)S(1)} %fusion.21.index, s32[1,1]{1,0:T(1,128)S(6)} %copy.37.valid, bf16[227,256]{1,0:T(8,128)(2,1)S(1)} %collective-permute-done.left.strip_w, bf16[227,256]{1,0:T(8,128)(2,1)S(1)} %collective-permute-done.1.right.strip_e, ...), custom_call_target="tpu_custom_call" | custom-call | flops 3221225472 | bytes 10485760 | tf_op jit(solution)/shard_map/pallas_call | solution.py:249
  27.2 1.4 %collective-permute-start.4 = (bf16[2048,128]{1,0:T(8,128)(2,1)S(1)}, bf16[2048,128]{1,0:T(8,128)(2,1)S(1)}, u32[]{:S(2)}, u32[]{:S(2)}) collective-permute-start(bf16[2048,128]{1,0:T(8,128)(2,1)S(1)} %get-tuple-element.30.b0), channel_id=1, source_target_pairs={{0,3},{1,0},{2,1},{3,2},{4,5},{5,6},{6,7},{7,4},{8,11},{9,8},{10,9... | collective-permute-start | bytes 1572872 | tf_op jit(solution)/shard_map/ppermute | solution.py:556
  28.6 4.9 %collective-permute-start.6 = (bf16[2048,128]{1,0:T(8,128)(2,1)S(1)}, bf16[2048,128]{1,0:T(8,128)(2,1)S(1)}, u32[]{:S(2)}, u32[]{:S(2)}) collective-permute-start(bf16[2048,128]{1,0:T(8,128)(2,1)S(1)} %get-tuple-element.30.b0), channel_id=1, source_target_pairs={{4,8},{12,16},{20,24},{28,32},{36,40},{44,48},{52,56},{60,64},{68,... | collective-permute-start | bytes 1572872 | tf_op jit(solution)/shard_map/ppermute | solution.py:541
  33.6 3.8 %shard_map.284 = (bf16[4096,512]{1,0:T(8,128)(2,1)S(1)}, f32[512,512]{1,0:T(8,128)S(1)}, bf16[512,512]{1,0:T(8,128)(2,1)S(1)}) custom-call(bf16[512,512]{1,0:T(8,128)(2,1)S(1)} %get-tuple-element.25.start, bf16[512,512]{1,0:T(8,128)(2,1)S(1)} %copy-done.10, bf16[512,512]{1,0:T(8,128)(2,1)S(1)} %copy-done.11, s32[1,4096]{1,0:T(1,128)S(1)} %bitcast.22, ...), custom_call_target="tpu_custom_call" | custom-call | flops 2684354560 | bytes 8388608 | tf_op jit(solution)/shard_map/pallas_call | solution.py:306
  37.4 0.8 collective-permute-start.5
  38.2 1.9 %collective-permute-start.7 = (bf16[2048,128]{1,0:T(8,128)(2,1)S(1)}, bf16[2048,128]{1,0:T(8,128)(2,1)S(1)}, u32[]{:S(2)}, u32[]{:S(2)}) collective-permute-start(bf16[2048,128]{1,0:T(8,128)(2,1)S(1)} %get-tuple-element.30.b0), channel_id=1, source_target_pairs={{0,4},{4,0},{8,12},{12,8},{16,20},{20,16},{24,28},{28,24},{32,36},... | collective-permute-start | bytes 1572872 | tf_op jit(solution)/shard_map/ppermute | solution.py:535
  40.1 1.9 %collective-permute-start.9 = (bf16[2048,128]{1,0:T(8,128)(2,1)S(1)}, bf16[2048,128]{1,0:T(8,128)(2,1)S(1)}, u32[]{:S(2)}, u32[]{:S(2)}) collective-permute-start(bf16[2048,128]{1,0:T(8,128)(2,1)S(1)} %collective-permute-done.4.b1), channel_id=1, source_target_pairs={{4,8},{12,16},{20,24},{28,32},{36,40},{44,48},{52,56},{60,64},{68,... | collective-permute-start | bytes 1572872 | tf_op jit(solution)/shard_map/ppermute | solution.py:541
  42.0 1.1 %collective-permute-start.8 = (bf16[2048,128]{1,0:T(8,128)(2,1)S(1)}, bf16[2048,128]{1,0:T(8,128)(2,1)S(1)}, u32[]{:S(2)}, u32[]{:S(2)}) collective-permute-start(bf16[2048,128]{1,0:T(8,128)(2,1)S(1)} %collective-permute-done.6.b3), channel_id=1, source_target_pairs={{0,3},{1,0},{2,1},{3,2},{4,5},{5,6},{6,7},{7,4},{8,11},{9,8},{10,9... | collective-permute-start | bytes 1572872 | tf_op jit(solution)/shard_map/ppermute | solution.py:556
  43.1 2.7 %collective-permute-done.5.b2 = bf16[2048,128]{1,0:T(8,128)(2,1)S(1)} collective-permute-done((bf16[2048,128]{1,0:T(8,128)(2,1)S(1)}, bf16[2048,128]{1,0:T(8,128)(2,1)S(1)}, u32[]{:S(2)}, u32[]{:S(2)}) %collective-permute-start.5) | collective-permute-done | bytes 524320 | tf_op jit(solution)/shard_map/ppermute | solution.py:556
  45.8 7.1 %collective-permute-start.11 = (bf16[2048,128]{1,0:T(8,128)(2,1)S(1)}, bf16[2048,128]{1,0:T(8,128)(2,1)S(1)}, u32[]{:S(2)}, u32[]{:S(2)}) collective-permute-start(bf16[2048,128]{1,0:T(8,128)(2,1)S(1)} %collective-permute-done.5.b2), channel_id=1, source_target_pairs={{0,4},{4,0},{8,12},{12,8},{16,20},{20,16},{24,28},{28,24},{32,36},... | collective-permute-start | bytes 1572872 | tf_op jit(solution)/shard_map/ppermute | solution.py:535
  53.8 1.9 %shard_map.285.shift = bf16[4096,512]{1,0:T(8,128)(2,1)S(1)} custom-call(bf16[512,512]{1,0:T(8,128)(2,1)S(1)} %get-tuple-element.31.target, s32[1,4096]{1,0:T(1,128)S(1)} %bitcast.23, f32[4,4096]{1,0:T(4,128)S(1)} %bitcast.21, f32[4,512]{1,0:T(4,128)S(1)} %copy-done.3, ...), custom_call_target="tpu_custom_call", output_to_operand_aliasing={{}: (4, {})} | custom-call | flops 1610612736 | bytes 8388608 | tf_op jit(solution)/shard_map/pallas_call | solution.py:336
  55.8 8.9 %shard_map.286.b0 = bf16[2048,128]{1,0:T(8,128)(2,1)S(1)} custom-call(s32[4096]{0:T(1024)S(1)} %fusion.14.index, s32[1,1]{1,0:T(1,128)S(6)} %copy.38.valid, bf16[2048,128]{1,0:T(8,128)(2,1)S(1)} %get-tuple-element.30.b0, bf16[2048,128]{1,0:T(8,128)(2,1)S(1)} %collective-permute-done.4.b1, bf16[2048,128]{1,0:T(8,128)(2,1)S(1)} %collective-permute-done.5.b2, ...), custom_call_target="tpu_custom_call" | custom-call | flops 4294967296 | bytes 12582912 | tf_op jit(solution)/shard_map/pallas_call | solution.py:405
  64.8 2.8 %collective-permute-start.14 = (bf16[2048,128]{1,0:T(8,128)(2,1)S(1)}, bf16[2048,128]{1,0:T(8,128)(2,1)S(1)}, u32[]{:S(2)}, u32[]{:S(2)}) collective-permute-start(bf16[2048,128]{1,0:T(8,128)(2,1)S(1)} %shard_map.286.b0), channel_id=1, source_target_pairs={{4,8},{12,16},{20,24},{28,32},{36,40},{44,48},{52,56},{60,64},{68,... | collective-permute-start | bytes 1572872 | tf_op jit(solution)/shard_map/ppermute | solution.py:541
  67.7 6.7 %collective-permute-done.12.b1 = bf16[2048,128]{1,0:T(8,128)(2,1)S(1)} collective-permute-done((bf16[2048,128]{1,0:T(8,128)(2,1)S(1)}, bf16[2048,128]{1,0:T(8,128)(2,1)S(1)}, u32[]{:S(2)}, u32[]{:S(2)}) %collective-permute-start.12) | collective-permute-done | bytes 524320 | tf_op jit(solution)/shard_map/ppermute | solution.py:556
  74.4 1.0 collective-permute-start.13
  75.3 1.9 %collective-permute-start.17 = (bf16[2048,128]{1,0:T(8,128)(2,1)S(1)}, bf16[2048,128]{1,0:T(8,128)(2,1)S(1)}, u32[]{:S(2)}, u32[]{:S(2)}) collective-permute-start(bf16[2048,128]{1,0:T(8,128)(2,1)S(1)} %collective-permute-done.12.b1), channel_id=1, source_target_pairs={{4,8},{12,16},{20,24},{28,32},{36,40},{44,48},{52,56},{60,64},{68,... | collective-permute-start | bytes 1572872 | tf_op jit(solution)/shard_map/ppermute | solution.py:541
  77.3 0.6 collective-permute-start.18
  77.9 0.6 collective-permute-start.16
  78.5 4.2 %collective-permute-done.13.b2 = bf16[2048,128]{1,0:T(8,128)(2,1)S(1)} collective-permute-done((bf16[2048,128]{1,0:T(8,128)(2,1)S(1)}, bf16[2048,128]{1,0:T(8,128)(2,1)S(1)}, u32[]{:S(2)}, u32[]{:S(2)}) %collective-permute-start.13) | collective-permute-done | bytes 524320 | tf_op jit(solution)/shard_map/ppermute | solution.py:556
  82.7 4.9 %collective-permute-start.19 = (bf16[2048,128]{1,0:T(8,128)(2,1)S(1)}, bf16[2048,128]{1,0:T(8,128)(2,1)S(1)}, u32[]{:S(2)}, u32[]{:S(2)}) collective-permute-start(bf16[2048,128]{1,0:T(8,128)(2,1)S(1)} %collective-permute-done.13.b2), channel_id=1, source_target_pairs={{0,4},{4,0},{8,12},{12,8},{16,20},{20,16},{24,28},{28,24},{32,36},... | collective-permute-start | bytes 1572872 | tf_op jit(solution)/shard_map/ppermute | solution.py:535
  87.6 1.8 %shard_map.287.target = bf16[2048,512]{1,0:T(8,128)(2,1)S(1)} custom-call(bf16[2048,512]{1,0:T(8,128)(2,1)S(1)} %get-tuple-element.36.embedded, bf16[512,512]{1,0:T(8,128)(2,1)S(1)} %copy-done), custom_call_target="tpu_custom_call" | custom-call | flops 1073741824 | bytes 4194304 | tf_op jit(solution)/shard_map/pallas_call | solution.py:429
  89.3 0.1 fusion.5.index
  89.5 0.3 collective-permute-done.16.b5
  89.8 10.9 %shard_map.288 = f32[227,1,2048]{2,1,0:T(1,128)} custom-call(s32[6144]{0:T(1024)S(1)} %fusion.5.index, bf16[2048,128]{1,0:T(8,128)(2,1)S(1)} %shard_map.286.b0, bf16[2048,128]{1,0:T(8,128)(2,1)S(1)} %collective-permute-done.12.b1, bf16[2048,128]{1,0:T(8,128)(2,1)S(1)} %collective-permute-done.13.b2, bf16[2048,128]{1,0:T(8,128)(2,1)S(1)} %collective-permute-done.14.b3, ...), custom_call_target="tpu_custom_call" | custom-call | flops 3221225472 | bytes 12582912 | tf_op jit(solution)/shard_map/pallas_call | solution.py:506
  (75 shorter events, 0.5 us)
Async XLA Ops:
  1.2 5.5 %collective-permute-start = (bf16[227,256]{1,0:T(8,128)(2,1)S(1)}, bf16[227,256]{1,0:T(8,128)(2,1)S(1)}, u32[]{:S(2)}, u32[]{:S(2)}) collective-permute-start(bf16[227,256]{1,0:T(8,128)(2,1)S(1)} %get-tuple-element.21.middle), channel_id=1, source_target_pairs={{0,1},{1,2},{2,3},{3,0},{4,5},{5,6},{6,7},{7,4},{8,9},{9,10},{10,1... | collective-permute-start | bytes 348680 | tf_op jit(solution)/shard_map/ppermute | solution.py:525
  2.6 4.2 %collective-permute-start.1 = (bf16[227,256]{1,0:T(8,128)(2,1)S(1)}, bf16[227,256]{1,0:T(8,128)(2,1)S(1)}, u32[]{:S(2)}, u32[]{:S(2)}) collective-permute-start(bf16[227,256]{1,0:T(8,128)(2,1)S(1)} %get-tuple-element.21.middle), channel_id=1, source_target_pairs={{1,0},{2,1},{3,2},{0,3},{5,4},{6,5},{7,6},{4,7},{9,8},{10,9},{11,1... | collective-permute-start | bytes 348680 | tf_op jit(solution)/shard_map/ppermute | solution.py:530
  6.8 10.7 %copy-start.5 = (bf16[512,512]{1,0:T(8,128)(2,1)S(1)}, bf16[512,512]{1,0:T(8,128)(2,1)}, u32[]{:S(2)}) copy-start(bf16[512,512]{1,0:T(8,128)(2,1)} %second.2) | copy-start | bytes 1572868
  6.8 10.7 %copy-start.6 = (bf16[512,512]{1,0:T(8,128)(2,1)S(1)}, bf16[512,512]{1,0:T(8,128)(2,1)}, u32[]{:S(2)}) copy-start(bf16[512,512]{1,0:T(8,128)(2,1)} %first_weight.1) | copy-start | bytes 1572868
  6.9 10.6 %collective-permute-start.2 = (bf16[227,768]{1,0:T(8,128)(2,1)S(1)}, bf16[227,768]{1,0:T(8,128)(2,1)S(1)}, u32[]{:S(2)}, u32[]{:S(2)}) collective-permute-start(bf16[227,768]{1,0:T(8,128)(2,1)S(1)} %shard_map.281), channel_id=1, source_target_pairs={{4,8},{12,16},{20,24},{28,32},{36,40},{44,48},{52,56},{60,64},{68,... | collective-permute-start | bytes 1046024 | tf_op jit(solution)/shard_map/ppermute | solution.py:541
  12.1 5.3 %collective-permute-start.3 = (bf16[227,768]{1,0:T(8,128)(2,1)S(1)}, bf16[227,768]{1,0:T(8,128)(2,1)S(1)}, u32[]{:S(2)}, u32[]{:S(2)}) collective-permute-start(bf16[227,768]{1,0:T(8,128)(2,1)S(1)} %shard_map.281), channel_id=1, source_target_pairs={{0,4},{4,0},{8,12},{12,8},{16,20},{20,16},{24,28},{28,24},{32,36},... | collective-permute-start | bytes 1046024 | tf_op jit(solution)/shard_map/ppermute | solution.py:535
  17.5 16.0 %copy-start.1 = (f32[1,1,4,4096]{3,2,1,0:T(4,128)S(1)}, f32[1,1,4,4096]{3,2,1,0:T(4,128)}, u32[]{:S(2)}) copy-start(f32[1,1,4,4096]{3,2,1,0:T(4,128)} %param.38) | copy-start | bytes 196612
  17.6 16.0 %copy-start.2 = (s32[1,1,4096]{2,1,0:T(1,128)S(1)}, s32[1,1,4096]{2,1,0:T(1,128)}, u32[]{:S(2)}) copy-start(s32[1,1,4096]{2,1,0:T(1,128)} %param.37) | copy-start | bytes 49156
  17.6 16.0 %copy-start.3 = (f32[4,512]{1,0:T(4,128)S(1)}, f32[4,512]{1,0:T(4,128)}, u32[]{:S(2)}) copy-start(f32[4,512]{1,0:T(4,128)} %edge_weight.5) | copy-start | bytes 24580
  17.6 16.0 %copy-start.10 = (bf16[512,512]{1,0:T(8,128)(2,1)S(1)}, bf16[512,512]{1,0:T(8,128)(2,1)}, u32[]{:S(2)}) copy-start(bf16[512,512]{1,0:T(8,128)(2,1)} %target_weight.1) | copy-start | bytes 1572868
  17.6 16.0 %copy-start.11 = (bf16[512,512]{1,0:T(8,128)(2,1)S(1)}, bf16[512,512]{1,0:T(8,128)(2,1)}, u32[]{:S(2)}) copy-start(bf16[512,512]{1,0:T(8,128)(2,1)} %state_weight.1) | copy-start | bytes 1572868
  27.2 10.2 %collective-permute-start.4 = (bf16[2048,128]{1,0:T(8,128)(2,1)S(1)}, bf16[2048,128]{1,0:T(8,128)(2,1)S(1)}, u32[]{:S(2)}, u32[]{:S(2)}) collective-permute-start(bf16[2048,128]{1,0:T(8,128)(2,1)S(1)} %get-tuple-element.30.b0), channel_id=1, source_target_pairs={{0,3},{1,0},{2,1},{3,2},{4,5},{5,6},{6,7},{7,4},{8,11},{9,8},{10,9... | collective-permute-start | bytes 1572872 | tf_op jit(solution)/shard_map/ppermute | solution.py:556
  28.6 13.5 %collective-permute-start.6 = (bf16[2048,128]{1,0:T(8,128)(2,1)S(1)}, bf16[2048,128]{1,0:T(8,128)(2,1)S(1)}, u32[]{:S(2)}, u32[]{:S(2)}) collective-permute-start(bf16[2048,128]{1,0:T(8,128)(2,1)S(1)} %get-tuple-element.30.b0), channel_id=1, source_target_pairs={{4,8},{12,16},{20,24},{28,32},{36,40},{44,48},{52,56},{60,64},{68,... | collective-permute-start | bytes 1572872 | tf_op jit(solution)/shard_map/ppermute | solution.py:541
  33.6 20.1 %copy-start.25 = (s32[1,1,4096]{2,1,0:T(1,128)S(1)}, s32[1,1,4096]{2,1,0:T(1,128)}, u32[]{:S(2)}) copy-start(s32[1,1,4096]{2,1,0:T(1,128)} %param.36) | copy-start | bytes 49156
  37.4 8.4 %collective-permute-start.5 = (bf16[2048,128]{1,0:T(8,128)(2,1)S(1)}, bf16[2048,128]{1,0:T(8,128)(2,1)S(1)}, u32[]{:S(2)}, u32[]{:S(2)}) collective-permute-start(bf16[2048,128]{1,0:T(8,128)(2,1)S(1)} %get-tuple-element.30.b0), channel_id=1, source_target_pairs={{0,1},{1,2},{2,3},{3,0},{4,7},{5,4},{6,5},{7,6},{8,9},{9,10},{10,1... | collective-permute-start | bytes 1572872 | tf_op jit(solution)/shard_map/ppermute | solution.py:556
  38.2 17.5 %collective-permute-start.7 = (bf16[2048,128]{1,0:T(8,128)(2,1)S(1)}, bf16[2048,128]{1,0:T(8,128)(2,1)S(1)}, u32[]{:S(2)}, u32[]{:S(2)}) collective-permute-start(bf16[2048,128]{1,0:T(8,128)(2,1)S(1)} %get-tuple-element.30.b0), channel_id=1, source_target_pairs={{0,4},{4,0},{8,12},{12,8},{16,20},{20,16},{24,28},{28,24},{32,36},... | collective-permute-start | bytes 1572872 | tf_op jit(solution)/shard_map/ppermute | solution.py:535
  40.1 15.6 %collective-permute-start.10 = (bf16[2048,128]{1,0:T(8,128)(2,1)S(1)}, bf16[2048,128]{1,0:T(8,128)(2,1)S(1)}, u32[]{:S(2)}, u32[]{:S(2)}) collective-permute-start(bf16[2048,128]{1,0:T(8,128)(2,1)S(1)} %collective-permute-done.4.b1), channel_id=1, source_target_pairs={{0,4},{4,0},{8,12},{12,8},{16,20},{20,16},{24,28},{28,24},{32,36},... | collective-permute-start | bytes 1572872 | tf_op jit(solution)/shard_map/ppermute | solution.py:535
  40.1 15.6 %collective-permute-start.9 = (bf16[2048,128]{1,0:T(8,128)(2,1)S(1)}, bf16[2048,128]{1,0:T(8,128)(2,1)S(1)}, u32[]{:S(2)}, u32[]{:S(2)}) collective-permute-start(bf16[2048,128]{1,0:T(8,128)(2,1)S(1)} %collective-permute-done.4.b1), channel_id=1, source_target_pairs={{4,8},{12,16},{20,24},{28,32},{36,40},{44,48},{52,56},{60,64},{68,... | collective-permute-start | bytes 1572872 | tf_op jit(solution)/shard_map/ppermute | solution.py:541
  42.0 13.7 %collective-permute-start.8 = (bf16[2048,128]{1,0:T(8,128)(2,1)S(1)}, bf16[2048,128]{1,0:T(8,128)(2,1)S(1)}, u32[]{:S(2)}, u32[]{:S(2)}) collective-permute-start(bf16[2048,128]{1,0:T(8,128)(2,1)S(1)} %collective-permute-done.6.b3), channel_id=1, source_target_pairs={{0,3},{1,0},{2,1},{3,2},{4,5},{5,6},{6,7},{7,4},{8,11},{9,8},{10,9... | collective-permute-start | bytes 1572872 | tf_op jit(solution)/shard_map/ppermute | solution.py:556
  45.8 9.9 %collective-permute-start.11 = (bf16[2048,128]{1,0:T(8,128)(2,1)S(1)}, bf16[2048,128]{1,0:T(8,128)(2,1)S(1)}, u32[]{:S(2)}, u32[]{:S(2)}) collective-permute-start(bf16[2048,128]{1,0:T(8,128)(2,1)S(1)} %collective-permute-done.5.b2), channel_id=1, source_target_pairs={{0,4},{4,0},{8,12},{12,8},{16,20},{20,16},{24,28},{28,24},{32,36},... | collective-permute-start | bytes 1572872 | tf_op jit(solution)/shard_map/ppermute | solution.py:535
  55.8 31.8 %copy-start = (bf16[512,512]{1,0:T(8,128)(2,1)S(1)}, bf16[512,512]{1,0:T(8,128)(2,1)}, u32[]{:S(2)}) copy-start(bf16[512,512]{1,0:T(8,128)(2,1)} %weight.1) | copy-start | bytes 1572868
  64.7 24.6 %copy-start.24 = (s32[1,1,3,2048]{3,1,2,0:T(1,128)S(1)}, s32[1,1,3,2048]{3,1,2,0:T(1,128)}, u32[]{:S(2)}) copy-start(s32[1,1,3,2048]{3,1,2,0:T(1,128)} %param.40) | copy-start | bytes 73732
  64.7 25.1 %copy-start.16 = (bf16[512,512]{1,0:T(8,128)(2,1)S(1)}, bf16[512,512]{1,0:T(8,128)(2,1)}, u32[]{:S(2)}) copy-start(bf16[512,512]{1,0:T(8,128)(2,1)} %hidden_weight.1) | copy-start | bytes 1572868
  64.7 25.1 %copy-start.18 = (bf16[512,227]{0,1:T(8,128)(2,1)S(1)}, bf16[512,227]{0,1:T(8,128)(2,1)}, u32[]{:S(2)}) copy-start(bf16[512,227]{0,1:T(8,128)(2,1)} %param.59) | copy-start | bytes 697348
  64.7 9.6 %collective-permute-start.12 = (bf16[2048,128]{1,0:T(8,128)(2,1)S(1)}, bf16[2048,128]{1,0:T(8,128)(2,1)S(1)}, u32[]{:S(2)}, u32[]{:S(2)}) collective-permute-start(bf16[2048,128]{1,0:T(8,128)(2,1)S(1)} %shard_map.286.b0), channel_id=1, source_target_pairs={{0,3},{1,0},{2,1},{3,2},{4,5},{5,6},{6,7},{7,4},{8,11},{9,8},{10,9... | collective-permute-start | bytes 1572872 | tf_op jit(solution)/shard_map/ppermute | solution.py:556
  64.8 13.0 %collective-permute-start.14 = (bf16[2048,128]{1,0:T(8,128)(2,1)S(1)}, bf16[2048,128]{1,0:T(8,128)(2,1)S(1)}, u32[]{:S(2)}, u32[]{:S(2)}) collective-permute-start(bf16[2048,128]{1,0:T(8,128)(2,1)S(1)} %shard_map.286.b0), channel_id=1, source_target_pairs={{4,8},{12,16},{20,24},{28,32},{36,40},{44,48},{52,56},{60,64},{68,... | collective-permute-start | bytes 1572872 | tf_op jit(solution)/shard_map/ppermute | solution.py:541
  74.4 8.3 %collective-permute-start.13 = (bf16[2048,128]{1,0:T(8,128)(2,1)S(1)}, bf16[2048,128]{1,0:T(8,128)(2,1)S(1)}, u32[]{:S(2)}, u32[]{:S(2)}) collective-permute-start(bf16[2048,128]{1,0:T(8,128)(2,1)S(1)} %shard_map.286.b0), channel_id=1, source_target_pairs={{0,1},{1,2},{2,3},{3,0},{4,7},{5,4},{6,5},{7,6},{8,9},{9,10},{10,1... | collective-permute-start | bytes 1572872 | tf_op jit(solution)/shard_map/ppermute | solution.py:556
  75.3 14.1 %collective-permute-start.15 = (bf16[2048,128]{1,0:T(8,128)(2,1)S(1)}, bf16[2048,128]{1,0:T(8,128)(2,1)S(1)}, u32[]{:S(2)}, u32[]{:S(2)}) collective-permute-start(bf16[2048,128]{1,0:T(8,128)(2,1)S(1)} %shard_map.286.b0), channel_id=1, source_target_pairs={{0,4},{4,0},{8,12},{12,8},{16,20},{20,16},{24,28},{28,24},{32,36},... | collective-permute-start | bytes 1572872 | tf_op jit(solution)/shard_map/ppermute | solution.py:535
  75.3 14.1 %collective-permute-start.17 = (bf16[2048,128]{1,0:T(8,128)(2,1)S(1)}, bf16[2048,128]{1,0:T(8,128)(2,1)S(1)}, u32[]{:S(2)}, u32[]{:S(2)}) collective-permute-start(bf16[2048,128]{1,0:T(8,128)(2,1)S(1)} %collective-permute-done.12.b1), channel_id=1, source_target_pairs={{4,8},{12,16},{20,24},{28,32},{36,40},{44,48},{52,56},{60,64},{68,... | collective-permute-start | bytes 1572872 | tf_op jit(solution)/shard_map/ppermute | solution.py:541
  77.3 12.2 %collective-permute-start.18 = (bf16[2048,128]{1,0:T(8,128)(2,1)S(1)}, bf16[2048,128]{1,0:T(8,128)(2,1)S(1)}, u32[]{:S(2)}, u32[]{:S(2)}) collective-permute-start(bf16[2048,128]{1,0:T(8,128)(2,1)S(1)} %collective-permute-done.12.b1), channel_id=1, source_target_pairs={{0,4},{4,0},{8,12},{12,8},{16,20},{20,16},{24,28},{28,24},{32,36},... | collective-permute-start | bytes 1572872 | tf_op jit(solution)/shard_map/ppermute | solution.py:535
  77.9 12.0 %collective-permute-start.16 = (bf16[2048,128]{1,0:T(8,128)(2,1)S(1)}, bf16[2048,128]{1,0:T(8,128)(2,1)S(1)}, u32[]{:S(2)}, u32[]{:S(2)}) collective-permute-start(bf16[2048,128]{1,0:T(8,128)(2,1)S(1)} %collective-permute-done.14.b3), channel_id=1, source_target_pairs={{0,3},{1,0},{2,1},{3,2},{4,5},{5,6},{6,7},{7,4},{8,11},{9,8},{10,9... | collective-permute-start | bytes 1572872 | tf_op jit(solution)/shard_map/ppermute | solution.py:556
  82.7 7.1 %collective-permute-start.19 = (bf16[2048,128]{1,0:T(8,128)(2,1)S(1)}, bf16[2048,128]{1,0:T(8,128)(2,1)S(1)}, u32[]{:S(2)}, u32[]{:S(2)}) collective-permute-start(bf16[2048,128]{1,0:T(8,128)(2,1)S(1)} %collective-permute-done.13.b2), channel_id=1, source_target_pairs={{0,4},{4,0},{8,12},{12,8},{16,20},{20,16},{24,28},{28,24},{32,36},... | collective-permute-start | bytes 1572872 | tf_op jit(solution)/shard_map/ppermute | solution.py:535
  (15 other events, 111.3 us)

commit v4 on v3

--- a/solution.py
+++ b/solution.py
@@ -68,14 +68,20 @@
 def pipeline(tiles, fetch, work, one, two, at_pair=lambda pair: None):
     fetch(0, one, 0, 1)
 
+    def nothing(piece, pieces_):
+        pass
+
     def body(pair, carry):
         at_pair(pair)
         tile = 2 * pair
         work(tile, one, functools.partial(fetch, tile + 1, two))
-        work(tile + 1, two, functools.partial(fetch, jnp.minimum(tile + 2, tiles - 1), one))
+        work(tile + 1, two, functools.partial(fetch, tile + 2, one))
         return carry
 
-    lax.fori_loop(0, tiles // 2, body, 0)
+    lax.fori_loop(0, tiles // 2 - 1, body, 0)
+    at_pair(tiles // 2 - 1)
+    work(tiles - 2, one, functools.partial(fetch, tiles - 1, two))
+    work(tiles - 1, two, nothing)
 
 
 def onehot(receivers, begin, valid, nodes):

time: 101 us -> 98.4 us (0.974)
  Pallas kernels: 40.6 us -> 37.9 us
    pallas_call x1, Pallas kernels: 10.9 us -> 9.21 us  [decode(): pl.pallas_call(decode_kernel, in_specs=[SMEM] + [VMEM] * 13, out_specs=HB...]
where the time goes in v4:
time: 98.4 us; the launch traced here: 98.1 us
  starting transfers between devices  40.5 us (41%)
  Pallas kernels  37.9 us (39%)
  waiting for transfers between devices  16.1 us (16%)
  between operations  2.07 us (2%)
  local copies, waits for them, and re-layouts  1.36 us (1%)
    ppermute x5, starting transfers between devices, far(): return lax.ppermute(values, 'lat', ups + [(b, a) for a, b in ups])  17.1 us
    ppermute x7, starting transfers between devices, near(): return lax.ppermute(values, 'lat', [(i, i ^ 1) for i in range(count)])  15.3 us
    ppermute x6, waiting for transfers between devices, lon_shift(): return lax.ppermute(values, ('lat', 'lon'), pairs)  13.4 us
    pallas_call x1, Pallas kernels, encode(): pl.pallas_call(encode_kernel, in_specs=[SMEM] * 2 + [VMEM] * 4 + [ANY] +...  9.24 us
    pallas_call x1, Pallas kernels, decode(): pl.pallas_call(decode_kernel, in_specs=[SMEM] + [VMEM] * 13, out_specs=HB...  9.21 us
    pallas_call x1, Pallas kernels, process(): pl.pallas_call(process_kernel, in_specs=[SMEM] * 2 + [VMEM] * 18, out_spe...  8.34 us
    ppermute x6, starting transfers between devices, lon_shift(): return lax.ppermute(values, ('lat', 'lon'), pairs)  5.14 us
    pallas_call x1, Pallas kernels, receive(): pl.pallas_call(receive_kernel, grid=(tiles,), in_specs=[pl.BlockSpec((nod...  3.85 us
  transfers between devices with their start and end apart: 20, of which 6 were waited for; matrix products, arithmetic and copies ran while one was open for 0% of the time, Pallas kernels for 11%

profile of v4, /device:TPU:3, one launch (start us, length us, event | category | flops | bytes accessed | tf_op | source)
XLA Modules:
  0.0 98.1 jit_solution(14378108309934660018)
XLA Ops:
  0.0 1.2 %copy.39 = bf16[1,1,2048,227]{2,3,1,0:T(8,128)(2,1)S(1)} copy(bf16[1,1,2048,227]{2,3,1,0:T(8,128)(2,1)} %param.30) | data formatting | bytes 1859584
  1.2 1.4 %collective-permute-start = (bf16[227,256]{1,0:T(8,128)(2,1)S(1)}, bf16[227,256]{1,0:T(8,128)(2,1)S(1)}, u32[]{:S(2)}, u32[]{:S(2)}) collective-permute-start(bf16[227,256]{1,0:T(8,128)(2,1)S(1)} %get-tuple-element.21.middle), channel_id=1, source_target_pairs={{0,1},{1,2},{2,3},{3,0},{4,5},{5,6},{6,7},{7,4},{8,9},{9,10},{10,1... | collective-permute-start | bytes 348680 | tf_op jit(solution)/shard_map/ppermute | solution.py:531
  2.6 1.5 %collective-permute-start.1 = (bf16[227,256]{1,0:T(8,128)(2,1)S(1)}, bf16[227,256]{1,0:T(8,128)(2,1)S(1)}, u32[]{:S(2)}, u32[]{:S(2)}) collective-permute-start(bf16[227,256]{1,0:T(8,128)(2,1)S(1)} %get-tuple-element.21.middle), channel_id=1, source_target_pairs={{1,0},{2,1},{3,2},{0,3},{5,4},{6,5},{7,6},{4,7},{9,8},{10,9},{11,1... | collective-permute-start | bytes 348680 | tf_op jit(solution)/shard_map/ppermute | solution.py:536
  4.8 2.0 %collective-permute-done.left.strip_w = bf16[227,256]{1,0:T(8,128)(2,1)S(1)} collective-permute-done((bf16[227,256]{1,0:T(8,128)(2,1)S(1)}, bf16[227,256]{1,0:T(8,128)(2,1)S(1)}, u32[]{:S(2)}, u32[]{:S(2)}) %collective-permute-start) | collective-permute-done | bytes 116256 | tf_op jit(solution)/shard_map/ppermute | solution.py:531
  6.9 5.2 %collective-permute-start.2 = (bf16[227,768]{1,0:T(8,128)(2,1)S(1)}, bf16[227,768]{1,0:T(8,128)(2,1)S(1)}, u32[]{:S(2)}, u32[]{:S(2)}) collective-permute-start(bf16[227,768]{1,0:T(8,128)(2,1)S(1)} %shard_map.281), channel_id=1, source_target_pairs={{4,8},{12,16},{20,24},{28,32},{36,40},{44,48},{52,56},{60,64},{68,... | collective-permute-start | bytes 1046024 | tf_op jit(solution)/shard_map/ppermute | solution.py:547
  12.1 1.0 %collective-permute-start.3 = (bf16[227,768]{1,0:T(8,128)(2,1)S(1)}, bf16[227,768]{1,0:T(8,128)(2,1)S(1)}, u32[]{:S(2)}, u32[]{:S(2)}) collective-permute-start(bf16[227,768]{1,0:T(8,128)(2,1)S(1)} %shard_map.281), channel_id=1, source_target_pairs={{0,4},{4,0},{8,12},{12,8},{16,20},{20,16},{24,28},{28,24},{32,36},... | collective-permute-start | bytes 1046024 | tf_op jit(solution)/shard_map/ppermute | solution.py:541
  13.2 3.5 %shard_map.282 = (bf16[2048,512]{1,0:T(8,128)(2,1)S(1)}, f32[8192,128]{1,0:T(8,128)S(1)}) custom-call(bf16[227,2048]{1,0:T(8,128)(2,1)S(1)} %get-tuple-element.22.fields_hbm.fields, bf16[227,512]{1,0:T(8,128)(2,1)S(1)} %copy-done.17, bf16[512,512]{1,0:T(8,128)(2,1)S(1)} %copy-done.4), custom_call_target="tpu_custom_call" | custom-call | flops 1610612736 | bytes 8388608 | tf_op jit(solution)/shard_map/pallas_call | solution.py:179
  16.8 0.7 collective-permute-done.2.strip_far
  17.6 9.2 %shard_map.283 = (bf16[512,512]{1,0:T(8,128)(2,1)S(1)}, bf16[2048,128]{1,0:T(8,128)(2,1)S(1)}) custom-call(s32[3072]{0:T(1024)S(1)} %fusion.21.index, s32[1,1]{1,0:T(1,128)S(6)} %copy.37.valid, bf16[227,256]{1,0:T(8,128)(2,1)S(1)} %collective-permute-done.left.strip_w, bf16[227,256]{1,0:T(8,128)(2,1)S(1)} %collective-permute-done.1.right.strip_e, ...), custom_call_target="tpu_custom_call" | custom-call | flops 3221225472 | bytes 10485760 | tf_op jit(solution)/shard_map/pallas_call | solution.py:255
  26.8 1.4 %collective-permute-start.4 = (bf16[2048,128]{1,0:T(8,128)(2,1)S(1)}, bf16[2048,128]{1,0:T(8,128)(2,1)S(1)}, u32[]{:S(2)}, u32[]{:S(2)}) collective-permute-start(bf16[2048,128]{1,0:T(8,128)(2,1)S(1)} %get-tuple-element.30.b0), channel_id=1, source_target_pairs={{0,3},{1,0},{2,1},{3,2},{4,5},{5,6},{6,7},{7,4},{8,11},{9,8},{10,9... | collective-permute-start | bytes 1572872 | tf_op jit(solution)/shard_map/ppermute | solution.py:562
  28.2 4.9 %collective-permute-start.6 = (bf16[2048,128]{1,0:T(8,128)(2,1)S(1)}, bf16[2048,128]{1,0:T(8,128)(2,1)S(1)}, u32[]{:S(2)}, u32[]{:S(2)}) collective-permute-start(bf16[2048,128]{1,0:T(8,128)(2,1)S(1)} %get-tuple-element.30.b0), channel_id=1, source_target_pairs={{4,8},{12,16},{20,24},{28,32},{36,40},{44,48},{52,56},{60,64},{68,... | collective-permute-start | bytes 1572872 | tf_op jit(solution)/shard_map/ppermute | solution.py:547
  33.2 3.8 %shard_map.284 = (bf16[4096,512]{1,0:T(8,128)(2,1)S(1)}, f32[512,512]{1,0:T(8,128)S(1)}, bf16[512,512]{1,0:T(8,128)(2,1)S(1)}) custom-call(bf16[512,512]{1,0:T(8,128)(2,1)S(1)} %get-tuple-element.25.start, bf16[512,512]{1,0:T(8,128)(2,1)S(1)} %copy-done.10, bf16[512,512]{1,0:T(8,128)(2,1)S(1)} %copy-done.11, s32[1,4096]{1,0:T(1,128)S(1)} %bitcast.22, ...), custom_call_target="tpu_custom_call" | custom-call | flops 2684354560 | bytes 8388608 | tf_op jit(solution)/shard_map/pallas_call | solution.py:312
  37.1 0.8 collective-permute-start.5
  37.8 1.9 %collective-permute-start.7 = (bf16[2048,128]{1,0:T(8,128)(2,1)S(1)}, bf16[2048,128]{1,0:T(8,128)(2,1)S(1)}, u32[]{:S(2)}, u32[]{:S(2)}) collective-permute-start(bf16[2048,128]{1,0:T(8,128)(2,1)S(1)} %get-tuple-element.30.b0), channel_id=1, source_target_pairs={{0,4},{4,0},{8,12},{12,8},{16,20},{20,16},{24,28},{28,24},{32,36},... | collective-permute-start | bytes 1572872 | tf_op jit(solution)/shard_map/ppermute | solution.py:541
  39.7 1.9 %collective-permute-start.9 = (bf16[2048,128]{1,0:T(8,128)(2,1)S(1)}, bf16[2048,128]{1,0:T(8,128)(2,1)S(1)}, u32[]{:S(2)}, u32[]{:S(2)}) collective-permute-start(bf16[2048,128]{1,0:T(8,128)(2,1)S(1)} %collective-permute-done.4.b1), channel_id=1, source_target_pairs={{4,8},{12,16},{20,24},{28,32},{36,40},{44,48},{52,56},{60,64},{68,... | collective-permute-start | bytes 1572872 | tf_op jit(solution)/shard_map/ppermute | solution.py:547
  41.7 1.2 %collective-permute-start.8 = (bf16[2048,128]{1,0:T(8,128)(2,1)S(1)}, bf16[2048,128]{1,0:T(8,128)(2,1)S(1)}, u32[]{:S(2)}, u32[]{:S(2)}) collective-permute-start(bf16[2048,128]{1,0:T(8,128)(2,1)S(1)} %collective-permute-done.6.b3), channel_id=1, source_target_pairs={{0,3},{1,0},{2,1},{3,2},{4,5},{5,6},{6,7},{7,4},{8,11},{9,8},{10,9... | collective-permute-start | bytes 1572872 | tf_op jit(solution)/shard_map/ppermute | solution.py:562
  42.9 2.5 %collective-permute-done.5.b2 = bf16[2048,128]{1,0:T(8,128)(2,1)S(1)} collective-permute-done((bf16[2048,128]{1,0:T(8,128)(2,1)S(1)}, bf16[2048,128]{1,0:T(8,128)(2,1)S(1)}, u32[]{:S(2)}, u32[]{:S(2)}) %collective-permute-start.5) | collective-permute-done | bytes 524320 | tf_op jit(solution)/shard_map/ppermute | solution.py:562
  45.5 7.0 %collective-permute-start.11 = (bf16[2048,128]{1,0:T(8,128)(2,1)S(1)}, bf16[2048,128]{1,0:T(8,128)(2,1)S(1)}, u32[]{:S(2)}, u32[]{:S(2)}) collective-permute-start(bf16[2048,128]{1,0:T(8,128)(2,1)S(1)} %collective-permute-done.5.b2), channel_id=1, source_target_pairs={{0,4},{4,0},{8,12},{12,8},{16,20},{20,16},{24,28},{28,24},{32,36},... | collective-permute-start | bytes 1572872 | tf_op jit(solution)/shard_map/ppermute | solution.py:541
  53.2 1.9 %shard_map.285.shift = bf16[4096,512]{1,0:T(8,128)(2,1)S(1)} custom-call(bf16[512,512]{1,0:T(8,128)(2,1)S(1)} %get-tuple-element.31.target, s32[1,4096]{1,0:T(1,128)S(1)} %bitcast.23, f32[4,4096]{1,0:T(4,128)S(1)} %bitcast.21, f32[4,512]{1,0:T(4,128)S(1)} %copy-done.3, ...), custom_call_target="tpu_custom_call", output_to_operand_aliasing={{}: (4, {})} | custom-call | flops 1610612736 | bytes 8388608 | tf_op jit(solution)/shard_map/pallas_call | solution.py:342
  55.2 8.3 %shard_map.286.b0 = bf16[2048,128]{1,0:T(8,128)(2,1)S(1)} custom-call(s32[4096]{0:T(1024)S(1)} %fusion.14.index, s32[1,1]{1,0:T(1,128)S(6)} %copy.38.valid, bf16[2048,128]{1,0:T(8,128)(2,1)S(1)} %get-tuple-element.30.b0, bf16[2048,128]{1,0:T(8,128)(2,1)S(1)} %collective-permute-done.4.b1, bf16[2048,128]{1,0:T(8,128)(2,1)S(1)} %collective-permute-done.5.b2, ...), custom_call_target="tpu_custom_call" | custom-call | flops 4294967296 | bytes 12582912 | tf_op jit(solution)/shard_map/pallas_call | solution.py:411
  63.7 3.2 %collective-permute-start.14 = (bf16[2048,128]{1,0:T(8,128)(2,1)S(1)}, bf16[2048,128]{1,0:T(8,128)(2,1)S(1)}, u32[]{:S(2)}, u32[]{:S(2)}) collective-permute-start(bf16[2048,128]{1,0:T(8,128)(2,1)S(1)} %shard_map.286.b0), channel_id=1, source_target_pairs={{4,8},{12,16},{20,24},{28,32},{36,40},{44,48},{52,56},{60,64},{68,... | collective-permute-start | bytes 1572872 | tf_op jit(solution)/shard_map/ppermute | solution.py:547
  66.9 6.3 %collective-permute-done.12.b1 = bf16[2048,128]{1,0:T(8,128)(2,1)S(1)} collective-permute-done((bf16[2048,128]{1,0:T(8,128)(2,1)S(1)}, bf16[2048,128]{1,0:T(8,128)(2,1)S(1)}, u32[]{:S(2)}, u32[]{:S(2)}) %collective-permute-start.12) | collective-permute-done | bytes 524320 | tf_op jit(solution)/shard_map/ppermute | solution.py:562
  73.2 1.0 %collective-permute-start.13 = (bf16[2048,128]{1,0:T(8,128)(2,1)S(1)}, bf16[2048,128]{1,0:T(8,128)(2,1)S(1)}, u32[]{:S(2)}, u32[]{:S(2)}) collective-permute-start(bf16[2048,128]{1,0:T(8,128)(2,1)S(1)} %shard_map.286.b0), channel_id=1, source_target_pairs={{0,1},{1,2},{2,3},{3,0},{4,7},{5,4},{6,5},{7,6},{8,9},{9,10},{10,1... | collective-permute-start | bytes 1572872 | tf_op jit(solution)/shard_map/ppermute | solution.py:562
  74.3 1.9 %collective-permute-start.17 = (bf16[2048,128]{1,0:T(8,128)(2,1)S(1)}, bf16[2048,128]{1,0:T(8,128)(2,1)S(1)}, u32[]{:S(2)}, u32[]{:S(2)}) collective-permute-start(bf16[2048,128]{1,0:T(8,128)(2,1)S(1)} %collective-permute-done.12.b1), channel_id=1, source_target_pairs={{4,8},{12,16},{20,24},{28,32},{36,40},{44,48},{52,56},{60,64},{68,... | collective-permute-start | bytes 1572872 | tf_op jit(solution)/shard_map/ppermute | solution.py:547
  76.2 0.7 collective-permute-start.18
  76.9 0.6 collective-permute-start.16
  77.5 4.0 %collective-permute-done.13.b2 = bf16[2048,128]{1,0:T(8,128)(2,1)S(1)} collective-permute-done((bf16[2048,128]{1,0:T(8,128)(2,1)S(1)}, bf16[2048,128]{1,0:T(8,128)(2,1)S(1)}, u32[]{:S(2)}, u32[]{:S(2)}) %collective-permute-start.13) | collective-permute-done | bytes 524320 | tf_op jit(solution)/shard_map/ppermute | solution.py:562
  81.5 4.7 %collective-permute-start.19 = (bf16[2048,128]{1,0:T(8,128)(2,1)S(1)}, bf16[2048,128]{1,0:T(8,128)(2,1)S(1)}, u32[]{:S(2)}, u32[]{:S(2)}) collective-permute-start(bf16[2048,128]{1,0:T(8,128)(2,1)S(1)} %collective-permute-done.13.b2), channel_id=1, source_target_pairs={{0,4},{4,0},{8,12},{12,8},{16,20},{20,16},{24,28},{28,24},{32,36},... | collective-permute-start | bytes 1572872 | tf_op jit(solution)/shard_map/ppermute | solution.py:541
  86.2 1.8 %shard_map.287.target = bf16[2048,512]{1,0:T(8,128)(2,1)S(1)} custom-call(bf16[2048,512]{1,0:T(8,128)(2,1)S(1)} %get-tuple-element.36.embedded, bf16[512,512]{1,0:T(8,128)(2,1)S(1)} %copy-done), custom_call_target="tpu_custom_call" | custom-call | flops 1073741824 | bytes 4194304 | tf_op jit(solution)/shard_map/pallas_call | solution.py:435
  88.0 0.1 fusion.5.index
  88.1 0.5 collective-permute-done.16.b5
  88.7 9.2 %shard_map.288 = f32[227,1,2048]{2,1,0:T(1,128)} custom-call(s32[6144]{0:T(1024)S(1)} %fusion.5.index, bf16[2048,128]{1,0:T(8,128)(2,1)S(1)} %shard_map.286.b0, bf16[2048,128]{1,0:T(8,128)(2,1)S(1)} %collective-permute-done.12.b1, bf16[2048,128]{1,0:T(8,128)(2,1)S(1)} %collective-permute-done.13.b2, bf16[2048,128]{1,0:T(8,128)(2,1)S(1)} %collective-permute-done.14.b3, ...), custom_call_target="tpu_custom_call" | custom-call | flops 3221225472 | bytes 12582912 | tf_op jit(solution)/shard_map/pallas_call | solution.py:512
  (75 shorter events, 0.5 us)
Async XLA Ops:
  1.2 5.5 %collective-permute-start = (bf16[227,256]{1,0:T(8,128)(2,1)S(1)}, bf16[227,256]{1,0:T(8,128)(2,1)S(1)}, u32[]{:S(2)}, u32[]{:S(2)}) collective-permute-start(bf16[227,256]{1,0:T(8,128)(2,1)S(1)} %get-tuple-element.21.middle), channel_id=1, source_target_pairs={{0,1},{1,2},{2,3},{3,0},{4,5},{5,6},{6,7},{7,4},{8,9},{9,10},{10,1... | collective-permute-start | bytes 348680 | tf_op jit(solution)/shard_map/ppermute | solution.py:531
  2.6 4.2 %collective-permute-start.1 = (bf16[227,256]{1,0:T(8,128)(2,1)S(1)}, bf16[227,256]{1,0:T(8,128)(2,1)S(1)}, u32[]{:S(2)}, u32[]{:S(2)}) collective-permute-start(bf16[227,256]{1,0:T(8,128)(2,1)S(1)} %get-tuple-element.21.middle), channel_id=1, source_target_pairs={{1,0},{2,1},{3,2},{0,3},{5,4},{6,5},{7,6},{4,7},{9,8},{10,9},{11,1... | collective-permute-start | bytes 348680 | tf_op jit(solution)/shard_map/ppermute | solution.py:536
  6.8 10.7 %copy-start.5 = (bf16[512,512]{1,0:T(8,128)(2,1)S(1)}, bf16[512,512]{1,0:T(8,128)(2,1)}, u32[]{:S(2)}) copy-start(bf16[512,512]{1,0:T(8,128)(2,1)} %second.2) | copy-start | bytes 1572868
  6.8 10.7 %copy-start.6 = (bf16[512,512]{1,0:T(8,128)(2,1)S(1)}, bf16[512,512]{1,0:T(8,128)(2,1)}, u32[]{:S(2)}) copy-start(bf16[512,512]{1,0:T(8,128)(2,1)} %first_weight.1) | copy-start | bytes 1572868
  6.9 10.6 %collective-permute-start.2 = (bf16[227,768]{1,0:T(8,128)(2,1)S(1)}, bf16[227,768]{1,0:T(8,128)(2,1)S(1)}, u32[]{:S(2)}, u32[]{:S(2)}) collective-permute-start(bf16[227,768]{1,0:T(8,128)(2,1)S(1)} %shard_map.281), channel_id=1, source_target_pairs={{4,8},{12,16},{20,24},{28,32},{36,40},{44,48},{52,56},{60,64},{68,... | collective-permute-start | bytes 1046024 | tf_op jit(solution)/shard_map/ppermute | solution.py:547
  12.1 5.3 %collective-permute-start.3 = (bf16[227,768]{1,0:T(8,128)(2,1)S(1)}, bf16[227,768]{1,0:T(8,128)(2,1)S(1)}, u32[]{:S(2)}, u32[]{:S(2)}) collective-permute-start(bf16[227,768]{1,0:T(8,128)(2,1)S(1)} %shard_map.281), channel_id=1, source_target_pairs={{0,4},{4,0},{8,12},{12,8},{16,20},{20,16},{24,28},{28,24},{32,36},... | collective-permute-start | bytes 1046024 | tf_op jit(solution)/shard_map/ppermute | solution.py:541
  17.5 15.6 %copy-start.1 = (f32[1,1,4,4096]{3,2,1,0:T(4,128)S(1)}, f32[1,1,4,4096]{3,2,1,0:T(4,128)}, u32[]{:S(2)}) copy-start(f32[1,1,4,4096]{3,2,1,0:T(4,128)} %param.38) | copy-start | bytes 196612
  17.6 15.6 %copy-start.2 = (s32[1,1,4096]{2,1,0:T(1,128)S(1)}, s32[1,1,4096]{2,1,0:T(1,128)}, u32[]{:S(2)}) copy-start(s32[1,1,4096]{2,1,0:T(1,128)} %param.37) | copy-start | bytes 49156
  17.6 15.6 %copy-start.3 = (f32[4,512]{1,0:T(4,128)S(1)}, f32[4,512]{1,0:T(4,128)}, u32[]{:S(2)}) copy-start(f32[4,512]{1,0:T(4,128)} %edge_weight.5) | copy-start | bytes 24580
  17.6 15.6 %copy-start.10 = (bf16[512,512]{1,0:T(8,128)(2,1)S(1)}, bf16[512,512]{1,0:T(8,128)(2,1)}, u32[]{:S(2)}) copy-start(bf16[512,512]{1,0:T(8,128)(2,1)} %target_weight.1) | copy-start | bytes 1572868
  17.6 15.6 %copy-start.11 = (bf16[512,512]{1,0:T(8,128)(2,1)S(1)}, bf16[512,512]{1,0:T(8,128)(2,1)}, u32[]{:S(2)}) copy-start(bf16[512,512]{1,0:T(8,128)(2,1)} %state_weight.1) | copy-start | bytes 1572868
  26.8 10.2 %collective-permute-start.4 = (bf16[2048,128]{1,0:T(8,128)(2,1)S(1)}, bf16[2048,128]{1,0:T(8,128)(2,1)S(1)}, u32[]{:S(2)}, u32[]{:S(2)}) collective-permute-start(bf16[2048,128]{1,0:T(8,128)(2,1)S(1)} %get-tuple-element.30.b0), channel_id=1, source_target_pairs={{0,3},{1,0},{2,1},{3,2},{4,5},{5,6},{6,7},{7,4},{8,11},{9,8},{10,9... | collective-permute-start | bytes 1572872 | tf_op jit(solution)/shard_map/ppermute | solution.py:562
  28.2 13.5 %collective-permute-start.6 = (bf16[2048,128]{1,0:T(8,128)(2,1)S(1)}, bf16[2048,128]{1,0:T(8,128)(2,1)S(1)}, u32[]{:S(2)}, u32[]{:S(2)}) collective-permute-start(bf16[2048,128]{1,0:T(8,128)(2,1)S(1)} %get-tuple-element.30.b0), channel_id=1, source_target_pairs={{4,8},{12,16},{20,24},{28,32},{36,40},{44,48},{52,56},{60,64},{68,... | collective-permute-start | bytes 1572872 | tf_op jit(solution)/shard_map/ppermute | solution.py:547
  33.2 19.9 %copy-start.25 = (s32[1,1,4096]{2,1,0:T(1,128)S(1)}, s32[1,1,4096]{2,1,0:T(1,128)}, u32[]{:S(2)}) copy-start(s32[1,1,4096]{2,1,0:T(1,128)} %param.36) | copy-start | bytes 49156
  37.1 8.4 %collective-permute-start.5 = (bf16[2048,128]{1,0:T(8,128)(2,1)S(1)}, bf16[2048,128]{1,0:T(8,128)(2,1)S(1)}, u32[]{:S(2)}, u32[]{:S(2)}) collective-permute-start(bf16[2048,128]{1,0:T(8,128)(2,1)S(1)} %get-tuple-element.30.b0), channel_id=1, source_target_pairs={{0,1},{1,2},{2,3},{3,0},{4,7},{5,4},{6,5},{7,6},{8,9},{9,10},{10,1... | collective-permute-start | bytes 1572872 | tf_op jit(solution)/shard_map/ppermute | solution.py:562
  37.8 17.3 %collective-permute-start.7 = (bf16[2048,128]{1,0:T(8,128)(2,1)S(1)}, bf16[2048,128]{1,0:T(8,128)(2,1)S(1)}, u32[]{:S(2)}, u32[]{:S(2)}) collective-permute-start(bf16[2048,128]{1,0:T(8,128)(2,1)S(1)} %get-tuple-element.30.b0), channel_id=1, source_target_pairs={{0,4},{4,0},{8,12},{12,8},{16,20},{20,16},{24,28},{28,24},{32,36},... | collective-permute-start | bytes 1572872 | tf_op jit(solution)/shard_map/ppermute | solution.py:541
  39.7 15.4 %collective-permute-start.10 = (bf16[2048,128]{1,0:T(8,128)(2,1)S(1)}, bf16[2048,128]{1,0:T(8,128)(2,1)S(1)}, u32[]{:S(2)}, u32[]{:S(2)}) collective-permute-start(bf16[2048,128]{1,0:T(8,128)(2,1)S(1)} %collective-permute-done.4.b1), channel_id=1, source_target_pairs={{0,4},{4,0},{8,12},{12,8},{16,20},{20,16},{24,28},{28,24},{32,36},... | collective-permute-start | bytes 1572872 | tf_op jit(solution)/shard_map/ppermute | solution.py:541
  39.7 15.4 %collective-permute-start.9 = (bf16[2048,128]{1,0:T(8,128)(2,1)S(1)}, bf16[2048,128]{1,0:T(8,128)(2,1)S(1)}, u32[]{:S(2)}, u32[]{:S(2)}) collective-permute-start(bf16[2048,128]{1,0:T(8,128)(2,1)S(1)} %collective-permute-done.4.b1), channel_id=1, source_target_pairs={{4,8},{12,16},{20,24},{28,32},{36,40},{44,48},{52,56},{60,64},{68,... | collective-permute-start | bytes 1572872 | tf_op jit(solution)/shard_map/ppermute | solution.py:547
  41.7 13.5 %collective-permute-start.8 = (bf16[2048,128]{1,0:T(8,128)(2,1)S(1)}, bf16[2048,128]{1,0:T(8,128)(2,1)S(1)}, u32[]{:S(2)}, u32[]{:S(2)}) collective-permute-start(bf16[2048,128]{1,0:T(8,128)(2,1)S(1)} %collective-permute-done.6.b3), channel_id=1, source_target_pairs={{0,3},{1,0},{2,1},{3,2},{4,5},{5,6},{6,7},{7,4},{8,11},{9,8},{10,9... | collective-permute-start | bytes 1572872 | tf_op jit(solution)/shard_map/ppermute | solution.py:562
  45.5 9.7 %collective-permute-start.11 = (bf16[2048,128]{1,0:T(8,128)(2,1)S(1)}, bf16[2048,128]{1,0:T(8,128)(2,1)S(1)}, u32[]{:S(2)}, u32[]{:S(2)}) collective-permute-start(bf16[2048,128]{1,0:T(8,128)(2,1)S(1)} %collective-permute-done.5.b2), channel_id=1, source_target_pairs={{0,4},{4,0},{8,12},{12,8},{16,20},{20,16},{24,28},{28,24},{32,36},... | collective-permute-start | bytes 1572872 | tf_op jit(solution)/shard_map/ppermute | solution.py:541
  55.2 31.0 %copy-start = (bf16[512,512]{1,0:T(8,128)(2,1)S(1)}, bf16[512,512]{1,0:T(8,128)(2,1)}, u32[]{:S(2)}) copy-start(bf16[512,512]{1,0:T(8,128)(2,1)} %weight.1) | copy-start | bytes 1572868
  63.6 24.4 %copy-start.24 = (s32[1,1,3,2048]{3,1,2,0:T(1,128)S(1)}, s32[1,1,3,2048]{3,1,2,0:T(1,128)}, u32[]{:S(2)}) copy-start(s32[1,1,3,2048]{3,1,2,0:T(1,128)} %param.40) | copy-start | bytes 73732
  63.6 25.1 %copy-start.16 = (bf16[512,512]{1,0:T(8,128)(2,1)S(1)}, bf16[512,512]{1,0:T(8,128)(2,1)}, u32[]{:S(2)}) copy-start(bf16[512,512]{1,0:T(8,128)(2,1)} %hidden_weight.1) | copy-start | bytes 1572868
  63.6 25.1 %copy-start.18 = (bf16[512,227]{0,1:T(8,128)(2,1)S(1)}, bf16[512,227]{0,1:T(8,128)(2,1)}, u32[]{:S(2)}) copy-start(bf16[512,227]{0,1:T(8,128)(2,1)} %param.59) | copy-start | bytes 697348
  63.6 9.6 %collective-permute-start.12 = (bf16[2048,128]{1,0:T(8,128)(2,1)S(1)}, bf16[2048,128]{1,0:T(8,128)(2,1)S(1)}, u32[]{:S(2)}, u32[]{:S(2)}) collective-permute-start(bf16[2048,128]{1,0:T(8,128)(2,1)S(1)} %shard_map.286.b0), channel_id=1, source_target_pairs={{0,3},{1,0},{2,1},{3,2},{4,5},{5,6},{6,7},{7,4},{8,11},{9,8},{10,9... | collective-permute-start | bytes 1572872 | tf_op jit(solution)/shard_map/ppermute | solution.py:562
  63.7 13.2 %collective-permute-start.14 = (bf16[2048,128]{1,0:T(8,128)(2,1)S(1)}, bf16[2048,128]{1,0:T(8,128)(2,1)S(1)}, u32[]{:S(2)}, u32[]{:S(2)}) collective-permute-start(bf16[2048,128]{1,0:T(8,128)(2,1)S(1)} %shard_map.286.b0), channel_id=1, source_target_pairs={{4,8},{12,16},{20,24},{28,32},{36,40},{44,48},{52,56},{60,64},{68,... | collective-permute-start | bytes 1572872 | tf_op jit(solution)/shard_map/ppermute | solution.py:547
  73.2 8.3 %collective-permute-start.13 = (bf16[2048,128]{1,0:T(8,128)(2,1)S(1)}, bf16[2048,128]{1,0:T(8,128)(2,1)S(1)}, u32[]{:S(2)}, u32[]{:S(2)}) collective-permute-start(bf16[2048,128]{1,0:T(8,128)(2,1)S(1)} %shard_map.286.b0), channel_id=1, source_target_pairs={{0,1},{1,2},{2,3},{3,0},{4,7},{5,4},{6,5},{7,6},{8,9},{9,10},{10,1... | collective-permute-start | bytes 1572872 | tf_op jit(solution)/shard_map/ppermute | solution.py:562
  74.3 13.9 %collective-permute-start.15 = (bf16[2048,128]{1,0:T(8,128)(2,1)S(1)}, bf16[2048,128]{1,0:T(8,128)(2,1)S(1)}, u32[]{:S(2)}, u32[]{:S(2)}) collective-permute-start(bf16[2048,128]{1,0:T(8,128)(2,1)S(1)} %shard_map.286.b0), channel_id=1, source_target_pairs={{0,4},{4,0},{8,12},{12,8},{16,20},{20,16},{24,28},{28,24},{32,36},... | collective-permute-start | bytes 1572872 | tf_op jit(solution)/shard_map/ppermute | solution.py:541
  74.3 13.9 %collective-permute-start.17 = (bf16[2048,128]{1,0:T(8,128)(2,1)S(1)}, bf16[2048,128]{1,0:T(8,128)(2,1)S(1)}, u32[]{:S(2)}, u32[]{:S(2)}) collective-permute-start(bf16[2048,128]{1,0:T(8,128)(2,1)S(1)} %collective-permute-done.12.b1), channel_id=1, source_target_pairs={{4,8},{12,16},{20,24},{28,32},{36,40},{44,48},{52,56},{60,64},{68,... | collective-permute-start | bytes 1572872 | tf_op jit(solution)/shard_map/ppermute | solution.py:547
  76.2 12.0 %collective-permute-start.18 = (bf16[2048,128]{1,0:T(8,128)(2,1)S(1)}, bf16[2048,128]{1,0:T(8,128)(2,1)S(1)}, u32[]{:S(2)}, u32[]{:S(2)}) collective-permute-start(bf16[2048,128]{1,0:T(8,128)(2,1)S(1)} %collective-permute-done.12.b1), channel_id=1, source_target_pairs={{0,4},{4,0},{8,12},{12,8},{16,20},{20,16},{24,28},{28,24},{32,36},... | collective-permute-start | bytes 1572872 | tf_op jit(solution)/shard_map/ppermute | solution.py:541
  76.9 11.8 %collective-permute-start.16 = (bf16[2048,128]{1,0:T(8,128)(2,1)S(1)}, bf16[2048,128]{1,0:T(8,128)(2,1)S(1)}, u32[]{:S(2)}, u32[]{:S(2)}) collective-permute-start(bf16[2048,128]{1,0:T(8,128)(2,1)S(1)} %collective-permute-done.14.b3), channel_id=1, source_target_pairs={{0,3},{1,0},{2,1},{3,2},{4,5},{5,6},{6,7},{7,4},{8,11},{9,8},{10,9... | collective-permute-start | bytes 1572872 | tf_op jit(solution)/shard_map/ppermute | solution.py:562
  81.5 7.1 %collective-permute-start.19 = (bf16[2048,128]{1,0:T(8,128)(2,1)S(1)}, bf16[2048,128]{1,0:T(8,128)(2,1)S(1)}, u32[]{:S(2)}, u32[]{:S(2)}) collective-permute-start(bf16[2048,128]{1,0:T(8,128)(2,1)S(1)} %collective-permute-done.13.b2), channel_id=1, source_target_pairs={{0,4},{4,0},{8,12},{12,8},{16,20},{20,16},{24,28},{28,24},{32,36},... | collective-permute-start | bytes 1572872 | tf_op jit(solution)/shard_map/ppermute | solution.py:541
  (15 other events, 111.3 us)
